TPU v7x, 32 devices: a whole 2x2x4 slice. The times are simulated.
32 devices in a mesh: seq: 4 (over x, core), fsdp: 8 (over z, y).
Axes of the slice: x: 2, y: 2, z: 4, core: 2. Of those that a mesh axis runs over, the one named last changes fastest.
Arguments:
- tokens: bfloat16 [8, 512, 2048], P('fsdp', 'seq'), may hold values from -6 to 6
- segments: int32 [8, 512], P('fsdp'), may hold values from 0 to 4, as said below
- positions: int32 [8, 512], P('fsdp', 'seq'), may hold values from 0 to 510, as said below
- gain_one: bfloat16 [2048], P(('seq', 'fsdp')), may hold values from 0.5 to 1.5
- w_query: bfloat16 [2048, 2048], P(('seq', 'fsdp')), may hold values from -0.125 to 0.125
- w_key: bfloat16 [2048, 128], P(('seq', 'fsdp')), may hold values from -0.125 to 0.125
- w_value: bfloat16 [2048, 128], P(('seq', 'fsdp')), may hold values from -0.125 to 0.125
- w_out: bfloat16 [2048, 2048], P(('seq', 'fsdp')), may hold values from -1 to 1
- gain_two: bfloat16 [2048], P(('seq', 'fsdp')), may hold values from 0.5 to 1.5
- w_gate: bfloat16 [2048, 5632], P(('seq', 'fsdp')), may hold values from -0.125 to 0.125
- w_up: bfloat16 [2048, 5632], P(('seq', 'fsdp')), may hold values from -0.125 to 0.125
- w_down: bfloat16 [5632, 2048], P(('seq', 'fsdp')), may hold values from -0.078125 to 0.078125
- cotangent: bfloat16 [8, 512, 2048], P('fsdp', 'seq'), may hold values from -6 to 6
Outputs:
- output: bfloat16 [8, 512, 2048], P('fsdp', 'seq')
- keys_out: bfloat16 [8, 512, 128], P('fsdp', 'seq')
- values_out: bfloat16 [8, 512, 128], P('fsdp', 'seq')
- grad_tokens: float32 [8, 512, 2048], P('fsdp', 'seq')
- grad_gain_one: float32 [2048], P(('seq', 'fsdp'))
- grad_w_query: float32 [2048, 2048], P(('seq', 'fsdp'))
- grad_w_key: float32 [2048, 128], P(('seq', 'fsdp'))
- grad_w_value: float32 [2048, 128], P(('seq', 'fsdp'))
- grad_w_out: float32 [2048, 2048], P(('seq', 'fsdp'))
- grad_gain_two: float32 [2048], P(('seq', 'fsdp'))
- grad_w_gate: float32 [2048, 5632], P(('seq', 'fsdp'))
- grad_w_up: float32 [2048, 5632], P(('seq', 'fsdp'))
- grad_w_down: float32 [5632, 2048], P(('seq', 'fsdp'))
Inputs may be any that keep to these rules, and one draw needn't show every extreme that they name: `segments`: segment ids never fall along a row; in every row one segment runs from the first block of 128 tokens into the last. `positions`: a token's position counts its place from the start of its segment.
All inputs are finite; a program needn't handle non-finite values.
Results may differ from a plain program's by a relative error of at most 0.013.
Values may be sent and summed in bfloat16 or wider, within the bound.
A program may use at most 448 MiB of HBM per device.

v0:
```python
import jax
import jax.numpy as jnp
from jax import lax
from jax.sharding import PartitionSpec as P

epsilon = 1e-05


def angle_tables(position_row, head_size):
    half_head = head_size // 2
    frequency = 10000.0 ** (-jnp.arange(half_head, dtype=jnp.float32) * 2.0 / head_size)
    phase_angle = position_row.astype(jnp.float32)[:, None] * frequency[None, :]
    return (jnp.cos(phase_angle)[:, None, :], jnp.sin(phase_angle)[:, None, :])


def rotate(tensor_in, cosine, sine):
    half_head = tensor_in.shape[-1] // 2
    first_half = tensor_in[..., :half_head]
    second_half = tensor_in[..., half_head:]
    return jnp.concatenate(
        [first_half * cosine - second_half * sine, second_half * cosine + first_half * sine], -1
    )


def contract_last(left, right):
    return lax.dot_general(
        left, right, (((1,), (1,)), ((), ())), preferred_element_type=jnp.float32
    )


def contract_first(left, right):
    return lax.dot_general(
        left, right, (((0,), (0,)), ((), ())), preferred_element_type=jnp.float32
    )


def norm_back(grad_normed, inputs, inverse_rms, gain_full):
    scaled = grad_normed * gain_full
    width = inputs.shape[-1]
    inner_sum = jnp.sum(scaled * inputs, -1, keepdims=True)
    grad_input = inverse_rms * scaled - inputs * inverse_rms**3 * inner_sum / width
    grad_gain = jnp.sum(grad_normed * inputs * inverse_rms, 0)
    return (grad_input, grad_gain)


def per_device(
    tokens,
    segments,
    positions,
    gain_one,
    w_query,
    w_key,
    w_value,
    w_out,
    gain_two,
    w_gate,
    w_up,
    w_down,
    cotangent,
):
    seq_len = tokens.shape[1]
    head_size = w_key.shape[1]
    row_len = segments.shape[1]
    attn_set = (
        lax.all_gather(gain_one, ("seq", "fsdp"), axis=0, tiled=True),
        lax.all_gather(w_query, ("seq", "fsdp"), axis=0, tiled=True),
        lax.all_gather(w_key, ("seq", "fsdp"), axis=0, tiled=True),
        lax.all_gather(w_value, ("seq", "fsdp"), axis=0, tiled=True),
        lax.all_gather(w_out, ("seq", "fsdp"), axis=0, tiled=True),
    )
    gain_one_full, query_full, key_full, value_full, out_full = attn_set
    n_heads = query_full.shape[1] // head_size
    offset = lax.axis_index("seq") * seq_len
    segment_full = segments[0]
    segment_local = lax.dynamic_slice_in_dim(segment_full, offset, seq_len)
    cosine, sine = angle_tables(positions[0], head_size)
    inputs = tokens[0].astype(jnp.float32)
    inverse_one = lax.rsqrt(jnp.mean(inputs * inputs, -1, keepdims=True) + epsilon)
    normed_one = (inputs * inverse_one * gain_one_full.astype(jnp.float32)).astype(jnp.bfloat16)
    queries = jnp.dot(normed_one, query_full, preferred_element_type=jnp.float32)
    key_proj = jnp.dot(normed_one, key_full, preferred_element_type=jnp.float32)
    value_proj = jnp.dot(normed_one, value_full, preferred_element_type=jnp.float32)
    query_rot = rotate(queries.reshape(seq_len, n_heads, head_size), cosine, sine).astype(
        jnp.bfloat16
    )
    key_rot = rotate(key_proj[:, None, :], cosine, sine)[:, 0, :].astype(jnp.bfloat16)
    value_low = value_proj.astype(jnp.bfloat16)
    key_all, value_all = (
        lax.all_gather(key_rot, "seq", axis=0, tiled=True),
        lax.all_gather(value_low, "seq", axis=0, tiled=True),
    )
    scale = head_size ** (-0.5)
    query_flat = query_rot.reshape(seq_len * n_heads, head_size)
    token_index = offset + jnp.arange(seq_len)
    allowed = (jnp.arange(row_len)[None, :] <= token_index[:, None]) & (
        segment_full[None, :] == segment_local[:, None]
    )

    def masked_scores():
        raw = contract_last(query_flat, key_all) * scale
        raw = raw.reshape(seq_len, n_heads, row_len)
        return jnp.where(allowed[:, None, :], raw, -1e30)

    scores = masked_scores()
    row_max = jnp.max(scores, -1, keepdims=True)
    exp_scores = jnp.exp(scores - row_max)
    row_total = jnp.sum(exp_scores, -1, keepdims=True)
    log_total = row_max + jnp.log(row_total)
    probs_low = (exp_scores / row_total).astype(jnp.bfloat16).reshape(seq_len * n_heads, row_len)
    attended = jnp.dot(probs_low, value_all, preferred_element_type=jnp.float32)
    attended_low = attended.reshape(seq_len, n_heads * head_size).astype(jnp.bfloat16)
    residual = inputs + jnp.dot(attended_low, out_full, preferred_element_type=jnp.float32)
    ffn_set = (
        lax.all_gather(gain_two, ("seq", "fsdp"), axis=0, tiled=True),
        lax.all_gather(w_gate, ("seq", "fsdp"), axis=0, tiled=True),
        lax.all_gather(w_up, ("seq", "fsdp"), axis=0, tiled=True),
        lax.all_gather(w_down, ("seq", "fsdp"), axis=0, tiled=True),
    )
    gain_two_full, gate_full, up_full, down_full = ffn_set
    inverse_two = lax.rsqrt(jnp.mean(residual * residual, -1, keepdims=True) + epsilon)
    normed_two = (residual * inverse_two * gain_two_full.astype(jnp.float32)).astype(jnp.bfloat16)
    gate_proj = jnp.dot(normed_two, gate_full, preferred_element_type=jnp.float32)
    up_proj = jnp.dot(normed_two, up_full, preferred_element_type=jnp.float32)
    sigmoid_gate = jax.nn.sigmoid(gate_proj)
    inner_low = (gate_proj * sigmoid_gate * up_proj).astype(jnp.bfloat16)
    output = residual + jnp.dot(inner_low, down_full, preferred_element_type=jnp.float32)
    gain_two_back, gate_back, up_back, down_back = (
        lax.all_gather(gain_two, ("seq", "fsdp"), axis=0, tiled=True),
        lax.all_gather(w_gate, ("seq", "fsdp"), axis=0, tiled=True),
        lax.all_gather(w_up, ("seq", "fsdp"), axis=0, tiled=True),
        lax.all_gather(w_down, ("seq", "fsdp"), axis=0, tiled=True),
    )
    gain_one_back, query_back, key_back, value_back, out_back = (
        lax.all_gather(gain_one, ("seq", "fsdp"), axis=0, tiled=True),
        lax.all_gather(w_query, ("seq", "fsdp"), axis=0, tiled=True),
        lax.all_gather(w_key, ("seq", "fsdp"), axis=0, tiled=True),
        lax.all_gather(w_value, ("seq", "fsdp"), axis=0, tiled=True),
        lax.all_gather(w_out, ("seq", "fsdp"), axis=0, tiled=True),
    )
    grad_out = cotangent[0].astype(jnp.float32)
    grad_out_low = cotangent[0]
    column_block = inner_low
    grad_w_down = lax.psum_scatter(
        contract_first(column_block, grad_out_low), ("seq", "fsdp"), scatter_dimension=0, tiled=True
    )
    grad_inner = contract_last(grad_out_low, down_back)
    grad_gate = (
        grad_inner * up_proj * sigmoid_gate * (1.0 + gate_proj * (1.0 - sigmoid_gate))
    ).astype(jnp.bfloat16)
    grad_up = (grad_inner * gate_proj * sigmoid_gate).astype(jnp.bfloat16)
    both_grads = jnp.concatenate([grad_gate, grad_up], 1)
    ff_width = gate_back.shape[1]
    column_block = normed_two
    ffn_pair = lax.psum_scatter(
        contract_first(column_block, both_grads), ("seq", "fsdp"), scatter_dimension=0, tiled=True
    )
    grad_w_gate = ffn_pair[:, :ff_width]
    grad_w_up = ffn_pair[:, ff_width:]
    grad_normed_two = contract_last(grad_gate, gate_back) + contract_last(grad_up, up_back)
    grad_resid_norm, grad_gain_two_local = norm_back(
        grad_normed_two, residual, inverse_two, gain_two_back.astype(jnp.float32)
    )
    grad_residual = grad_out + grad_resid_norm
    grad_resid_low = grad_residual.astype(jnp.bfloat16)
    column_block = attended_low
    grad_w_out = lax.psum_scatter(
        contract_first(column_block, grad_resid_low),
        ("seq", "fsdp"),
        scatter_dimension=0,
        tiled=True,
    )
    grad_attended = contract_last(grad_resid_low, out_back).astype(jnp.bfloat16)
    grad_att_flat = grad_attended.reshape(seq_len * n_heads, head_size)
    grad_probs = contract_last(grad_att_flat, value_all).reshape(seq_len, n_heads, row_len)
    probs_full = jnp.exp(masked_scores() - log_total)
    delta_rows = jnp.sum(probs_full * grad_probs, -1, keepdims=True)
    grad_scores = (
        (probs_full * (grad_probs - delta_rows))
        .astype(jnp.bfloat16)
        .reshape(seq_len * n_heads, row_len)
    )
    grad_query_rot = jnp.dot(grad_scores, key_all, preferred_element_type=jnp.float32) * scale
    grad_key_all = contract_first(grad_scores, query_flat) * scale
    grad_value_all = contract_first(probs_low, grad_att_flat)
    grad_key_part, grad_value_part = (
        lax.psum_scatter(grad_key_all, "seq", scatter_dimension=0, tiled=True),
        lax.psum_scatter(grad_value_all, "seq", scatter_dimension=0, tiled=True),
    )
    grad_query = rotate(grad_query_rot.reshape(seq_len, n_heads, head_size), cosine, -sine)
    grad_query = grad_query.reshape(seq_len, n_heads * head_size).astype(jnp.bfloat16)
    grad_key = rotate(grad_key_part[:, None, :], cosine, -sine)[:, 0, :].astype(jnp.bfloat16)
    grad_value = grad_value_part.astype(jnp.bfloat16)
    proj_grads = jnp.concatenate([grad_query, grad_key, grad_value], 1)
    query_width = query_back.shape[1]
    column_block = normed_one
    proj_triple = lax.psum_scatter(
        contract_first(column_block, proj_grads), ("seq", "fsdp"), scatter_dimension=0, tiled=True
    )
    grad_w_query = proj_triple[:, :query_width]
    grad_w_key = proj_triple[:, query_width : query_width + head_size]
    grad_w_value = proj_triple[:, query_width + head_size :]
    grad_normed_one = (
        contract_last(grad_query, query_back)
        + contract_last(grad_key, key_back)
        + contract_last(grad_value, value_back)
    )
    grad_in_norm, grad_gain_one_local = norm_back(
        grad_normed_one, inputs, inverse_one, gain_one_back.astype(jnp.float32)
    )
    grad_tokens = grad_residual + grad_in_norm
    grad_gain_one, grad_gain_two = (
        lax.psum_scatter(grad_gain_one_local, ("seq", "fsdp"), scatter_dimension=0, tiled=True),
        lax.psum_scatter(grad_gain_two_local, ("seq", "fsdp"), scatter_dimension=0, tiled=True),
    )
    return (
        output.astype(jnp.bfloat16)[None],
        key_rot[None],
        value_low[None],
        grad_tokens[None],
        grad_gain_one,
        grad_w_query,
        grad_w_key,
        grad_w_value,
        grad_w_out,
        grad_gain_two,
        grad_w_gate,
        grad_w_up,
        grad_w_down,
    )


def solution(mesh):
    placed = (
        P("fsdp", "seq", None),
        P("fsdp", None),
        P("fsdp", "seq"),
        P(("seq", "fsdp")),
        P(("seq", "fsdp"), None),
        P(("seq", "fsdp"), None),
        P(("seq", "fsdp"), None),
        P(("seq", "fsdp"), None),
        P(("seq", "fsdp")),
        P(("seq", "fsdp"), None),
        P(("seq", "fsdp"), None),
        P(("seq", "fsdp"), None),
        P("fsdp", "seq", None),
    )
    return jax.shard_map(
        per_device,
        mesh=mesh,
        in_specs=placed,
        out_specs=(
            P("fsdp", "seq", None),
            P("fsdp", "seq", None),
            P("fsdp", "seq", None),
            P("fsdp", "seq", None),
            P(("seq", "fsdp")),
            P(("seq", "fsdp"), None),
            P(("seq", "fsdp"), None),
            P(("seq", "fsdp"), None),
            P(("seq", "fsdp"), None),
            P(("seq", "fsdp")),
            P(("seq", "fsdp"), None),
            P(("seq", "fsdp"), None),
            P(("seq", "fsdp"), None),
        ),
        check_vma=False,
    )
```

profile of v0, /device:TPU:0, one launch (start us, length us, event | category | flops | bytes accessed | tf_op | source)
XLA Modules:
  0.0 4196.1 jit_solution(3539756912877713469)
XLA Ops:
  12.4 42.6 %all-reduce.5 = (bf16[2048]{0:T(1024)(128)(2,1)S(1)}, bf16[2048]{0:T(1024)(128)(2,1)S(1)}) all-reduce(bf16[2048]{0:T(1024)(128)(2,1)S(1)} %dynamic-update-slice, bf16[2048]{0:T(1024)(128)(2,1)S(1)} %dynamic-update-slice.1), channel_id=1, replica_groups=mesh['seq'=4,'fsdp'=8] {'seq','fsdp'}, use_global_device_ids=true, to_apply=%add | all-reduce | flops 4096 | bytes 16384
  56.9 71.5 %all_gather.44 = bf16[2048,128]{1,0:T(8,128)(2,1)S(1)} all-gather(bf16[64,128]{1,0:T(8,128)(2,1)} %param.18), channel_id=1, replica_groups=mesh['seq'=4,'fsdp'=8] {'seq','fsdp'}, dimensions={0}, use_global_device_ids=true | all-gather | bytes 540672 | tf_op jit(solution)/shard_map/all_gather | solution.py:67
  130.3 5.4 all-gather
  135.8 69.7 %all_gather.46 = bf16[2048,128]{1,0:T(8,128)(2,1)S(1)} all-gather(bf16[64,128]{1,0:T(8,128)(2,1)S(1)} %copy-done.36), channel_id=1, replica_groups=mesh['seq'=4,'fsdp'=8] {'seq','fsdp'}, dimensions={0}, use_global_device_ids=true | all-gather | bytes 540672 | tf_op jit(solution)/shard_map/all_gather | solution.py:68
  205.8 5.9 all_gather.47
  212.7 11.7 copy.51
  224.4 5.9 fusion.36
  237.3 5.1 multiply_reduce_fusion.3
  243.4 83.5 %all-gather.13.cloned.1.call-done = bf16[2048,5632]{1,0:T(8,128)(2,1)} async-done(((bf16[64,5632]{1,0:T(8,128)(2,1)}), bf16[2048,5632]{1,0:T(8,128)(2,1)}) %all-gather.13.cloned.1.call-update) | async-done | bytes 23068688 | tf_op jit(solution)/shard_map/all_gather | solution.py:116
  326.8 12.5 fusion.88
  339.3 133.1 %all-gather.11.cloned.1.call-done = bf16[2048,5632]{1,0:T(8,128)(2,1)} async-done(((bf16[64,5632]{1,0:T(8,128)(2,1)}), bf16[2048,5632]{1,0:T(8,128)(2,1)}) %all-gather.11.cloned.1.call-update) | async-done | bytes 23068688 | tf_op jit(solution)/shard_map/all_gather | solution.py:115
  472.4 12.5 fusion.87
  484.9 133.1 %all-gather.15.cloned.1.call-done = bf16[5632,2048]{1,0:T(8,128)(2,1)} async-done(((bf16[176,2048]{1,0:T(8,128)(2,1)}), bf16[5632,2048]{1,0:T(8,128)(2,1)}) %all-gather.15.cloned.1.call-update) | async-done | bytes 23068688 | tf_op jit(solution)/shard_map/all_gather | solution.py:117
  618.0 15.4 multiply_convert_fusion.1
  633.4 13.2 fusion.89
  646.6 14.0 multiply_reduce_fusion.1
  663.3 7.1 convolution_convert_fusion
  675.1 6.1 multiply_reduce_fusion
  681.2 3.0 multiply_convert_fusion
  696.6 19.4 reduce-scatter.7.cloned.1.call-done
  717.1 7.9 fusion.29
  726.5 41.6 fusion.4
  769.6 8.5 fusion.53
  779.1 20.3 fusion.47
  800.9 6.5 fusion.90
  807.5 12.5 fusion.9
  821.0 40.3 all-reduce.4
  863.9 68.4 %reduce-scatter.11.cloned.1.call-done = f32[64,2304]{1,0:T(8,128)} async-done(((f32[2048,2304]{1,0:T(8,128)}), f32[64,2304]{1,0:T(8,128)}) %reduce-scatter.11.cloned.1.call-update) | async-done | bytes 589840 | tf_op jit(solution)/shard_map/reduce_scatter | solution.py:196
  935.6 1923.2 %reduce-scatter.15.cloned.1.call-done = f32[64,11264]{1,0:T(8,128)} async-done(((f32[2048,11264]{1,0:T(8,128)}), f32[64,11264]{1,0:T(8,128)}) %reduce-scatter.15.cloned.1.call-update) | async-done | bytes 2883600 | tf_op jit(solution)/shard_map/reduce_scatter | solution.py:154
  2858.8 3.6 fusion.83
  2862.3 357.2 %reduce-scatter.13.cloned.1.call-done = f32[64,2048]{1,0:T(8,128)} async-done(((f32[2048,2048]{1,0:T(8,128)}), f32[64,2048]{1,0:T(8,128)}) %reduce-scatter.13.cloned.1.call-update) | async-done | bytes 524304 | tf_op jit(solution)/shard_map/reduce_scatter | solution.py:166
  3219.6 969.5 %reduce-scatter.17.cloned.1.call-done = f32[176,2048]{1,0:T(8,128)} async-done(((f32[5632,2048]{1,0:T(8,128)}), f32[176,2048]{1,0:T(8,128)}) %reduce-scatter.17.cloned.1.call-update) | async-done | bytes 1441808 | tf_op jit(solution)/shard_map/reduce_scatter | solution.py:143
  (172 shorter events, 50.9 us)
Async XLA Ops:
  7.2 198.2 %copy-start.2 = (bf16[1,128,2048]{2,1,0:T(8,128)(2,1)S(1)}, bf16[1,128,2048]{2,1,0:T(8,128)(2,1)}, u32[]{:S(2)}) copy-start(bf16[1,128,2048]{2,1,0:T(8,128)(2,1)} %param.13) | copy-start | bytes 1572868
  7.2 122.8 %copy-start.45 = (s32[1,128]{1,0:T(1,128)S(1)}, s32[1,128]{1,0:T(1,128)}, u32[]{:S(2)}) copy-start(s32[1,128]{1,0:T(1,128)} %param.15) | copy-start | bytes 1540
  7.2 128.6 %copy-start.36 = (bf16[64,128]{1,0:T(8,128)(2,1)S(1)}, bf16[64,128]{1,0:T(8,128)(2,1)}, u32[]{:S(2)}) copy-start(bf16[64,128]{1,0:T(8,128)(2,1)} %param.19) | copy-start | bytes 49156
  7.2 204.5 %copy-start.43 = (s32[1,512]{1,0:T(1,128)S(1)}, s32[1,512]{1,0:T(1,128)}, u32[]{:S(2)}) copy-start(s32[1,512]{1,0:T(1,128)} %param.14) | copy-start | bytes 6148
  7.2 205.4 %all-gather.7.cloned.1.call-start = ((), (), s32[]{:S(2)}) async-start(), calls=%async_computation.6 | async-start | bytes 8650752 | tf_op jit(solution)/shard_map/all_gather | solution.py:66
  8.0 229.3 %all-gather.9.cloned.1.call-start = ((), (), s32[]{:S(2)}) async-start(), calls=%async_computation.7 | async-start | bytes 8650752 | tf_op jit(solution)/shard_map/all_gather | solution.py:69
  8.7 318.1 %all-gather.13.cloned.1.call-start = ((), (), s32[]{:S(2)}) async-start(), calls=%async_computation.9 | async-start | bytes 23789568 | tf_op jit(solution)/shard_map/all_gather | solution.py:116
  9.4 463.0 %all-gather.11.cloned.1.call-start = ((), (), s32[]{:S(2)}) async-start(), calls=%async_computation.8 | async-start | bytes 23789568 | tf_op jit(solution)/shard_map/all_gather | solution.py:115
  10.0 608.0 %all-gather.15.cloned.1.call-start = ((), (), s32[]{:S(2)}) async-start(), calls=%async_computation.10 | async-start | bytes 23789568 | tf_op jit(solution)/shard_map/all_gather | solution.py:117
  10.6 685.0 %reduce-scatter.9.cloned.1.call-start = ((), (), s32[]{:S(2)}) async-start(), calls=%async_computation.12 | async-start | bytes 327680 | tf_op jit(solution)/shard_map/reduce_scatter | solution.py:187
  55.0 169.3 %copy-start.39 = (f32[64]{0:T(128)}, f32[64]{0:T(128)S(1)}, u32[]{:S(2)}) copy-start(f32[64]{0:T(128)S(1)} %multiply_power_fusion) | copy-start | bytes 772
  56.9 167.5 %copy-start.37 = (f32[128]{0:T(128)}, f32[128]{0:T(128)S(1)}, u32[]{:S(2)}) copy-start(f32[128]{0:T(128)S(1)} %get-tuple-element.81) | copy-start | bytes 1540
  128.4 83.3 %copy-start.16 = (bf16[2048,128]{1,0:T(8,128)(2,1)}, bf16[2048,128]{1,0:T(8,128)(2,1)S(1)}, u32[]{:S(2)}) copy-start(bf16[2048,128]{1,0:T(8,128)(2,1)S(1)} %all_gather.44) | copy-start | bytes 1572868
  130.1 94.3 %copy-start.41 = (f32[128]{0:T(128)}, f32[128]{0:T(128)S(1)}, u32[]{:S(2)}) copy-start(f32[128]{0:T(128)S(1)} %convert_bitcast_fusion.1) | copy-start | bytes 1540
  130.3 94.1 %copy-start.25 = (bf16[128,1,64]{0,2,1:T(8,128)(2,1)}, bf16[128,1,64]{0,2,1:T(8,128)(2,1)S(1)}, u32[]{:S(2)}) copy-start(bf16[128,1,64]{0,2,1:T(8,128)(2,1)S(1)} %get-tuple-element.75) | copy-start | bytes 49156
  130.3 94.1 %copy-start.27 = (bf16[128,1,64]{0,2,1:T(8,128)(2,1)}, bf16[128,1,64]{0,2,1:T(8,128)(2,1)S(1)}, u32[]{:S(2)}) copy-start(bf16[128,1,64]{0,2,1:T(8,128)(2,1)S(1)} %get-tuple-element.76) | copy-start | bytes 49156
  135.8 95.5 %copy-start.21 = (bf16[512,1,128]{0,2,1:T(8,128)(2,1)}, bf16[512,1,128]{0,2,1:T(8,128)(2,1)S(1)}, u32[]{:S(2)}) copy-start(bf16[512,1,128]{0,2,1:T(8,128)(2,1)S(1)} %all-gather) | copy-start | bytes 393220
  205.8 18.6 copy-start.34
  633.4 13.2 copy-start.7
  675.0 41.0 reduce-scatter.7.cloned.1.call-start
  690.3 242.0 %reduce-scatter.11.cloned.1.call-start = ((), (), s32[]{:S(2)}) async-start(), calls=%async_computation.13 | async-start | bytes 19464192 | tf_op jit(solution)/shard_map/reduce_scatter | solution.py:196
  690.3 25.7 copy-start.40
  690.4 25.7 copy-start.42
  690.4 26.7 copy-start.3
  690.4 26.7 copy-start.38
  695.6 29.4 copy-start.11
  696.5 28.5 copy-start.23
  725.1 2133.7 %reduce-scatter.15.cloned.1.call-start = ((), (), s32[]{:S(2)}) async-start(), calls=%async_computation.15 | async-start | bytes 95158272 | tf_op jit(solution)/shard_map/reduce_scatter | solution.py:154
  768.1 2451.5 %reduce-scatter.13.cloned.1.call-start = ((), (), s32[]{:S(2)}) async-start(), calls=%async_computation.14 | async-start | bytes 17301504 | tf_op jit(solution)/shard_map/reduce_scatter | solution.py:166
  778.1 3411.0 %reduce-scatter.17.cloned.1.call-start = ((), (), s32[]{:S(2)}) async-start(), calls=%async_computation.16 | async-start | bytes 47579136 | tf_op jit(solution)/shard_map/reduce_scatter | solution.py:143
  807.5 12.9 copy-start.19
  820.1 42.4 %copy-start.44 = (f32[128]{0:T(128)S(1)}, f32[128]{0:T(128)}, u32[]{:S(2)}) copy-start(f32[128]{0:T(128)} %get-tuple-element.80) | copy-start | bytes 1540
  (25 other events, 116.3 us)
Sparse Core Ops, SparseCore 0:
  11.0 84.0 all-gather.6
  98.1 81.6 all-gather.8
  182.7 144.1 all-gather.12
  329.6 142.7 all-gather.10
  475.2 142.7 all-gather.14
  675.1 18.1 reduce-scatter.8
  695.9 20.0 reduce-scatter.6
  725.2 207.0 reduce-scatter.10
  934.6 1924.0 reduce-scatter.14
  2861.5 358.0 reduce-scatter.12
  3222.5 966.5 reduce-scatter.16
where the time goes:
time: 4200 us
  waiting for transfers between devices  3690 us (88%)
  blocking collectives  235 us (6%)
  matrix products  200 us (5%)
    reduce_scatter x1, waiting for transfers between devices, per_device(): lax.psum_scatter(contract_first(column_block, both_grads), ('seq', 'fsdp'...  1920 us
    reduce_scatter x1, waiting for transfers between devices, per_device(): lax.psum_scatter(contract_first(column_block, grad_out_low), ('seq', 'fsd...  970 us
    reduce_scatter x1, waiting for transfers between devices, per_device(): lax.psum_scatter(contract_first(column_block, grad_resid_low), ('seq', 'f...  357 us
    all_gather x1, waiting for transfers between devices, per_device(): lax.all_gather(w_gate, ('seq', 'fsdp'), axis=0, tiled=True)  133 us
    all_gather x1, waiting for transfers between devices, per_device(): lax.all_gather(w_down, ('seq', 'fsdp'), axis=0, tiled=True)  133 us
  transfers between devices with their start and end apart: 11, of which 8 were waited for; matrix products, arithmetic and copies ran while one was open for 4% of the time, Pallas kernels for 0%

commit v1 on v0

v1 whole, which is shorter than its diff:
```python
import functools

import jax
import jax.numpy as jnp
from jax import lax
from jax.experimental import pallas as pl
from jax.experimental.pallas import tpu as pltpu
from jax.sharding import PartitionSpec as P

epsilon = 1e-05
MESH = pl.DeviceIdType.MESH
VMEM_LIMIT = 60 * 2**20
bf16 = jnp.bfloat16
f32 = jnp.float32


def dot(left, right):
    return jnp.dot(left, right, preferred_element_type=f32)


def contract_last(left, right):
    return lax.dot_general(left, right, (((1,), (1,)), ((), ())), preferred_element_type=f32)


def contract_first(left, right):
    return lax.dot_general(left, right, (((0,), (0,)), ((), ())), preferred_element_type=f32)


class Arrival:
    def __init__(self, copy):
        self.copy, self.waited = copy, False

    def wait(self):
        if not self.waited:
            self.waited = True
            self.copy.wait_recv()


class Links:
    def __init__(self, send, recv):
        self.send, self.recv, self.sent = send, recv, []
        self.s, self.f = lax.axis_index("seq"), lax.axis_index("fsdp")

    def greet(self, masks):
        barrier = pltpu.get_barrier_semaphore()
        for a, b in masks:
            pl.semaphore_signal(
                barrier, inc=1, device_id=(self.s ^ a, self.f ^ b), device_id_type=MESH
            )
        pl.semaphore_wait(barrier, len(masks))

    def start(self, source, target, mask):
        i = len(self.sent)
        copy = pltpu.make_async_remote_copy(
            src_ref=source,
            dst_ref=target,
            send_sem=self.send.at[i],
            recv_sem=self.recv.at[i],
            device_id=(self.s ^ mask[0], self.f ^ mask[1]),
            device_id_type=MESH,
        )
        copy.start()
        self.sent.append(Arrival(copy))
        return self.sent[-1]

    def pass_on(self, block, mask):
        return self.start(block, block, mask)

    def finish(self):
        for arrival in self.sent:
            arrival.wait()
        for arrival in self.sent:
            arrival.copy.wait_send()


class Group:
    def __init__(self, links, own, full, FQ):
        self.links, self.full, self.FQ = links, full, FQ
        self.s, self.tb = links.s, links.f // FQ
        self.there = links.start(own, full.at[self.s, self.tb], (0, FQ))
        self.across = links.start(own, full.at[self.s, self.tb], (2, 0))
        links.start(own, full.at[self.s, self.tb], (1, 0))

    def relay(self):
        s, tb, full = self.s, self.tb, self.full
        self.there.wait()
        across_two = self.links.pass_on(full.at[s, 1 - tb], (2, 0))
        self.links.pass_on(full.at[s, 1 - tb], (1, 0))
        self.across.wait()
        self.links.pass_on(full.at[s ^ 2, tb], (1, 0))
        across_two.wait()
        self.links.pass_on(full.at[s ^ 2, 1 - tb], (1, 0))


class Local:
    def __init__(self, sems, pairs):
        self.copies = [pltpu.make_async_copy(a, b, sems.at[i]) for i, (a, b) in enumerate(pairs)]
        self.open = set(range(len(pairs)))
        for copy in self.copies:
            copy.start()

    def wait(self, *which):
        for i in which or sorted(self.open):
            self.open.discard(i)
            self.copies[i].wait()


def row_loop(rows, step, body):
    if rows % step:
        body(slice(0, rows))
        return

    @pl.loop(0, rows // step)
    def _(i):
        body(pl.ds(pl.multiple_of(i * step, step), step))


def communicate(
    body, args, outs, copies, collective_id, in_vmem=False, out_vmem=False, scratch=(), kept=1
):
    def spec(inside):
        return pl.BlockSpec(memory_space=pltpu.VMEM if inside else pl.ANY)

    return pl.pallas_call(
        body,
        out_shape=outs,
        in_specs=[spec(in_vmem)] * len(args),
        out_specs=[spec(out_vmem)] * len(outs),
        scratch_shapes=[
            pltpu.SemaphoreType.DMA((copies,)),
            pltpu.SemaphoreType.DMA((copies,)),
            pltpu.SemaphoreType.DMA((kept,)),
            *scratch,
        ],
        compiler_params=pltpu.CompilerParams(
            collective_id=collective_id, has_side_effects=True, vmem_limit_bytes=VMEM_LIMIT
        ),
    )(*args)


def shape(dims, kind=bf16):
    return jax.ShapeDtypeStruct(dims, kind)


def group_masks(FQ):
    return [(a, b) for a in range(4) for b in (0, FQ) if (a, b) != (0, 0)]


def gather_all_kernel(FH, FQ, *refs):
    tok, pos, wq, kvg, wo, gate, up, down, cot = refs[:9]
    tok_g, pos_g, q_g, kv_g, o_g, gate_g, up_g, down_g, cot_g = refs[9:18]
    send, recv, here = refs[18:]
    links = Links(send, recv)
    s, f = links.s, links.f
    tb, q = f // FQ, f % FQ
    t = 2 * s + tb
    evens = [2 * k for k in range(1, FH)]
    evens_q = [b for b in evens if b < FQ]
    links.greet([(a, 0) for a in (1, 2, 3)] + [(0, 1)] + [(0, b) for b in evens] + [(a, FQ) for a in (1, 2, 3)])
    local = Local(
        here,
        [
            (wq.at[s], q_g.at[s, f]),
            (kvg, kv_g.at[s, f]),
            (gate.at[t], gate_g.at[t, q]),
            (up.at[t], up_g.at[t, q]),
            (tok, tok_g.at[s]),
            (pos, pos_g.at[s]),
            (wo, o_g.at[f]),
            (down, down_g.at[q]),
            (cot, cot_g.at[s, tb]),
        ],
    )
    first = []
    for a in (1, 2, 3):
        first.append(links.start(wq.at[s ^ a], q_g.at[s, f], (a, 0)))
        first.append(links.start(kvg, kv_g.at[s, f], (a, 0)))
    tok_x = links.start(tok, tok_g.at[s], (2, 0))
    links.start(tok, tok_g.at[s], (1, 0))
    for a in (1, 2, 3):
        links.start(pos, pos_g.at[s], (a, 0))
    links.start(wo, o_g.at[f], (0, 1))
    o_z = [links.start(wo, o_g.at[f], (0, b)) for b in evens]
    local.wait(0, 1)
    for arrival in first:
        arrival.wait()
    for r in (q_g, kv_g):
        links.pass_on(r.at[:, f], (0, 1))
    qk_z = [[links.pass_on(r.at[:, f], (0, b)) for r in (q_g, kv_g)] for b in evens]
    ffn = []
    for a, b in group_masks(FQ):
        to = 2 * (s ^ a) + (tb ^ (b // FQ))
        ffn.append(links.start(gate.at[to], gate_g.at[t, q], (a, b)))
        ffn.append(links.start(up.at[to], up_g.at[t, q], (a, b)))
    cot_group = Group(links, cot, cot_g, FQ)
    for k, b in enumerate(evens):
        o_z[k].wait()
        links.pass_on(o_g.at[f ^ b], (0, 1))
        for r, arrival in zip((q_g, kv_g), qk_z[k]):
            arrival.wait()
            links.pass_on(r.at[:, f ^ b], (0, 1))
    tok_x.wait()
    links.pass_on(tok_g.at[s ^ 2], (1, 0))
    down_y = links.start(down, down_g.at[q], (0, 1))
    down_z = [links.start(down, down_g.at[q], (0, b)) for b in evens_q]
    local.wait(2, 3)
    for arrival in ffn:
        arrival.wait()
    gu_y = [links.pass_on(r.at[:, q], (0, 1)) for r in (gate_g, up_g)]
    gu_z = [[links.pass_on(r.at[:, q], (0, b)) for r in (gate_g, up_g)] for b in evens_q]
    cot_group.relay()
    half = down_g.shape[2] // 2
    low_half, high_half = pl.ds(0, half), pl.ds(half, half)
    low_t, high_t = pl.ds(0, 4), pl.ds(4, 4)
    down_y.wait()
    for b in evens_q:
        links.pass_on(down_g.at[q ^ 1, :, high_half], (0, b))
    for arrival, b in zip(down_z, evens_q):
        arrival.wait()
        links.pass_on(down_g.at[q ^ b, :, low_half], (0, 1))
    for r, arrival in zip((gate_g, up_g), gu_y):
        arrival.wait()
        for b in evens_q:
            links.pass_on(r.at[high_t, q ^ 1], (0, b))
    for arrivals, b in zip(gu_z, evens_q):
        for r, arrival in zip((gate_g, up_g), arrivals):
            arrival.wait()
            links.pass_on(r.at[low_t, q ^ b], (0, 1))
    links.finish()
    local.wait()


def gather_group_kernel(FQ, own, full, send, recv, here):
    links = Links(send, recv)
    links.greet([(1, 0), (2, 0), (0, FQ)])
    local = Local(here, [(own, full.at[links.s, links.f // FQ])])
    Group(links, own, full, FQ).relay()
    links.finish()
    local.wait()


def gather_row_kernel(own, full, send, recv, here):
    links = Links(send, recv)
    links.greet([(1, 0), (2, 0)])
    s = links.s
    local = Local(here, [(own, full.at[s])])
    across = links.start(own, full.at[s], (2, 0))
    links.start(own, full.at[s], (1, 0))
    across.wait()
    links.pass_on(full.at[s ^ 2], (1, 0))
    links.finish()
    local.wait()


class RowSum:
    def __init__(self, links, parts, from_core, from_x, to_x):
        self.links, self.parts = links, parts
        self.from_core, self.from_x, self.to_x = from_core, from_x, to_x
        self.x, self.core = links.s // 2, links.s % 2
        self.far = links.start(parts.at[1 - self.x, 1 - self.core], from_core.at[0], (1, 0))
        self.near = links.start(parts.at[self.x, 1 - self.core], from_core.at[1], (1, 0))

    def middle(self):
        self.far.wait()
        x, core = self.x, self.core

        def add(rows):
            total = self.parts[1 - x, core, rows].astype(f32) + self.from_core[0, rows].astype(f32)
            self.to_x[rows] = total.astype(bf16)

        row_loop(self.to_x.shape[0], 16, add)
        self.across = self.links.start(self.to_x, self.from_x, (2, 0))

    def total(self, rows):
        return (
            self.parts[self.x, self.core, rows].astype(f32)
            + self.from_core[1, rows].astype(f32)
            + self.from_x[rows].astype(f32)
        )

    def last(self, out):
        self.near.wait()
        self.across.wait()

        def add(rows):
            out[rows] = self.total(rows)

        row_loop(out.shape[0], 16, add)


def sum_row_kernel(parts, out, send, recv, here, from_core, from_x, to_x):
    links = Links(send, recv)
    links.greet([(1, 0), (2, 0)])
    total = RowSum(links, parts, from_core, from_x, to_x)
    total.middle()
    total.last(out)
    links.finish()


class GroupSum:
    def __init__(self, links, parts, bufs, FQ):
        self.links, self.parts, self.FQ = links, parts, FQ
        self.from_core, self.from_x, self.to_x, self.from_t, self.to_t = bufs
        self.x, self.core, self.tb = links.s // 2, links.s % 2, links.f // FQ
        self.far = links.start(parts.at[1 - self.x, 1 - self.core], self.from_core.at[0], (1, 0))
        self.near = links.start(parts.at[self.x, 1 - self.core], self.from_core.at[1], (1, 0))

    def to_other_x(self):
        self.far.wait()
        x, core = self.x, self.core

        def add(rows):
            for j in (0, 1):
                total = self.parts[1 - x, core, j, rows].astype(f32)
                self.to_x[j, rows] = (total + self.from_core[0, j, rows].astype(f32)).astype(bf16)

        row_loop(self.to_x.shape[1], 16, add)
        self.across = self.links.start(self.to_x, self.from_x, (2, 0))

    def total(self, j, rows):
        return (
            self.parts[self.x, self.core, j, rows].astype(f32)
            + self.from_core[1, j, rows].astype(f32)
            + self.from_x[j, rows].astype(f32)
        )

    def to_other_t(self):
        self.near.wait()
        self.across.wait()

        def add(rows):
            self.to_t[rows] = self.total(1 - self.tb, rows).astype(bf16)

        row_loop(self.to_t.shape[0], 16, add)
        self.there = self.links.start(self.to_t, self.from_t, (0, self.FQ))

    def last(self, out):
        self.there.wait()

        def add(rows):
            out[rows] = self.total(self.tb, rows) + self.from_t[rows].astype(f32)

        row_loop(out.shape[0], 16, add)


def group_sum_scratch(seq_len, width):
    block = (seq_len, width)
    return [
        pltpu.VMEM((2, 2, *block), bf16),
        pltpu.VMEM((2, *block), bf16),
        pltpu.VMEM((2, *block), bf16),
        pltpu.VMEM(block, bf16),
        pltpu.VMEM(block, bf16),
    ]


class WeightSum:
    def __init__(self, links, parts, total, bufs, first):
        self.links, self.parts, self.total = links, parts, total
        self.low_l, self.low_mid, self.low_w, self.high_w, self.high_mid, self.high_l = bufs
        leads, self.W = parts.shape[:2]
        self.rows = parts.shape[3]
        self.low, self.high = range(first), range(first, leads)
        self.l = links.f % 2
        self.w = (links.f // 2) % self.W
        if self.low:
            source = parts.at[pl.ds(0, first), :, 1 - self.l]
            self.by_l = links.start(source, self.low_l, (0, 1))
        if self.high:
            self.by_w = [
                links.start(
                    parts.at[pl.ds(first, leads - first), self.w ^ k], self.high_w.at[k - 1], (0, 2 * k)
                )
                for k in range(1, self.W)
            ]

    def middle(self):
        parts, w, l = self.parts, self.w, self.l
        if self.low:
            self.by_l.wait()
            for k in range(1, self.W):
                for i in self.low:

                    def add(rows, k=k, i=i):
                        total = parts[i, w ^ k, l, rows].astype(f32)
                        total += self.low_l[i, w ^ k, rows].astype(f32)
                        self.low_mid[k - 1, i, rows] = total.astype(bf16)

                    row_loop(self.rows, 16, add)
            self.low_end = [
                self.links.start(self.low_mid.at[k - 1], self.low_w.at[k - 1], (0, 2 * k))
                for k in range(1, self.W)
            ]
        if self.high:
            for arrival in self.by_w:
                arrival.wait()
            for j, i in enumerate(self.high):

                def add(rows, i=i, j=j):
                    total = parts[i, w, 1 - l, rows].astype(f32)
                    for k in range(1, self.W):
                        total += self.high_w[k - 1, j, 1 - l, rows].astype(f32)
                    self.high_mid[j, rows] = total.astype(bf16)

                row_loop(self.rows, 16, add)
            self.high_end = self.links.start(self.high_mid, self.high_l, (0, 1))

    def last(self):
        parts, w, l = self.parts, self.w, self.l
        if self.low:
            for arrival in self.low_end:
                arrival.wait()
            for i in self.low:

                def add(rows, i=i):
                    total = parts[i, w, l, rows].astype(f32) + self.low_l[i, w, rows].astype(f32)
                    for k in range(1, self.W):
                        total += self.low_w[k - 1, i, rows].astype(f32)
                    self.total[i, rows] = total.astype(self.total.dtype)

                row_loop(self.rows, 16, add)
        if self.high:
            self.high_end.wait()
            for j, i in enumerate(self.high):

                def add(rows, i=i, j=j):
                    total = parts[i, w, l, rows].astype(f32) + self.high_l[j, rows].astype(f32)
                    for k in range(1, self.W):
                        total += self.high_w[k - 1, j, l, rows].astype(f32)
                    self.total[i, rows] = total.astype(self.total.dtype)

                row_loop(self.rows, 16, add)


def weight_sum_scratch(parts, first):
    leads, W, _, rows, width = parts
    block = (rows, width)
    high = leads - first
    return [
        pltpu.VMEM((max(first, 1), W, *block), bf16),
        pltpu.VMEM((max(W - 1, 1), max(first, 1), *block), bf16),
        pltpu.VMEM((max(W - 1, 1), max(first, 1), *block), bf16),
        pltpu.VMEM((max(W - 1, 1), max(high, 1), 2, *block) if high else (8, 128), bf16),
        pltpu.VMEM((max(high, 1), *block) if high else (8, 128), bf16),
        pltpu.VMEM((max(high, 1), *block) if high else (8, 128), bf16),
    ]


def sum_ffn_kernel(FQ, *refs):
    back, out, gate, up, down = refs[:5]
    back_sum, out_sum, gate_own, up_own, down_sum = refs[5:10]
    send, recv, here = refs[10:13]
    refs = refs[13:]
    back_bufs, out_bufs, gate_bufs, up_bufs, down_bufs = refs[:5], refs[5:10], refs[10:16], refs[16:22], refs[22:28]
    gate_sum, up_sum = refs[28:]
    links = Links(send, recv)
    W = gate.shape[1]
    links.greet([(0, 1)] + [(0, 2 * k) for k in range(1, W)] + group_masks(FQ))
    t = 2 * links.s + links.f // FQ
    back_total = GroupSum(links, back, back_bufs, FQ)
    sums = [
        WeightSum(links, gate, gate_sum, gate_bufs, 4),
        WeightSum(links, up, up_sum, up_bufs, 4),
        WeightSum(links, down, down_sum, down_bufs, 1),
    ]
    out_total = GroupSum(links, out, out_bufs, FQ)
    back_total.to_other_x()
    out_total.to_other_x()
    back_total.to_other_t()
    out_total.to_other_t()
    back_total.last(back_sum)
    out_total.last(out_sum)
    for weight in sums:
        weight.middle()
    for weight in sums:
        weight.last()
    for a, b in group_masks(FQ):
        to = 2 * (links.s ^ a) + ((links.f // FQ) ^ (b // FQ))
        links.start(gate_sum.at[to], gate_own.at[t], (a, b))
        links.start(up_sum.at[to], up_own.at[t], (a, b))
    gate_own[t] = gate_sum[t]
    up_own[t] = up_sum[t]
    links.finish()


def sum_attention_kernel(FH, *refs):
    back, qo, kv = refs[:3]
    back_sum, q_own, o_sum, kv_sum = refs[3:7]
    send, recv, here, from_core, from_x, to_x = refs[7:13]
    qo_bufs, kv_bufs, qo_total, kv_total, kv_own = refs[13:19], refs[19:25], refs[25], refs[26], refs[27]
    links = Links(send, recv)
    links.greet([(1, 0), (2, 0), (3, 0), (0, 1)] + [(0, 2 * k) for k in range(1, FH)])
    s = links.s
    back_total = RowSum(links, back, from_core, from_x, to_x)
    kv_weight = WeightSum(links, kv, kv_total, kv_bufs, 4)
    qo_weight = WeightSum(links, qo, qo_total, qo_bufs, 8)
    back_total.middle()
    kv_weight.middle()
    qo_weight.middle()
    back_total.last(back_sum)
    kv_weight.last()
    for a in (1, 2, 3):
        links.start(kv_total.at[s ^ a], kv_own.at[s], (a, 0))
    qo_weight.last()
    for a in (1, 2, 3):
        links.start(qo_total.at[s ^ a], q_own.at[s], (a, 0))
    q_own[s] = qo_total[s]
    kv_own[s] = kv_total[s]
    for i in range(4):
        o_sum[i] = qo_total[4 + i].astype(f32)
    links.finish()

    def add(rows):
        total = kv_own[0, rows].astype(f32)
        for i in range(1, 4):
            total += kv_own[i, rows].astype(f32)
        kv_sum[rows] = total

    row_loop(kv_sum.shape[0], 16, add)


def angle_tables(position_row, head_size):
    half_head = head_size // 2
    frequency = 10000.0 ** (-jnp.arange(half_head, dtype=f32) * 2.0 / head_size)
    phase_angle = position_row.astype(f32)[:, None] * frequency[None, :]
    return (jnp.cos(phase_angle), jnp.sin(phase_angle))


def rotate(tensor_in, cosine, sine):
    half_head = tensor_in.shape[-1] // 2
    first_half = tensor_in[..., :half_head]
    second_half = tensor_in[..., half_head:]
    return jnp.concatenate(
        [first_half * cosine - second_half * sine, second_half * cosine + first_half * sine], -1
    )


def norm_back(grad_normed, inputs, inverse_rms, gain_full):
    scaled = grad_normed * gain_full
    width = inputs.shape[-1]
    inner_sum = jnp.sum(scaled * inputs, -1, keepdims=True)
    return inverse_rms * scaled - inputs * inverse_rms**3 * inner_sum / width


def per_device(
    S,
    F,
    tokens,
    segments,
    positions,
    gain_one,
    w_query,
    w_key,
    w_value,
    w_out,
    gain_two,
    w_gate,
    w_up,
    w_down,
    cotangent,
):
    T, D = tokens.shape[1:]
    head = w_key.shape[1]
    row_len = segments.shape[1]
    rows = w_query.shape[0]
    down_rows = w_down.shape[0]
    FF = w_gate.shape[1]
    FH, FQ = F // 2, F // 2
    W = FQ // 2
    TG = 2 * S
    HC = w_query.shape[1] // S
    heads = HC // head
    FC = FF // TG
    s = lax.axis_index("seq")

    def column_blocks(weight, n):
        return weight.reshape(rows, n, -1).transpose(1, 0, 2)

    gains = jnp.stack([gain_one, gain_two], 1)
    kvg = jnp.concatenate([w_key, w_value, gains, jnp.zeros((rows, head - 2), bf16)], 1)
    KV = kvg.shape[1]
    pos_block = jnp.broadcast_to(positions, (8, T))
    args = (
        tokens[0],
        pos_block,
        column_blocks(w_query, S),
        kvg,
        w_out,
        column_blocks(w_gate, TG),
        column_blocks(w_up, TG),
        w_down,
        cotangent[0],
    )
    outs = [
        shape((S, T, D)),
        shape((S, 8, T), jnp.int32),
        shape((S, F, rows, HC)),
        shape((S, F, rows, KV)),
        shape((F, rows, D)),
        shape((TG, FQ, rows, FC)),
        shape((TG, FQ, rows, FC)),
        shape((FQ, down_rows, D)),
        shape((S, 2, T, D)),
    ]
    tok, pos, wq, kvg, wo, gate_w, up_w, down_w, cot = communicate(
        functools.partial(gather_all_kernel, FH, FQ), args, outs, 120 + 24 * F, 0, kept=9
    )
    wq = wq.reshape(D, HC)
    kvg = kvg.reshape(D, KV)
    w_kv = kvg[:, : 2 * head]
    gain_one = kvg[:, 2 * head].astype(f32)
    gain_two = kvg[:, 2 * head + 1].astype(f32)
    wo = wo.reshape(HC, D)
    gate_w, up_w = gate_w.reshape(D, FC), up_w.reshape(D, FC)
    down_w = down_w.reshape(FC, D)
    cot = cot.reshape(TG * T, D)

    cosine, sine = angle_tables(pos[:, 0].reshape(row_len), head)
    row_in = tok.reshape(row_len, D).astype(f32)
    inverse_one = lax.rsqrt(jnp.mean(row_in * row_in, -1, keepdims=True) + epsilon)
    normed_one = (row_in * inverse_one * gain_one).astype(bf16)
    queries = dot(normed_one, wq)
    kv = dot(normed_one, w_kv)
    query_rot = rotate(
        queries.reshape(row_len, heads, head).transpose(1, 0, 2), cosine, sine
    ).astype(bf16)
    key_rot = rotate(kv[:, :head], cosine, sine).astype(bf16)
    value_low = kv[:, head:].astype(bf16)
    scale = head ** (-0.5)
    segment = segments[0]
    index = jnp.arange(row_len)
    allowed = (index[None, :] <= index[:, None]) & (segment[None, :] == segment[:, None])
    scores = jnp.einsum("htd,ud->htu", query_rot, key_rot, preferred_element_type=f32) * scale
    scores = jnp.where(allowed[None], scores, -1e30)
    row_max = jnp.max(scores, -1, keepdims=True)
    exp_scores = jnp.exp(scores - row_max)
    probs = exp_scores / jnp.sum(exp_scores, -1, keepdims=True)
    probs_low = probs.astype(bf16)
    attended = jnp.einsum("htu,ud->thd", probs_low, value_low, preferred_element_type=f32)
    attended = attended.reshape(row_len, HC).astype(bf16)
    part = dot(attended, wo).astype(bf16)

    def sum_row(parts, collective_id):
        block = (T, D)
        return communicate(
            sum_row_kernel,
            (parts.reshape(2, 2, T, D),),
            [shape(block, f32)],
            8,
            collective_id,
            in_vmem=True,
            out_vmem=True,
            scratch=[
                pltpu.VMEM((2, *block), bf16),
                pltpu.VMEM(block, bf16),
                pltpu.VMEM(block, bf16),
            ],
        )[0]

    inputs = tokens[0].astype(f32)
    residual = inputs + sum_row(part, 1)
    inverse_two = lax.rsqrt(jnp.mean(residual * residual, -1, keepdims=True) + epsilon)
    normed_two = (residual * inverse_two * gain_two).astype(bf16)
    (normed_all,) = communicate(
        functools.partial(gather_group_kernel, FQ), (normed_two,), [shape((S, 2, T, D))], 8, 2
    )
    normed_all = normed_all.reshape(TG * T, D)

    gate_proj = dot(normed_all, gate_w)
    up_proj = dot(normed_all, up_w)
    sig = jax.nn.sigmoid(gate_proj)
    inner = (gate_proj * sig * up_proj).astype(bf16)
    out_part = dot(inner, down_w).astype(bf16)
    grad_inner = contract_last(cot, down_w)
    grad_gate = (grad_inner * up_proj * sig * (1.0 + gate_proj * (1.0 - sig))).astype(bf16)
    grad_up = (grad_inner * gate_proj * sig).astype(bf16)
    back_part = (contract_last(grad_gate, gate_w) + contract_last(grad_up, up_w)).astype(bf16)
    half = D // 2
    grad_down_part = jnp.stack(
        [contract_first(inner, cot[:, :half]), contract_first(inner, cot[:, half:])]
    ).astype(bf16)
    grad_gate_part = contract_first(normed_all, grad_gate).astype(bf16)
    grad_up_part = contract_first(normed_all, grad_up).astype(bf16)

    gu_shape = (TG, W, 2, rows, FC)
    down_shape = (2, W, 2, down_rows, half)
    back_two, out_sum, grad_gate_own, grad_up_own, grad_down = communicate(
        functools.partial(sum_ffn_kernel, FQ),
        (
            back_part.reshape(2, 2, 2, T, D),
            out_part.reshape(2, 2, 2, T, D),
            grad_gate_part.reshape(gu_shape),
            grad_up_part.reshape(gu_shape),
            grad_down_part.reshape(down_shape),
        ),
        [
            shape((T, D), f32),
            shape((T, D), f32),
            shape((TG, rows, FC)),
            shape((TG, rows, FC)),
            shape((2, down_rows, half), f32),
        ],
        40 + 6 * F,
        3,
        in_vmem=True,
        out_vmem=True,
        scratch=group_sum_scratch(T, D) * 2
        + weight_sum_scratch(gu_shape, 4) * 2
        + weight_sum_scratch(down_shape, 1)
        + [pltpu.VMEM((TG, rows, FC), bf16)] * 2,
    )
    output = (residual + out_sum).astype(bf16)
    grad_w_gate = grad_gate_own.transpose(1, 0, 2).reshape(rows, FF).astype(f32)
    grad_w_up = grad_up_own.transpose(1, 0, 2).reshape(rows, FF).astype(f32)
    grad_w_down = grad_down.transpose(1, 0, 2).reshape(down_rows, D)

    grad_residual = cotangent[0].astype(f32) + norm_back(back_two, residual, inverse_two, gain_two)
    grad_gain_two = jnp.sum(back_two * residual * inverse_two, 0)
    (grad_row,) = communicate(
        gather_row_kernel, (grad_residual.astype(bf16),), [shape((S, T, D))], 4, 4
    )
    grad_row = grad_row.reshape(row_len, D)
    grad_attended = contract_last(grad_row, wo).astype(bf16)
    grad_att = grad_attended.reshape(row_len, heads, head).transpose(1, 0, 2)
    grad_probs = jnp.einsum("htd,ud->htu", grad_att, value_low, preferred_element_type=f32)
    delta = jnp.sum(probs * grad_probs, -1, keepdims=True)
    grad_scores = (probs * (grad_probs - delta)).astype(bf16)
    grad_query_rot = jnp.einsum("htu,ud->htd", grad_scores, key_rot, preferred_element_type=f32)
    grad_key_rot = jnp.einsum("htu,htd->ud", grad_scores, query_rot, preferred_element_type=f32)
    grad_value = jnp.einsum("htu,htd->ud", probs_low, grad_att, preferred_element_type=f32)
    grad_query = rotate(grad_query_rot * scale, cosine, -sine)
    grad_query = grad_query.transpose(1, 0, 2).reshape(row_len, HC).astype(bf16)
    grad_key = rotate(grad_key_rot * scale, cosine, -sine)
    grad_kv = jnp.concatenate([grad_key, grad_value], 1).astype(bf16)
    back_one_part = contract_last(grad_query, wq) + contract_last(grad_kv, w_kv)
    grad_gain_one = jnp.sum(back_one_part * row_in * inverse_one, 0)
    grad_wq_part = contract_first(normed_one, grad_query).astype(bf16)
    grad_wo_part = contract_first(attended, grad_row).astype(bf16)
    grad_wkv_part = contract_first(normed_one, grad_kv).astype(bf16)
    grad_gains = jnp.stack([grad_gain_one, grad_gain_two], 1).astype(bf16)
    grad_kvg_part = jnp.concatenate([grad_wkv_part, grad_gains, jnp.zeros((D, head - 2), bf16)], 1)
    qo_part = jnp.concatenate(
        [
            grad_wq_part.reshape(S, FH, 2, rows, HC),
            grad_wo_part.reshape(FH, 2, rows, S, HC).transpose(3, 0, 1, 2, 4),
        ]
    )
    kv_shape = (S, FH, 2, rows, KV)
    back_one, grad_wq_own, grad_wo, grad_kvg = communicate(
        functools.partial(sum_attention_kernel, FH),
        (
            back_one_part.astype(bf16).reshape(2, 2, T, D),
            qo_part,
            grad_kvg_part.reshape(kv_shape),
        ),
        [
            shape((T, D), f32),
            shape((S, rows, HC)),
            shape((S, rows, HC), f32),
            shape((rows, KV), f32),
        ],
        24 + 4 * F,
        5,
        in_vmem=True,
        out_vmem=True,
        scratch=[
            pltpu.VMEM((2, T, D), bf16),
            pltpu.VMEM((T, D), bf16),
            pltpu.VMEM((T, D), bf16),
            *weight_sum_scratch(qo_part.shape, 2 * S),
            *weight_sum_scratch(kv_shape, S),
            pltpu.VMEM((2 * S, rows, HC), bf16),
            pltpu.VMEM((S, rows, KV), bf16),
            pltpu.VMEM((S, rows, KV), bf16),
        ],
    )
    own_inverse = lax.rsqrt(jnp.mean(inputs * inputs, -1, keepdims=True) + epsilon)
    grad_tokens = grad_residual + norm_back(back_one, inputs, own_inverse, gain_one)
    grad_w_query = grad_wq_own.transpose(1, 0, 2).reshape(rows, S * HC).astype(f32)
    grad_w_out = grad_wo.transpose(1, 0, 2).reshape(rows, D)
    offset = s * T
    return (
        output[None],
        lax.dynamic_slice_in_dim(key_rot, offset, T)[None],
        lax.dynamic_slice_in_dim(value_low, offset, T)[None],
        grad_tokens[None],
        grad_kvg[:, 2 * head],
        grad_w_query,
        grad_kvg[:, :head],
        grad_kvg[:, head : 2 * head],
        grad_w_out,
        grad_kvg[:, 2 * head + 1],
        grad_w_gate,
        grad_w_up,
        grad_w_down,
    )


def solution(mesh):
    token_spec = P("fsdp", "seq", None)
    flat, matrix = P(("seq", "fsdp")), P(("seq", "fsdp"), None)
    return jax.shard_map(
        functools.partial(per_device, mesh.shape["seq"], mesh.shape["fsdp"]),
        mesh=mesh,
        in_specs=(
            token_spec,
            P("fsdp", None),
            P("fsdp", "seq"),
            flat,
            matrix,
            matrix,
            matrix,
            matrix,
            flat,
            matrix,
            matrix,
            matrix,
            token_spec,
        ),
        out_specs=(
            token_spec,
            token_spec,
            token_spec,
            token_spec,
            flat,
            matrix,
            matrix,
            matrix,
            matrix,
            flat,
            matrix,
            matrix,
            matrix,
        ),
        check_vma=False,
    )
```

time: 4200 us -> 733 us (0.17)
  waiting for transfers between devices: 3690 us -> 0 us
  Pallas kernels: 0 us -> 555 us
  blocking collectives: 235 us -> 0 us
  matrix products: 200 us -> 85 us
    reduce_scatter x6 -> x0, waiting for transfers between devices: 3340 us -> none  [the longest x1 1920 us: per_device(): lax.psum_scatter(contract_first(column_block, both_grads), ('seq', 'fsdp'...]
    pallas_call x0 -> x6, Pallas kernels: none -> 555 us  [communicate(): pl.pallas_call(body, out_shape=outs, in_specs=[spec(in_vmem)] * len(args)...]
    all_gather x5 -> x0, waiting for transfers between devices: 350 us -> none  [the longest x1 133 us: per_device(): lax.all_gather(w_gate, ('seq', 'fsdp'), axis=0, tiled=True)]
    all_gather x4 -> x0, blocking collectives: 153 us -> none  [the longest x1 71.5 us: per_device(): lax.all_gather(w_key, ('seq', 'fsdp'), axis=0, tiled=True)]
    unnamed x2 -> x0, blocking collectives: 82.9 us -> none
    dot_general x6 -> x7, matrix products: 82 us -> 22.9 us  [contract_first(): lax.dot_general(left, right, (((0,), (0,)), ((), ())), preferred_element_...]
    dot_general x9 -> x6, matrix products: 64.3 us -> 21.3 us  [contract_last(): lax.dot_general(left, right, (((1,), (1,)), ((), ())), preferred_element_...]
  transfers between devices with their start and end apart: 11 -> 0, of which waited for: 8 -> 0; matrix products, arithmetic and copies ran while one was open for 4% -> 0% of each run, Pallas kernels for 0% -> 0%
where the time goes in v1:
time: 733 us; the launch traced here: 719 us
  Pallas kernels  555 us (76%)
  matrix products  85 us (12%)
  local copies, waits for them, and re-layouts  48.3 us (7%)
  other arithmetic  28.2 us (4%)
    pallas_call x6, Pallas kernels, communicate(): pl.pallas_call(body, out_shape=outs, in_specs=[spec(in_vmem)] * len(args)...  555 us
    dot_general x6, matrix products, dot(): return jnp.dot(left, right, preferred_element_type=f32)  30.3 us
    dot_general x7, matrix products, contract_first(): lax.dot_general(left, right, (((0,), (0,)), ((), ())), preferred_element_...  22.9 us
    dot_general x6, matrix products, contract_last(): lax.dot_general(left, right, (((1,), (1,)), ((), ())), preferred_element_...  21.3 us

profile of v1, /device:TPU:0, one launch (start us, length us, event | category | flops | bytes accessed | tf_op | source)
XLA Modules:
  0.0 718.8 jit_solution(3653731193577082019)
XLA Ops:
  8.3 204.5 %shard_map.231 = (bf16[4,128,2048]{2,1,0:T(8,128)(2,1)}, s32[4,8,128]{2,1,0:T(8,128)}, bf16[4,8,64,512]{3,2,1,0:T(8,128)(2,1)}, bf16[4,8,64,384]{3,2,1,0:T(8,128...) custom-call(bf16[128,2048]{1,0:T(8,128)(2,1)} %bitcast.168, ...), custom_call_target="tpu_custom_call" | custom-call | tf_op jit(solution)/shard_map/pallas_call | solution.py:124
  212.8 2.6 slice_convert_fusion
  221.1 4.1 copy.46
  225.3 3.5 convolution_bitcast_fusion
  230.6 4.6 fusion.80
  235.2 2.8 convolution_convert_fusion.8
  238.1 2.6 convolution_convert_fusion.5
  240.7 19.0 %shard_map.232 = f32[128,2048]{1,0:T(8,128)} custom-call(bf16[2,2,128,2048]{3,2,1,0:T(8,128)(2,1)} %bitcast.185), custom_call_target="tpu_custom_call" | custom-call | tf_op jit(solution)/shard_map/pallas_call | solution.py:124
  264.8 40.8 %shard_map.233 = bf16[4,2,128,2048]{3,2,1,0:T(8,128)(2,1)} custom-call(bf16[128,2048]{1,0:T(8,128)(2,1)} %multiply_convert_fusion.4.own), custom_call_target="tpu_custom_call" | custom-call | tf_op jit(solution)/shard_map/pallas_call | solution.py:124
  305.7 8.0 %fusion.88 = f32[1024,704]{0,1:T(8,128)} fusion(bf16[1024,2048]{1,0:T(8,128)(2,1)} %bitcast.171, bf16[2048,704]{1,0:T(8,128)(2,1)} %bitcast.219), kind=kOutput, calls=%fused_computation.146 | convolution fusion | flops 2952790016 | bytes 9961472 | tf_op jit(solution)/shard_map/dot_general | solution.py:18
  313.7 4.9 fusion.87
  318.6 7.5 %multiply_convert_fusion.1 = (bf16[1024,704]{0,1:T(8,128)(2,1)S(1)}, bf16[1024,704]{0,1:T(8,128)(2,1)}, bf16[1024,704]{0,1:T(8,128)(2,1)S(1)}) fusion(f32[1024,704]{0,1:T(8,128)} %fusion.88, f32[1024,704]{0,1:T(8,128)} %fusion.87, bf16[1024,2048]{1,0:T(8,128)(2,1)S(1)} %bitcast.173, bf16[2048,704]{1,0:T(8,128)(2,1)S(1)} %bitcast.217), kind=kOutput, calls=%fused_computation.27 | convolution fusion | flops 2964324352 | bytes 17170432 | tf_op jit(solution)/shard_map/dot_general | solution.py:18
  331.4 4.5 convolution_convert_fusion.1
  335.9 4.6 copy.52
  340.5 7.3 %convolution_convert_fusion.2 = bf16[2048,704]{0,1:T(8,128)(2,1)} fusion(bf16[1024,704]{0,1:T(8,128)(2,1)} %get-tuple-element.60, bf16[1024,2048]{1,0:T(8,128)(2,1)} %bitcast.172), kind=kOutput, calls=%fused_computation.20 | convolution fusion | flops 2954231808 | bytes 8519680 | tf_op jit(solution)/shard_map/dot_general | solution.py:26
  347.8 4.8 copy.51
  352.6 7.9 %convolution_convert_fusion = bf16[1024,2048]{1,0:T(8,128)(2,1)} fusion(bf16[1024,704]{0,1:T(8,128)(2,1)} %copy-done.54, bf16[704,2048]{1,0:T(8,128)(2,1)} %bitcast.221), kind=kOutput, calls=%fused_computation.18 | convolution fusion | flops 2954887168 | bytes 8519680 | tf_op jit(solution)/shard_map/dot_general | solution.py:18
  360.5 3.5 fusion.89
  364.1 5.2 add_convert_fusion
  369.3 160.6 %shard_map.234 = (f32[128,2048]{1,0:T(8,128)}, f32[128,2048]{1,0:T(8,128)}, bf16[8,64,704]{2,1,0:T(8,128)(2,1)}, bf16[8,64,704]{2,1,0:T(8,128)(2,1)}, f32[2,176,1024]{2,1,0:T(8,128)}) custom-call(bf16[2,2,2,128,2048]{4,3,2,1,0:T(8,128)(2,1)} %bitcast.176, bf16[2,2,2,128,2048]{4,3,2,1,0:T(8,128)(2,1)} %bitcast.175, bf16[8,2,2,64,704]{4,3,2,1,0:T(8,128)(2,1)} %bitcast.164, ...), custom_call_target="tpu_custom_call" | custom-call | tf_op jit(solution)/shard_map/pallas_call | solution.py:124
  531.4 3.3 fusion.78
  534.7 17.3 %shard_map.235 = bf16[4,128,2048]{2,1,0:T(8,128)(2,1)} custom-call(bf16[128,2048]{1,0:T(8,128)(2,1)} %get-tuple-element.55.own), custom_call_target="tpu_custom_call" | custom-call | tf_op jit(solution)/shard_map/pallas_call | solution.py:124
  552.1 3.7 convolution_convert_fusion.7
  564.2 3.3 fusion.7
  569.7 4.5 convolution_convert_fusion.4
  574.2 2.6 convolution_convert_fusion.3
  576.8 3.3 reshape.368
  581.7 2.3 pad_maximum_fusion.refs_1_
  584.1 113.1 %shard_map.236 = (f32[128,2048]{1,0:T(8,128)}, bf16[4,64,512]{2,1,0:T(8,128)(2,1)}, f32[4,64,512]{2,1,0:T(8,128)}, f32[64,384]{1,0:T(8,128)}) custom-call(bf16[2,2,128,2048]{3,2,1,0:T(8,128)(2,1)} %bitcast.169, bf16[8,4,2,64,512]{4,3,2,1,0:T(8,128)(2,1)} %pad_maximum_fusion.refs_1_, bf16[4,4,2,64,384]{4,3,2,1,0:T(8,128)(2,1)} %bitcast.170), custom_call_target="tpu_custom_call" | custom-call | tf_op jit(solution)/shard_map/pallas_call | solution.py:124
  698.8 2.8 fusion.29
  706.9 2.8 reshape.376
  711.9 2.8 reshape.377
  (178 shorter events, 51.8 us)
Async XLA Ops:
  0.6 5.3 copy-start.28
  2.6 4.2 copy-start.44
  2.6 4.3 copy-start.34
  2.6 4.3 copy-start.35
  2.6 5.1 copy-start.45
  217.9 17.4 %copy-start.22 = (f32[512,256]{0,1:T(8,128)}, f32[512,256]{0,1:T(8,128)S(1)}, u32[]{:S(2)}) copy-start(f32[512,256]{0,1:T(8,128)S(1)} %fusion.36) | copy-start | bytes 1572868
  218.6 6.7 copy-start.30
  218.6 6.7 copy-start.40
  219.2 342.6 %copy-start.17 = (bf16[512,64]{0,1:T(8,128)(2,1)}, bf16[512,64]{0,1:T(8,128)(2,1)S(1)}, u32[]{:S(2)}) copy-start(bf16[512,64]{0,1:T(8,128)(2,1)S(1)} %get-tuple-element.79) | copy-start | bytes 196612
  219.2 342.6 %copy-start.19 = (bf16[512,64]{0,1:T(8,128)(2,1)}, bf16[512,64]{0,1:T(8,128)(2,1)S(1)}, u32[]{:S(2)}) copy-start(bf16[512,64]{0,1:T(8,128)(2,1)S(1)} %get-tuple-element.80) | copy-start | bytes 196612
  225.3 4.4 copy-start.38
  229.7 5.5 copy-start.24
  240.7 19.0 %copy-start.2 = (bf16[1,128,2048]{2,1,0:T(8,128)(2,1)S(1)}, bf16[1,128,2048]{2,1,0:T(8,128)(2,1)}, u32[]{:S(2)}) copy-start(bf16[1,128,2048]{2,1,0:T(8,128)(2,1)} %param.13) | copy-start | bytes 1572868
  305.6 8.1 %copy-start.46 = (bf16[4,2,128,2048]{3,2,1,0:T(8,128)(2,1)S(1)}, bf16[4,2,128,2048]{3,2,1,0:T(8,128)(2,1)}, u32[]{:S(2)}) copy-start(bf16[4,2,128,2048]{3,2,1,0:T(8,128)(2,1)} %get-tuple-element.36) | copy-start | bytes 12582916
  305.7 8.1 %copy-start.50 = (bf16[4,176,2048]{2,1,0:T(8,128)(2,1)S(1)}, bf16[4,176,2048]{2,1,0:T(8,128)(2,1)}, u32[]{:S(2)}) copy-start(bf16[4,176,2048]{2,1,0:T(8,128)(2,1)} %get-tuple-element.37) | copy-start | bytes 8650756
  313.7 4.9 copy-start.6
  313.7 4.9 copy-start.47
  326.1 5.3 copy-start.56
  352.6 7.9 %copy-start.49 = (bf16[8,4,64,704]{3,2,1,0:T(8,128)(2,1)S(1)}, bf16[8,4,64,704]{3,2,1,0:T(8,128)(2,1)}, u32[]{:S(2)}) copy-start(bf16[8,4,64,704]{3,2,1,0:T(8,128)(2,1)} %get-tuple-element.39) | copy-start | bytes 8650756
  352.6 7.9 %copy-start.55 = (bf16[1024,704]{0,1:T(8,128)(2,1)S(1)}, bf16[1024,704]{0,1:T(8,128)(2,1)}, u32[]{:S(2)}) copy-start(bf16[1024,704]{0,1:T(8,128)(2,1)} %get-tuple-element.60) | copy-start | bytes 4325380
  369.3 160.6 %copy-start.39 = (f32[128]{0:T(128)S(1)}, f32[128]{0:T(128)}, u32[]{:S(2)}) copy-start(f32[128]{0:T(128)} %get-tuple-element.87) | copy-start | bytes 1540
  369.3 162.1 %copy-start.9 = (bf16[1,128,2048]{2,1,0:T(8,128)(2,1)S(1)}, bf16[1,128,2048]{2,1,0:T(8,128)(2,1)}, u32[]{:S(2)}) copy-start(bf16[1,128,2048]{2,1,0:T(8,128)(2,1)} %param.25) | copy-start | bytes 1572868
  369.3 162.1 %copy-start.42 = (f32[128]{0:T(128)S(1)}, f32[128]{0:T(128)}, u32[]{:S(2)}) copy-start(f32[128]{0:T(128)} %get-tuple-element.86) | copy-start | bytes 1540
  569.7 4.5 copy-start.10
  569.7 4.5 copy-start.53
  584.0 113.2 %copy-start.3 = (bf16[1,128,2048]{2,1,0:T(8,128)(2,1)S(1)}, bf16[1,128,2048]{2,1,0:T(8,128)(2,1)}, u32[]{:S(2)}) copy-start(bf16[1,128,2048]{2,1,0:T(8,128)(2,1)} %param.13) | copy-start | bytes 1572868
  584.0 114.7 %copy-start.5 = (f32[128,2048]{1,0:T(8,128)S(1)}, f32[128,2048]{1,0:T(8,128)}, u32[]{:S(2)}) copy-start(f32[128,2048]{1,0:T(8,128)} %get-tuple-element.56) | copy-start | bytes 3145732
  697.2 4.4 copy-start.27
  698.8 4.5 copy-start.29
  698.8 5.8 copy-start.16
  704.8 4.9 copy-start.15
  709.8 4.9 copy-start.14
  (26 other events, 66.2 us)

commit v2 on v1

--- a/solution.py
+++ b/solution.py
@@ -38,7 +38,7 @@
 
 class Links:
     def __init__(self, send, recv):
-        self.send, self.recv, self.sent = send, recv, []
+        self.send, self.recv, self.sent, self.count = send, recv, [], 0
         self.s, self.f = lax.axis_index("seq"), lax.axis_index("fsdp")
 
     def greet(self, masks):
@@ -49,16 +49,19 @@
             )
         pl.semaphore_wait(barrier, len(masks))
 
-    def start(self, source, target, mask):
-        i = len(self.sent)
-        copy = pltpu.make_async_remote_copy(
+    def copy(self, source, target, device):
+        self.count += 1
+        return pltpu.make_async_remote_copy(
             src_ref=source,
             dst_ref=target,
-            send_sem=self.send.at[i],
-            recv_sem=self.recv.at[i],
-            device_id=(self.s ^ mask[0], self.f ^ mask[1]),
+            send_sem=self.send.at[self.count - 1],
+            recv_sem=self.recv.at[self.count - 1],
+            device_id=device,
             device_id_type=MESH,
         )
+
+    def start(self, source, target, mask):
+        copy = self.copy(source, target, (self.s ^ mask[0], self.f ^ mask[1]))
         copy.start()
         self.sent.append(Arrival(copy))
         return self.sent[-1]
@@ -118,14 +121,15 @@
 def communicate(
     body, args, outs, copies, collective_id, in_vmem=False, out_vmem=False, scratch=(), kept=1
 ):
-    def spec(inside):
-        return pl.BlockSpec(memory_space=pltpu.VMEM if inside else pl.ANY)
+    def specs(inside, n):
+        inside = [inside] * n if isinstance(inside, bool) else inside
+        return [pl.BlockSpec(memory_space=pltpu.VMEM if i else pl.ANY) for i in inside]
 
     return pl.pallas_call(
         body,
         out_shape=outs,
-        in_specs=[spec(in_vmem)] * len(args),
-        out_specs=[spec(out_vmem)] * len(outs),
+        in_specs=specs(in_vmem, len(args)),
+        out_specs=specs(out_vmem, len(outs)),
         scratch_shapes=[
             pltpu.SemaphoreType.DMA((copies,)),
             pltpu.SemaphoreType.DMA((copies,)),
@@ -146,17 +150,116 @@
     return [(a, b) for a in range(4) for b in (0, FQ) if (a, b) != (0, 0)]
 
 
-def gather_all_kernel(FH, FQ, *refs):
-    tok, pos, wq, kvg, wo, gate, up, down, cot = refs[:9]
-    tok_g, pos_g, q_g, kv_g, o_g, gate_g, up_g, down_g, cot_g = refs[9:18]
-    send, recv, here = refs[18:]
+class Line:
+    def __init__(self, links, views, FH):
+        self.links, self.views, self.FH = links, views, FH
+        self.h, self.l = links.f // 2, links.f % 2
+        self.right, self.left, self.pending = [], [], []
+
+    def here(self, h):
+        return self.views(2 * h + self.l)
+
+    def step(self, j):
+        h, FH = self.h, self.FH
+        rights = [
+            self.links.copy(block, block, (self.links.s, self.links.f + 2))
+            for block in self.here(lax.max(h - j, 0))
+        ]
+        lefts = [
+            self.links.copy(block, block, (self.links.s, self.links.f - 2))
+            for block in self.here(lax.min(h + j, FH - 1))
+        ]
+        for i in range(len(rights)):
+
+            @pl.when((h >= j) & (h < FH - 1))
+            def _():
+                rights[i].start()
+
+            @pl.when((h + j < FH) & (h > 0))
+            def _():
+                lefts[i].start()
+
+        self.right.append(rights)
+        self.left.append(lefts)
+
+    def arrived(self, j):
+        h, FH = self.h, self.FH
+        up = self.here(lax.max(h - 1 - j, 0))
+        down = self.here(lax.min(h + 1 + j, FH - 1))
+        for i in range(len(up)):
+            for blocks, copies, there in (
+                (up, self.right[j], h - 1 - j >= 0),
+                (down, self.left[j], h + 1 + j < FH),
+            ):
+                on = self.links.copy(
+                    blocks[i], blocks[i], (self.links.s, self.links.f ^ 1)
+                )
+                self.pending.append((on, there))
+
+                @pl.when(there)
+                def _():
+                    copies[i].wait_recv()
+                    on.start()
+
+    def finish(self):
+        h, FH = self.h, self.FH
+        for on, there in self.pending:
+
+            @pl.when(there)
+            def _():
+                on.wait_recv()
+                on.wait_send()
+
+        for j in range(FH - 1):
+            for i in range(len(self.right[j])):
+
+                @pl.when((h >= j) & (h < FH - 1))
+                def _():
+                    self.right[j][i].wait_send()
+
+                @pl.when((h + j < FH) & (h > 0))
+                def _():
+                    self.left[j][i].wait_send()
+
+
+def rows_of(ref):
+    return ref[...].reshape(-1, ref.shape[-1])
+
+
+def rotation(table):
+    half = table.shape[-1] // 2
+    swapped = pltpu.roll(table, half, 1)
+    first = lax.broadcasted_iota(jnp.int32, table.shape, 1) < half
+    return jnp.where(first, table, swapped), jnp.where(first, -swapped, table)
+
+
+def turn(vector, factors):
+    return vector * factors[0] + pltpu.roll(vector, vector.shape[-1] // 2, 1) * factors[1]
+
+
+def forward_kernel(FH, FQ, *refs):
+    tok, tab, wq, kvg, wo, gate, up, down, cot, bias = refs[:10]
+    (q_g, kv_g, o_g, gate_g, up_g, down_g, cot_g) = refs[10:17]
+    (tab_g, normed_one, q_rot, k_rot, v_low, attended, keys, values) = refs[17:25]
+    residual, normed_all, tok_g = refs[25:28]
+    send, recv, here, part, from_core, from_x, to_x, normed_two = refs[28:]
+    T = residual.shape[0]
+    D = residual.shape[1]
+    HC = attended.shape[1]
+    head = k_rot.shape[1]
+    row_len = k_rot.shape[0]
     links = Links(send, recv)
     s, f = links.s, links.f
+    x, core = s // 2, s % 2
     tb, q = f // FQ, f % FQ
     t = 2 * s + tb
-    evens = [2 * k for k in range(1, FH)]
-    evens_q = [b for b in evens if b < FQ]
-    links.greet([(a, 0) for a in (1, 2, 3)] + [(0, 1)] + [(0, b) for b in evens] + [(a, FQ) for a in (1, 2, 3)])
+    evens_q = [2 * k for k in range(1, FQ // 2)]
+    links.greet(
+        [(a, 0) for a in (1, 2, 3)]
+        + [(0, 1)]
+        + [(0, 2 * k) for k in range(1, FH)]
+        + [(a, FQ) for a in (1, 2, 3)]
+    )
     local = Local(
         here,
         [
@@ -164,9 +267,9 @@
             (kvg, kv_g.at[s, f]),
             (gate.at[t], gate_g.at[t, q]),
             (up.at[t], up_g.at[t, q]),
+            (wo, o_g.at[f]),
             (tok, tok_g.at[s]),
-            (pos, pos_g.at[s]),
-            (wo, o_g.at[f]),
+            (tab, tab_g.at[s]),
             (down, down_g.at[q]),
             (cot, cot_g.at[s, tb]),
         ],
@@ -175,32 +278,33 @@
     for a in (1, 2, 3):
         first.append(links.start(wq.at[s ^ a], q_g.at[s, f], (a, 0)))
         first.append(links.start(kvg, kv_g.at[s, f], (a, 0)))
+    local.wait(4)
+    o_line = Line(links, lambda place: [o_g.at[place]], FH)
+    qk_line = Line(links, lambda place: [q_g.at[:, place], kv_g.at[:, place]], FH)
+    o_line.step(0)
+    needed = [links.pass_on(o_g.at[f], (0, 1))]
     tok_x = links.start(tok, tok_g.at[s], (2, 0))
-    links.start(tok, tok_g.at[s], (1, 0))
-    for a in (1, 2, 3):
-        links.start(pos, pos_g.at[s], (a, 0))
-    links.start(wo, o_g.at[f], (0, 1))
-    o_z = [links.start(wo, o_g.at[f], (0, b)) for b in evens]
+    needed.append(links.start(tok, tok_g.at[s], (1, 0)))
+    needed += [links.start(tab, tab_g.at[s], (a, 0)) for a in (1, 2, 3)]
     local.wait(0, 1)
     for arrival in first:
         arrival.wait()
-    for r in (q_g, kv_g):
-        links.pass_on(r.at[:, f], (0, 1))
-    qk_z = [[links.pass_on(r.at[:, f], (0, b)) for r in (q_g, kv_g)] for b in evens]
+    qk_line.step(0)
+    needed += [links.pass_on(r.at[:, f], (0, 1)) for r in (q_g, kv_g)]
     ffn = []
     for a, b in group_masks(FQ):
         to = 2 * (s ^ a) + (tb ^ (b // FQ))
         ffn.append(links.start(gate.at[to], gate_g.at[t, q], (a, b)))
         ffn.append(links.start(up.at[to], up_g.at[t, q], (a, b)))
-    cot_group = Group(links, cot, cot_g, FQ)
-    for k, b in enumerate(evens):
-        o_z[k].wait()
-        links.pass_on(o_g.at[f ^ b], (0, 1))
-        for r, arrival in zip((q_g, kv_g), qk_z[k]):
-            arrival.wait()
-            links.pass_on(r.at[:, f ^ b], (0, 1))
     tok_x.wait()
-    links.pass_on(tok_g.at[s ^ 2], (1, 0))
+    needed.append(links.pass_on(tok_g.at[s ^ 2], (1, 0)))
+    for j in range(FH - 1):
+        o_line.arrived(j)
+        if j + 1 < FH - 1:
+            o_line.step(j + 1)
+        qk_line.arrived(j)
+        if j + 1 < FH - 1:
+            qk_line.step(j + 1)
     down_y = links.start(down, down_g.at[q], (0, 1))
     down_z = [links.start(down, down_g.at[q], (0, b)) for b in evens_q]
     local.wait(2, 3)
@@ -208,7 +312,84 @@
         arrival.wait()
     gu_y = [links.pass_on(r.at[:, q], (0, 1)) for r in (gate_g, up_g)]
     gu_z = [[links.pass_on(r.at[:, q], (0, b)) for r in (gate_g, up_g)] for b in evens_q]
-    cot_group.relay()
+    cot_group = Group(links, cot, cot_g, FQ)
+    for arrival in needed:
+        arrival.wait()
+    o_line.finish()
+    qk_line.finish()
+    local.wait(5, 6)
+
+    place = lax.broadcasted_iota(jnp.int32, (8, head), 0)
+    lane = lax.broadcasted_iota(jnp.int32, (8, head), 1)
+    pick = (place == lane).astype(bf16)
+    kv_full = rows_of(kv_g)
+    gains = contract_last(pick, kv_full[:, 2 * head :])
+    gain_one, gain_two = gains[0:1], gains[1:2]
+
+    @pl.loop(0, row_len // 16)
+    def _(i):
+        rows = pl.ds(pl.multiple_of(i * 16, 16), 16)
+        inner = pl.ds(pl.multiple_of(lax.rem(i, T // 16) * 16, 16), 16)
+        value = tok_g[i // (T // 16), inner].astype(f32)
+        inverse = lax.rsqrt(jnp.mean(value * value, -1, keepdims=True) + epsilon)
+        normed_one[rows] = (value * inverse * gain_one).astype(bf16)
+
+    factors = rotation(rows_of(tab_g))
+    kv = dot(normed_one[...], kv_full[:, : 2 * head])
+    k_rot[...] = turn(kv[:, :head], factors).astype(bf16)
+    v_low[...] = kv[:, head:].astype(bf16)
+    heads = HC // head
+    for n in range(0, heads, 2):
+        columns = slice(n * head, (n + 2) * head)
+        both = dot(normed_one[...], q_g[:, :, :, columns].reshape(D, 2 * head))
+        for j in (0, 1):
+            q_rot[n + j] = turn(both[:, j * head : (j + 1) * head], factors).astype(bf16)
+    keys[...] = k_rot[pl.ds(pl.multiple_of(s * T, T), T)]
+    values[...] = v_low[pl.ds(pl.multiple_of(s * T, T), T)]
+    scale = head ** (-0.5)
+    for r in range(row_len // T):
+        rows, seen = slice(r * T, (r + 1) * T), slice(0, (r + 1) * T)
+        for n in range(heads):
+            scores = contract_last(q_rot[n, rows], k_rot[seen]) * scale + bias[rows, seen]
+            scores = jnp.exp(scores - jnp.max(scores, -1, keepdims=True))
+            probs = (scores / jnp.sum(scores, -1, keepdims=True)).astype(bf16)
+            attended[rows, n * head : (n + 1) * head] = dot(probs, v_low[seen]).astype(bf16)
+
+    def project(x_to, core_to):
+        rows = attended[pl.ds(pl.multiple_of((2 * x_to + core_to) * T, T), T)]
+        for n in range(0, D, HC):
+            columns = slice(n, n + HC)
+            full = o_g[:, :, columns].reshape(HC, HC)
+            part[x_to, core_to, :, columns] = dot(rows, full).astype(bf16)
+
+    project(1 - x, 1 - core)
+    far = links.start(part.at[1 - x, 1 - core], from_core.at[0], (1, 0))
+    project(1 - x, core)
+    project(x, 1 - core)
+    near = links.start(part.at[x, 1 - core], from_core.at[1], (1, 0))
+    far.wait()
+
+    def add_x(rows):
+        total = part[1 - x, core, rows].astype(f32) + from_core[0, rows].astype(f32)
+        to_x[rows] = total.astype(bf16)
+
+    row_loop(T, 16, add_x)
+    across = links.start(to_x, from_x, (2, 0))
+    project(x, core)
+    near.wait()
+    across.wait()
+
+    def add_last(rows):
+        total = tok_g[s, rows].astype(f32) + part[x, core, rows].astype(f32)
+        total += from_core[1, rows].astype(f32) + from_x[rows].astype(f32)
+        residual[rows] = total
+        inverse = lax.rsqrt(jnp.mean(total * total, -1, keepdims=True) + epsilon)
+        normed_two[rows] = (total * inverse * gain_two).astype(bf16)
+
+    row_loop(T, 16, add_last)
+    normed_group = Group(links, normed_two, normed_all, FQ)
+    mine = pltpu.make_async_copy(normed_two, normed_all.at[s, tb], here.at[9])
+    mine.start()
     half = down_g.shape[2] // 2
     low_half, high_half = pl.ds(0, half), pl.ds(half, half)
     low_t, high_t = pl.ds(0, 4), pl.ds(4, 4)
@@ -226,17 +407,11 @@
         for r, arrival in zip((gate_g, up_g), arrivals):
             arrival.wait()
             links.pass_on(r.at[low_t, q ^ b], (0, 1))
+    cot_group.relay()
+    normed_group.relay()
     links.finish()
     local.wait()
-
-
-def gather_group_kernel(FQ, own, full, send, recv, here):
-    links = Links(send, recv)
-    links.greet([(1, 0), (2, 0), (0, FQ)])
-    local = Local(here, [(own, full.at[links.s, links.f // FQ])])
-    Group(links, own, full, FQ).relay()
-    links.finish()
-    local.wait()
+    mine.wait()
 
 
 def gather_row_kernel(own, full, send, recv, here):
@@ -286,15 +461,6 @@
             out[rows] = self.total(rows)
 
         row_loop(out.shape[0], 16, add)
-
-
-def sum_row_kernel(parts, out, send, recv, here, from_core, from_x, to_x):
-    links = Links(send, recv)
-    links.greet([(1, 0), (2, 0)])
-    total = RowSum(links, parts, from_core, from_x, to_x)
-    total.middle()
-    total.last(out)
-    links.finish()
 
 
 class GroupSum:
@@ -579,31 +745,58 @@
     gains = jnp.stack([gain_one, gain_two], 1)
     kvg = jnp.concatenate([w_key, w_value, gains, jnp.zeros((rows, head - 2), bf16)], 1)
     KV = kvg.shape[1]
-    pos_block = jnp.broadcast_to(positions, (8, T))
-    args = (
-        tokens[0],
-        pos_block,
-        column_blocks(w_query, S),
-        kvg,
-        w_out,
-        column_blocks(w_gate, TG),
-        column_blocks(w_up, TG),
-        w_down,
-        cotangent[0],
-    )
+    table = jnp.concatenate(angle_tables(positions[0], head), 1)
+    segment = segments[0]
+    index = jnp.arange(row_len)
+    allowed = (index[None, :] <= index[:, None]) & (segment[None, :] == segment[:, None])
+    bias = jnp.where(allowed, 0.0, -1e30)
     outs = [
-        shape((S, T, D)),
-        shape((S, 8, T), jnp.int32),
-        shape((S, F, rows, HC)),
-        shape((S, F, rows, KV)),
-        shape((F, rows, D)),
-        shape((TG, FQ, rows, FC)),
-        shape((TG, FQ, rows, FC)),
-        shape((FQ, down_rows, D)),
-        shape((S, 2, T, D)),
+        (True, (S, F, rows, HC), bf16),
+        (True, (S, F, rows, KV), bf16),
+        (True, (F, rows, D), bf16),
+        (False, (TG, FQ, rows, FC), bf16),
+        (False, (TG, FQ, rows, FC), bf16),
+        (False, (FQ, down_rows, D), bf16),
+        (False, (S, 2, T, D), bf16),
+        (True, (S, T, head), f32),
+        (True, (row_len, D), bf16),
+        (True, (heads, row_len, head), bf16),
+        (True, (row_len, head), bf16),
+        (True, (row_len, head), bf16),
+        (True, (row_len, HC), bf16),
+        (True, (T, head), bf16),
+        (True, (T, head), bf16),
+        (True, (T, D), f32),
+        (False, (S, 2, T, D), bf16),
+        (True, (S, T, D), bf16),
     ]
-    tok, pos, wq, kvg, wo, gate_w, up_w, down_w, cot = communicate(
-        functools.partial(gather_all_kernel, FH, FQ), args, outs, 120 + 24 * F, 0, kept=9
+    (wq, kvg, wo, gate_w, up_w, down_w, cot, table, normed_one, query_rot, key_rot, value_low, attended, keys, values, residual, normed_all, tok) = communicate(
+        functools.partial(forward_kernel, FH, FQ),
+        (
+            tokens[0],
+            table,
+            column_blocks(w_query, S),
+            kvg,
+            w_out,
+            column_blocks(w_gate, TG),
+            column_blocks(w_up, TG),
+            w_down,
+            cotangent[0],
+            bias,
+        ),
+        [shape(dims, kind) for _, dims, kind in outs],
+        120 + 18 * F,
+        0,
+        in_vmem=[False] * 9 + [True],
+        out_vmem=[inside for inside, _, _ in outs],
+        kept=10,
+        scratch=[
+            pltpu.VMEM((2, 2, T, D), bf16),
+            pltpu.VMEM((2, T, D), bf16),
+            pltpu.VMEM((T, D), bf16),
+            pltpu.VMEM((T, D), bf16),
+            pltpu.VMEM((T, D), bf16),
+        ],
     )
     wq = wq.reshape(D, HC)
     kvg = kvg.reshape(D, KV)
@@ -614,57 +807,12 @@
     gate_w, up_w = gate_w.reshape(D, FC), up_w.reshape(D, FC)
     down_w = down_w.reshape(FC, D)
     cot = cot.reshape(TG * T, D)
-
-    cosine, sine = angle_tables(pos[:, 0].reshape(row_len), head)
+    normed_all = normed_all.reshape(TG * T, D)
+    cosine, sine = jnp.split(table.reshape(row_len, head), 2, 1)
+    inputs = tokens[0].astype(f32)
     row_in = tok.reshape(row_len, D).astype(f32)
     inverse_one = lax.rsqrt(jnp.mean(row_in * row_in, -1, keepdims=True) + epsilon)
-    normed_one = (row_in * inverse_one * gain_one).astype(bf16)
-    queries = dot(normed_one, wq)
-    kv = dot(normed_one, w_kv)
-    query_rot = rotate(
-        queries.reshape(row_len, heads, head).transpose(1, 0, 2), cosine, sine
-    ).astype(bf16)
-    key_rot = rotate(kv[:, :head], cosine, sine).astype(bf16)
-    value_low = kv[:, head:].astype(bf16)
-    scale = head ** (-0.5)
-    segment = segments[0]
-    index = jnp.arange(row_len)
-    allowed = (index[None, :] <= index[:, None]) & (segment[None, :] == segment[:, None])
-    scores = jnp.einsum("htd,ud->htu", query_rot, key_rot, preferred_element_type=f32) * scale
-    scores = jnp.where(allowed[None], scores, -1e30)
-    row_max = jnp.max(scores, -1, keepdims=True)
-    exp_scores = jnp.exp(scores - row_max)
-    probs = exp_scores / jnp.sum(exp_scores, -1, keepdims=True)
-    probs_low = probs.astype(bf16)
-    attended = jnp.einsum("htu,ud->thd", probs_low, value_low, preferred_element_type=f32)
-    attended = attended.reshape(row_len, HC).astype(bf16)
-    part = dot(attended, wo).astype(bf16)
-
-    def sum_row(parts, collective_id):
-        block = (T, D)
-        return communicate(
-            sum_row_kernel,
-            (parts.reshape(2, 2, T, D),),
-            [shape(block, f32)],
-            8,
-            collective_id,
-            in_vmem=True,
-            out_vmem=True,
-            scratch=[
-                pltpu.VMEM((2, *block), bf16),
-                pltpu.VMEM(block, bf16),
-                pltpu.VMEM(block, bf16),
-            ],
-        )[0]
-
-    inputs = tokens[0].astype(f32)
-    residual = inputs + sum_row(part, 1)
     inverse_two = lax.rsqrt(jnp.mean(residual * residual, -1, keepdims=True) + epsilon)
-    normed_two = (residual * inverse_two * gain_two).astype(bf16)
-    (normed_all,) = communicate(
-        functools.partial(gather_group_kernel, FQ), (normed_two,), [shape((S, 2, T, D))], 8, 2
-    )
-    normed_all = normed_all.reshape(TG * T, D)
 
     gate_proj = dot(normed_all, gate_w)
     up_proj = dot(normed_all, up_w)
@@ -723,6 +871,11 @@
     grad_attended = contract_last(grad_row, wo).astype(bf16)
     grad_att = grad_attended.reshape(row_len, heads, head).transpose(1, 0, 2)
     grad_probs = jnp.einsum("htd,ud->htu", grad_att, value_low, preferred_element_type=f32)
+    scale = head ** (-0.5)
+    scores = jnp.einsum("htd,ud->htu", query_rot, key_rot, preferred_element_type=f32) * scale
+    exp_scores = jnp.exp(scores + bias - jnp.max(scores + bias, -1, keepdims=True))
+    probs = exp_scores / jnp.sum(exp_scores, -1, keepdims=True)
+    probs_low = probs.astype(bf16)
     delta = jnp.sum(probs * grad_probs, -1, keepdims=True)
     grad_scores = (probs * (grad_probs - delta)).astype(bf16)
     grad_query_rot = jnp.einsum("htu,ud->htd", grad_scores, key_rot, preferred_element_type=f32)
@@ -778,11 +931,10 @@
     grad_tokens = grad_residual + norm_back(back_one, inputs, own_inverse, gain_one)
     grad_w_query = grad_wq_own.transpose(1, 0, 2).reshape(rows, S * HC).astype(f32)
     grad_w_out = grad_wo.transpose(1, 0, 2).reshape(rows, D)
-    offset = s * T
     return (
         output[None],
-        lax.dynamic_slice_in_dim(key_rot, offset, T)[None],
-        lax.dynamic_slice_in_dim(value_low, offset, T)[None],
+        keys[None],
+        values[None],
         grad_tokens[None],
         grad_kvg[:, 2 * head],
         grad_w_query,

time: 733 us -> 644 us (0.88)
  the two profiles are of different devices: /device:TPU:0 before, /device:TPU:13 now
where the time goes in v2:
time: 644 us; the launch traced here: 635 us
  Pallas kernels  503 us (78%)
  matrix products  73.4 us (11%)
  local copies, waits for them, and re-layouts  36.7 us (6%)
  other arithmetic  20.9 us (3%)
    pallas_call x4, Pallas kernels, communicate(): pl.pallas_call(body, out_shape=outs, in_specs=specs(in_vmem, len(args)),...  503 us
    dot_general x6, matrix products, contract_last(): lax.dot_general(left, right, (((1,), (1,)), ((), ())), preferred_element_...  20.5 us
    dot_general x7, matrix products, contract_first(): lax.dot_general(left, right, (((0,), (0,)), ((), ())), preferred_element_...  20.2 us
    dot_general x3, matrix products, dot(): return jnp.dot(left, right, preferred_element_type=f32)  19.9 us

profile of v2, /device:TPU:13, one launch (start us, length us, event | category | flops | bytes accessed | tf_op | source)
XLA Modules:
  0.0 635.3 jit_solution(15637716519290834528)
XLA Ops:
  2.4 1.9 reshape.243
  4.3 1.9 reshape.244
  10.6 200.8 %shard_map.228 = (bf16[4,8,64,512]{3,2,1,0:T(8,128)(2,1)}, bf16[4,8,64,384]{3,2,1,0:T(8,128)(2,1)}, bf16[8,64,2048]{2,1,0:T(8,128)(2,1)}, bf16[8,4,64,704]{3,2,1...) custom-call(bf16[128,2048]{1,0:T(8,128)(2,1)} %bitcast.149, ...), custom_call_target="tpu_custom_call" | custom-call | tf_op jit(solution)/shard_map/pallas_call | solution.py:128
  211.4 6.6 %fusion.61 = f32[1024,704]{0,1:T(8,128)S(1)} fusion(bf16[1024,2048]{1,0:T(8,128)(2,1)} %bitcast.180, bf16[2048,704]{1,0:T(8,128)(2,1)} %bitcast.189), kind=kOutput, calls=%fused_computation.105 | convolution fusion | flops 2952790016 | bytes 9961472 | tf_op jit(solution)/shard_map/dot_general | solution.py:18
  218.0 3.2 fusion.60
  221.2 5.7 multiply_convert_fusion.1
  228.6 1.7 fusion.15
  230.3 1.9 pad_maximum_fusion.1.refs_4_
  233.6 3.5 fusion.62
  237.1 5.3 add_convert_fusion
  242.5 3.4 convolution_convert_fusion.1
  245.9 2.8 copy.46
  248.7 5.8 convolution_convert_fusion.2
  254.5 2.8 copy.45
  257.3 7.7 %convolution_convert_fusion = bf16[1024,2048]{1,0:T(8,128)(2,1)} fusion(bf16[1024,704]{0,1:T(8,128)(2,1)} %copy-done.38, bf16[704,2048]{1,0:T(8,128)(2,1)} %bitcast.191), kind=kOutput, calls=%fused_computation.11 | convolution fusion | flops 2954887168 | bytes 8519680 | tf_op jit(solution)/shard_map/dot_general | solution.py:18
  265.0 158.5 %shard_map.229 = (f32[128,2048]{1,0:T(8,128)}, f32[128,2048]{1,0:T(8,128)}, bf16[8,64,704]{2,1,0:T(8,128)(2,1)}, bf16[8,64,704]{2,1,0:T(8,128)(2,1)}, f32[2,176,1024]{2,1,0:T(8,128)}) custom-call(bf16[2,2,2,128,2048]{4,3,2,1,0:T(8,128)(2,1)} %bitcast.150, bf16[2,2,2,128,2048]{4,3,2,1,0:T(8,128)(2,1)} %bitcast.151, bf16[8,2,2,64,704]{4,3,2,1,0:T(8,128)(2,1)} %bitcast.145, ...), custom_call_target="tpu_custom_call" | custom-call | tf_op jit(solution)/shard_map/pallas_call | solution.py:128
  423.7 2.5 slice_convert_fusion
  426.8 2.8 fusion.52
  429.6 18.6 %shard_map.230 = bf16[4,128,2048]{2,1,0:T(8,128)(2,1)} custom-call(bf16[128,2048]{1,0:T(8,128)(2,1)} %get-tuple-element.73.own), custom_call_target="tpu_custom_call" | custom-call | tf_op jit(solution)/shard_map/pallas_call | solution.py:128
  448.2 4.4 convolution_convert_fusion.6
  453.0 4.5 fusion.55
  457.5 3.0 multiply_reduce_fusion.1
  467.3 3.3 fusion.22
  474.7 3.3 fusion.2
  480.1 4.3 convolution_convert_fusion.4
  484.4 2.6 convolution_convert_fusion.3
  487.1 3.3 reshape.262
  492.0 2.5 pad_maximum_fusion.refs_1_
  494.5 124.7 %shard_map.231 = (f32[128,2048]{1,0:T(8,128)}, bf16[4,64,512]{2,1,0:T(8,128)(2,1)}, f32[4,64,512]{2,1,0:T(8,128)}, f32[64,384]{1,0:T(8,128)}) custom-call(bf16[2,2,128,2048]{3,2,1,0:T(8,128)(2,1)} %bitcast.147, bf16[8,4,2,64,512]{4,3,2,1,0:T(8,128)(2,1)} %pad_maximum_fusion.refs_1_, bf16[4,4,2,64,384]{4,3,2,1,0:T(8,128)(2,1)} %bitcast.148), custom_call_target="tpu_custom_call" | custom-call | tf_op jit(solution)/shard_map/pallas_call | solution.py:128
  621.1 2.8 fusion.30
  628.0 1.7 reshape.270
  630.8 1.7 reshape.271
  (134 shorter events, 34.3 us)
Async XLA Ops:
  2.3 5.3 copy-start.26
  4.2 4.7 copy-start.18
  4.2 5.4 copy-start.27
  4.2 5.5 copy-start.28
  4.3 5.6 copy-start.24
  4.3 5.6 copy-start.25
  211.4 6.6 %copy-start.30 = (bf16[4,2,128,2048]{3,2,1,0:T(8,128)(2,1)S(1)}, bf16[4,2,128,2048]{3,2,1,0:T(8,128)(2,1)}, u32[]{:S(2)}) copy-start(bf16[4,2,128,2048]{3,2,1,0:T(8,128)(2,1)} %get-tuple-element.41) | copy-start | bytes 12582916
  211.4 6.6 %copy-start.33 = (bf16[4,176,2048]{2,1,0:T(8,128)(2,1)S(1)}, bf16[4,176,2048]{2,1,0:T(8,128)(2,1)}, u32[]{:S(2)}) copy-start(bf16[4,176,2048]{2,1,0:T(8,128)(2,1)} %get-tuple-element.42) | copy-start | bytes 8650756
  218.0 3.2 copy-start.29
  218.0 3.2 copy-start.31
  230.2 2.9 copy-start.32
  230.2 3.3 copy-start.39
  233.6 3.6 copy-start.40
  265.0 158.6 %copy-start.1 = (f32[128,2048]{1,0:T(8,128)S(1)}, f32[128,2048]{1,0:T(8,128)}, u32[]{:S(2)}) copy-start(f32[128,2048]{1,0:T(8,128)} %get-tuple-element.40) | copy-start | bytes 3145732
  423.5 3.0 copy-start.6
  448.2 4.4 copy-start
  448.2 4.7 copy-start.20
  453.0 4.5 copy-start.36
  453.0 4.5 copy-start.37
  457.4 3.5 copy-start.4
  467.3 3.3 copy-start.34
  480.1 4.4 copy-start.8
  480.1 4.4 copy-start.35
  494.5 124.7 %copy-start.5 = (f32[2048,1]{1,0:T(8,128)S(1)}, f32[2048,1]{1,0:T(8,128)}, u32[]{:S(2)}) copy-start(f32[2048,1]{1,0:T(8,128)} %get-tuple-element.80) | copy-start | bytes 24580
  494.5 125.0 %copy-start.3 = (bf16[1,128,2048]{2,1,0:T(8,128)(2,1)S(1)}, bf16[1,128,2048]{2,1,0:T(8,128)(2,1)}, u32[]{:S(2)}) copy-start(bf16[1,128,2048]{2,1,0:T(8,128)(2,1)} %param.13) | copy-start | bytes 1572868
  619.5 4.4 copy-start.17
  621.1 3.7 copy-start.15
  621.1 4.5 copy-start.19
  621.1 5.8 copy-start.14
  629.8 2.6 copy-start.11
  630.8 2.9 copy-start.23
  630.8 3.5 copy-start.22
  (9 other events, 14.4 us)

commit v3 on v2

v3 whole, which is shorter than its diff:
```python
import functools

import jax
import jax.numpy as jnp
from jax import lax
from jax.experimental import pallas as pl
from jax.experimental.pallas import tpu as pltpu
from jax.sharding import PartitionSpec as P

epsilon = 1e-05
MESH = pl.DeviceIdType.MESH
VMEM_LIMIT = 64 * 2**20 - 2**18
bf16 = jnp.bfloat16
f32 = jnp.float32


def dot(left, right):
    return jnp.dot(left, right, preferred_element_type=f32)


def contract_last(left, right):
    return lax.dot_general(left, right, (((1,), (1,)), ((), ())), preferred_element_type=f32)


def contract_first(left, right):
    return lax.dot_general(left, right, (((0,), (0,)), ((), ())), preferred_element_type=f32)


class Arrival:
    def __init__(self, copy):
        self.copy, self.waited, self.left = copy, False, False

    def wait(self):
        if not self.waited:
            self.waited = True
            self.copy.wait_recv()

    def wait_sent(self):
        if not self.left:
            self.left = True
            self.copy.wait_send()


class Links:
    def __init__(self, send, recv):
        self.send, self.recv, self.sent, self.count = send, recv, [], 0
        self.s, self.f = lax.axis_index("seq"), lax.axis_index("fsdp")

    def greet(self, masks):
        barrier = pltpu.get_barrier_semaphore()
        for a, b in masks:
            pl.semaphore_signal(
                barrier, inc=1, device_id=(self.s ^ a, self.f ^ b), device_id_type=MESH
            )
        pl.semaphore_wait(barrier, len(masks))

    def copy(self, source, target, device):
        self.count += 1
        return pltpu.make_async_remote_copy(
            src_ref=source,
            dst_ref=target,
            send_sem=self.send.at[self.count - 1],
            recv_sem=self.recv.at[self.count - 1],
            device_id=device,
            device_id_type=MESH,
        )

    def start(self, source, target, mask):
        copy = self.copy(source, target, (self.s ^ mask[0], self.f ^ mask[1]))
        copy.start()
        self.sent.append(Arrival(copy))
        return self.sent[-1]

    def pass_on(self, block, mask):
        return self.start(block, block, mask)

    def finish(self):
        for arrival in self.sent:
            arrival.wait()
        for arrival in self.sent:
            arrival.wait_sent()


class Group:
    def __init__(self, links, own, full, FQ):
        self.links, self.full = links, full
        self.x, self.core, self.tb = links.s // 2, links.s % 2, links.f // FQ
        place = full.at[self.x, self.tb, self.core]
        self.there = links.start(own, place, (0, FQ))
        self.across = links.start(own, place, (2, 0))
        links.start(own, place, (1, 0))

    def relay(self):
        x, tb, core, full = self.x, self.tb, self.core, self.full
        self.there.wait()
        across_two = self.links.pass_on(full.at[x, 1 - tb, core], (2, 0))
        self.links.pass_on(full.at[x, 1 - tb, core], (1, 0))
        self.across.wait()
        self.links.pass_on(full.at[1 - x, tb, core], (1, 0))
        across_two.wait()
        self.links.pass_on(full.at[1 - x, 1 - tb, core], (1, 0))


class Local:
    def __init__(self, sems, pairs, base=0):
        self.copies = [
            pltpu.make_async_copy(a, b, sems.at[base + i]) for i, (a, b) in enumerate(pairs)
        ]
        self.open = set(range(len(pairs)))
        for copy in self.copies:
            copy.start()

    def wait(self, *which):
        for i in which or sorted(self.open):
            self.open.discard(i)
            self.copies[i].wait()


def row_loop(rows, step, body):
    block_loop(1, rows, step, lambda i, part: body(part))


def block_loop(n, rows, step, body):
    if rows % step:
        for i in range(n):
            body(i, slice(0, rows))
        return
    steps = rows // step

    @pl.loop(0, n * steps)
    def _(k):
        body(k // steps, pl.ds(pl.multiple_of(lax.rem(k, steps) * step, step), step))


def communicate(
    body, args, outs, copies, collective_id, in_vmem=False, out_vmem=False, scratch=(), kept=1
):
    def specs(inside, n):
        inside = [inside] * n if isinstance(inside, bool) else inside
        return [pl.BlockSpec(memory_space=pltpu.VMEM if i else pl.ANY) for i in inside]

    return pl.pallas_call(
        body,
        out_shape=outs,
        in_specs=specs(in_vmem, len(args)),
        out_specs=specs(out_vmem, len(outs)),
        scratch_shapes=[
            pltpu.SemaphoreType.DMA((copies,)),
            pltpu.SemaphoreType.DMA((copies,)),
            pltpu.SemaphoreType.DMA((kept,)),
            *scratch,
        ],
        compiler_params=pltpu.CompilerParams(
            collective_id=collective_id, has_side_effects=True, vmem_limit_bytes=VMEM_LIMIT
        ),
    )(*args)


def shape(dims, kind=bf16):
    return jax.ShapeDtypeStruct(dims, kind)


def group_masks(FQ):
    return [(a, b) for a in range(4) for b in (0, FQ) if (a, b) != (0, 0)]


class Line:
    def __init__(self, links, views, FH):
        self.links, self.views, self.FH = links, views, FH
        self.h, self.l = links.f // 2, links.f % 2
        self.right, self.left, self.pending = [], [], []

    def here(self, h):
        return self.views(2 * h + self.l)

    def step(self, j):
        h, FH = self.h, self.FH
        rights = [
            self.links.copy(block, block, (self.links.s, self.links.f + 2))
            for block in self.here(lax.max(h - j, 0))
        ]
        lefts = [
            self.links.copy(block, block, (self.links.s, self.links.f - 2))
            for block in self.here(lax.min(h + j, FH - 1))
        ]
        for i in range(len(rights)):

            @pl.when((h >= j) & (h < FH - 1))
            def _():
                rights[i].start()

            @pl.when((h + j < FH) & (h > 0))
            def _():
                lefts[i].start()

        self.right.append(rights)
        self.left.append(lefts)

    def arrived(self, j):
        h, FH = self.h, self.FH
        up = self.here(lax.max(h - 1 - j, 0))
        down = self.here(lax.min(h + 1 + j, FH - 1))
        for i in range(len(up)):
            for blocks, copies, there in (
                (up, self.right[j], h - 1 - j >= 0),
                (down, self.left[j], h + 1 + j < FH),
            ):
                on = self.links.copy(
                    blocks[i], blocks[i], (self.links.s, self.links.f ^ 1)
                )
                self.pending.append((on, there))

                @pl.when(there)
                def _():
                    copies[i].wait_recv()
                    on.start()

    def finish(self):
        h, FH = self.h, self.FH
        for on, there in self.pending:

            @pl.when(there)
            def _():
                on.wait_recv()
                on.wait_send()

        for j in range(FH - 1):
            for i in range(len(self.right[j])):

                @pl.when((h >= j) & (h < FH - 1))
                def _():
                    self.right[j][i].wait_send()

                @pl.when((h + j < FH) & (h > 0))
                def _():
                    self.left[j][i].wait_send()


def rows_of(ref):
    return ref[...].reshape(-1, ref.shape[-1])


def rotation(table):
    half = table.shape[-1] // 2
    swapped = pltpu.roll(table, half, 1)
    first = lax.broadcasted_iota(jnp.int32, table.shape, 1) < half
    return jnp.where(first, table, swapped), jnp.where(first, -swapped, table)


def turn(vector, factors):
    return vector * factors[0] + pltpu.roll(vector, vector.shape[-1] // 2, 1) * factors[1]


def forward_kernel(FH, FQ, *refs):
    tok, tab, wq, kvg, wo, gate, up, down, cot, bias = refs[:10]
    (q_g, kv_g, o_g, gate_g, up_g, down_g, cot_g) = refs[10:17]
    (tab_g, normed_one, q_rot, k_rot, v_low, attended, keys, values) = refs[17:25]
    residual, normed_all, gains = refs[25:28]
    send, recv, here, tok_g, part, from_core, from_x, to_x, normed_two = refs[28:]
    T = residual.shape[0]
    D = residual.shape[1]
    HC = attended.shape[1]
    head = k_rot.shape[1]
    row_len = k_rot.shape[0]
    links = Links(send, recv)
    s, f = links.s, links.f
    x, core = s // 2, s % 2
    tb, q = f // FQ, f % FQ
    t = 2 * s + tb
    evens_q = [2 * k for k in range(1, FQ // 2)]
    links.greet(
        [(a, 0) for a in (1, 2, 3)]
        + [(0, 1)]
        + [(0, 2 * k) for k in range(1, FH)]
        + [(a, FQ) for a in (1, 2, 3)]
    )
    local = Local(
        here,
        [
            (wq.at[s], q_g.at[s, f]),
            (kvg, kv_g.at[s, f]),
            (gate.at[t], gate_g.at[t, q]),
            (up.at[t], up_g.at[t, q]),
            (wo, o_g.at[f]),
            (tok, tok_g.at[s]),
            (tab, tab_g.at[s]),
            (down, down_g.at[q]),
            (cot, cot_g.at[x, tb, core]),
        ],
    )
    first = []
    for a in (1, 2, 3):
        first.append(links.start(wq.at[s ^ a], q_g.at[s, f], (a, 0)))
        first.append(links.start(kvg, kv_g.at[s, f], (a, 0)))
    local.wait(4)
    o_line = Line(links, lambda place: [o_g.at[place]], FH)
    qk_line = Line(links, lambda place: [q_g.at[:, place], kv_g.at[:, place]], FH)
    o_line.step(0)
    needed = [links.pass_on(o_g.at[f], (0, 1))]
    tok_x = links.start(tok, tok_g.at[s], (2, 0))
    needed.append(links.start(tok, tok_g.at[s], (1, 0)))
    needed += [links.start(tab, tab_g.at[s], (a, 0)) for a in (1, 2, 3)]
    local.wait(0, 1)
    for arrival in first:
        arrival.wait()
    qk_line.step(0)
    needed += [links.pass_on(r.at[:, f], (0, 1)) for r in (q_g, kv_g)]
    ffn = []
    for a, b in group_masks(FQ):
        to = 2 * (s ^ a) + (tb ^ (b // FQ))
        ffn.append(links.start(gate.at[to], gate_g.at[t, q], (a, b)))
        ffn.append(links.start(up.at[to], up_g.at[t, q], (a, b)))
    tok_x.wait()
    needed.append(links.pass_on(tok_g.at[s ^ 2], (1, 0)))
    for j in range(FH - 1):
        o_line.arrived(j)
        if j + 1 < FH - 1:
            o_line.step(j + 1)
        qk_line.arrived(j)
        if j + 1 < FH - 1:
            qk_line.step(j + 1)
    down_y = links.start(down, down_g.at[q], (0, 1))
    down_z = [links.start(down, down_g.at[q], (0, b)) for b in evens_q]
    local.wait(2, 3)
    for arrival in ffn:
        arrival.wait()
    gu_y = [links.pass_on(r.at[:, q], (0, 1)) for r in (gate_g, up_g)]
    gu_z = [[links.pass_on(r.at[:, q], (0, b)) for r in (gate_g, up_g)] for b in evens_q]
    cot_group = Group(links, cot, cot_g, FQ)
    for arrival in needed:
        arrival.wait()
    o_line.finish()
    qk_line.finish()
    local.wait(5, 6)

    place = lax.broadcasted_iota(jnp.int32, (8, head), 0)
    lane = lax.broadcasted_iota(jnp.int32, (8, head), 1)
    pick = (place == lane).astype(bf16)
    kv_full = rows_of(kv_g)
    gains[...] = contract_last(pick, kv_full[:, 2 * head :])
    gain_one, gain_two = gains[0:1], gains[1:2]

    @pl.loop(0, row_len // 16)
    def _(i):
        rows = pl.ds(pl.multiple_of(i * 16, 16), 16)
        inner = pl.ds(pl.multiple_of(lax.rem(i, T // 16) * 16, 16), 16)
        value = tok_g[i // (T // 16), inner].astype(f32)
        inverse = lax.rsqrt(jnp.mean(value * value, -1, keepdims=True) + epsilon)
        normed_one[rows] = (value * inverse * gain_one).astype(bf16)

    factors = rotation(rows_of(tab_g))
    kv = dot(normed_one[...], kv_full[:, : 2 * head])
    k_rot[...] = turn(kv[:, :head], factors).astype(bf16)
    v_low[...] = kv[:, head:].astype(bf16)
    heads = HC // head
    for n in range(0, heads, 2):
        columns = slice(n * head, (n + 2) * head)
        both = dot(normed_one[...], q_g[:, :, :, columns].reshape(D, 2 * head))
        for j in (0, 1):
            q_rot[n + j] = turn(both[:, j * head : (j + 1) * head], factors).astype(bf16)
    keys[...] = k_rot[pl.ds(pl.multiple_of(s * T, T), T)]
    values[...] = v_low[pl.ds(pl.multiple_of(s * T, T), T)]
    scale = head ** (-0.5)
    for r in range(row_len // T):
        rows, seen = slice(r * T, (r + 1) * T), slice(0, (r + 1) * T)
        for n in range(heads):
            scores = contract_last(q_rot[n, rows], k_rot[seen]) * scale + bias[rows, seen].astype(f32)
            scores = jnp.exp(scores - jnp.max(scores, -1, keepdims=True))
            probs = (scores / jnp.sum(scores, -1, keepdims=True)).astype(bf16)
            attended[rows, n * head : (n + 1) * head] = dot(probs, v_low[seen]).astype(bf16)

    def project(x_to, core_to):
        rows = attended[pl.ds(pl.multiple_of((2 * x_to + core_to) * T, T), T)]
        for n in range(0, D, HC):
            columns = slice(n, n + HC)
            full = o_g[:, :, columns].reshape(HC, HC)
            part[x_to, core_to, :, columns] = dot(rows, full).astype(bf16)

    project(1 - x, 1 - core)
    far = links.start(part.at[1 - x, 1 - core], from_core.at[0], (1, 0))
    project(1 - x, core)
    project(x, 1 - core)
    near = links.start(part.at[x, 1 - core], from_core.at[1], (1, 0))
    far.wait()

    def add_x(rows):
        total = part[1 - x, core, rows].astype(f32) + from_core[0, rows].astype(f32)
        to_x[rows] = total.astype(bf16)

    row_loop(T, 16, add_x)
    across = links.start(to_x, from_x, (2, 0))
    project(x, core)
    near.wait()
    across.wait()

    def add_last(rows):
        total = tok_g[s, rows].astype(f32) + part[x, core, rows].astype(f32)
        total += from_core[1, rows].astype(f32) + from_x[rows].astype(f32)
        residual[rows] = total
        inverse = lax.rsqrt(jnp.mean(total * total, -1, keepdims=True) + epsilon)
        normed_two[rows] = (total * inverse * gain_two).astype(bf16)

    row_loop(T, 16, add_last)
    normed_group = Group(links, normed_two, normed_all, FQ)
    mine = pltpu.make_async_copy(normed_two, normed_all.at[x, tb, core], here.at[9])
    mine.start()
    half = down_g.shape[2] // 2
    low_half, high_half = pl.ds(0, half), pl.ds(half, half)
    low_t, high_t = pl.ds(0, 4), pl.ds(4, 4)
    down_y.wait()
    for b in evens_q:
        links.pass_on(down_g.at[q ^ 1, :, high_half], (0, b))
    for arrival, b in zip(down_z, evens_q):
        arrival.wait()
        links.pass_on(down_g.at[q ^ b, :, low_half], (0, 1))
    for r, arrival in zip((gate_g, up_g), gu_y):
        arrival.wait()
        for b in evens_q:
            links.pass_on(r.at[high_t, q ^ 1], (0, b))
    for arrivals, b in zip(gu_z, evens_q):
        for r, arrival in zip((gate_g, up_g), arrivals):
            arrival.wait()
            links.pass_on(r.at[low_t, q ^ b], (0, 1))
    cot_group.relay()
    normed_group.relay()
    links.finish()
    local.wait()
    mine.wait()


class RowSum:
    def __init__(self, links, parts, from_core, from_x):
        self.links, self.parts, self.from_core, self.from_x = links, parts, from_core, from_x
        self.x, self.core = links.s // 2, links.s % 2

    def far(self):
        x, core = 1 - self.x, 1 - self.core
        self.to_far = self.links.start(self.parts.at[x, core], self.from_core.at[x], (1, 0))

    def near(self):
        x, core = self.x, 1 - self.core
        self.to_near = self.links.start(self.parts.at[x, core], self.from_core.at[x], (1, 0))

    def middle(self):
        self.to_far.wait()
        x, core = 1 - self.x, self.core

        def add(rows):
            total = self.parts[x, core, rows].astype(f32) + self.from_core[x, rows].astype(f32)
            self.parts[x, core, rows] = total.astype(bf16)

        row_loop(self.from_x.shape[0], 16, add)
        self.across = self.links.start(self.parts.at[x, core], self.from_x, (2, 0))

    def arrive(self):
        self.to_near.wait()
        self.across.wait()

    def total(self, rows):
        return (
            self.parts[self.x, self.core, rows].astype(f32)
            + self.from_core[self.x, rows].astype(f32)
            + self.from_x[rows].astype(f32)
        )


class GroupSum:
    def __init__(self, links, parts, from_core, from_x, from_t, FQ):
        self.links, self.parts, self.FQ = links, parts, FQ
        self.from_core, self.from_x, self.from_t = from_core, from_x, from_t
        self.x, self.core, self.tb = links.s // 2, links.s % 2, links.f // FQ
        self.T = from_t.shape[0]
        self.by_core, self.by_x, self.sent = {}, {}, []

    def send_core(self, name, x, tb):
        arrival = self.links.start(
            self.parts.at[x, tb, 1 - self.core], self.from_core.at[x, tb], (1, 0)
        )
        self.by_core[name] = arrival
        self.sent.append(arrival)

    def far(self, name, tb):
        self.by_core[name].wait()
        x, core = 1 - self.x, self.core

        def add(rows):
            total = self.parts[x, tb, core, rows].astype(f32)
            total += self.from_core[x, tb, rows].astype(f32)
            self.parts[x, tb, core, rows] = total.astype(bf16)

        row_loop(self.T, 16, add)
        arrival = self.links.start(self.parts.at[x, tb, core], self.from_x.at[tb], (2, 0))
        self.by_x[name] = arrival
        self.sent.append(arrival)

    def partial(self, tb, rows):
        return (
            self.parts[self.x, tb, self.core, rows].astype(f32)
            + self.from_core[self.x, tb, rows].astype(f32)
            + self.from_x[tb, rows].astype(f32)
        )

    def to_t(self, core_name, x_name):
        self.by_core[core_name].wait()
        self.by_x[x_name].wait()
        tb = 1 - self.tb

        def add(rows):
            self.parts[self.x, tb, self.core, rows] = self.partial(tb, rows).astype(bf16)

        row_loop(self.T, 16, add)
        self.there = self.links.start(
            self.parts.at[self.x, tb, self.core], self.from_t, (0, self.FQ)
        )
        self.sent.append(self.there)

    def arrive(self, core_name, x_name):
        self.by_core[core_name].wait()
        self.by_x[x_name].wait()
        self.there.wait()

    def total(self, rows):
        return self.partial(self.tb, rows) + self.from_t[rows].astype(f32)


class PieceByL:
    def __init__(self, links, parts, by_l, by_w):
        self.links, self.parts, self.by_l, self.by_w = links, parts, by_l, by_w
        self.n, self.W, _, self.rows = parts.shape[:4]
        self.l = links.f % 2
        self.w = (links.f // 2) % self.W
        self.first = links.start(parts.at[:, :, 1 - self.l], by_l, (0, 1))

    def middle(self):
        self.first.wait()
        l, self.second = self.l, []
        for k in range(1, self.W):
            w = self.w ^ k

            def add(i, rows, w=w):
                total = self.parts[i, w, l, rows].astype(f32) + self.by_l[i, w, rows].astype(f32)
                self.parts[i, w, l, rows] = total.astype(bf16)

            block_loop(self.n, self.rows, 16, add)
            self.second.append(
                self.links.start(self.parts.at[:, w, l], self.by_w.at[k - 1], (0, 2 * k))
            )

    def last(self, store=None):
        for arrival in self.second:
            arrival.wait()

        def add(i, rows):
            total = self.parts[i, self.w, self.l, rows].astype(f32)
            total += self.by_l[i, self.w, rows].astype(f32)
            for k in range(1, self.W):
                total += self.by_w[k - 1, i, rows].astype(f32)
            if store is None:
                self.parts[i, self.w, self.l, rows] = total.astype(bf16)
            else:
                store(i, rows, total)

        block_loop(self.n, self.rows, 16, add)


class PieceByW:
    def __init__(self, links, parts, by_l, by_w):
        self.links, self.parts, self.by_l, self.by_w = links, parts, by_l, by_w
        self.n, self.W, _, self.rows = parts.shape[:4]
        self.l = links.f % 2
        self.w = (links.f // 2) % self.W
        self.first = [
            links.start(parts.at[:, self.w ^ k], by_w.at[k - 1], (0, 2 * k))
            for k in range(1, self.W)
        ]

    def partial(self, i, l, rows):
        total = self.parts[i, self.w, l, rows].astype(f32)
        for k in range(1, self.W):
            total += self.by_w[k - 1, i, l, rows].astype(f32)
        return total

    def middle(self):
        for arrival in self.first:
            arrival.wait()
        l = 1 - self.l

        def add(i, rows):
            self.parts[i, self.w, l, rows] = self.partial(i, l, rows).astype(bf16)

        block_loop(self.n, self.rows, 16, add)
        self.second = self.links.start(self.parts.at[:, self.w, l], self.by_l, (0, 1))

    def last(self, store=None):
        self.second.wait()

        def add(i, rows):
            total = self.partial(i, self.l, rows) + self.by_l[i, rows].astype(f32)
            if store is None:
                self.parts[i, self.w, self.l, rows] = total.astype(bf16)
            else:
                store(i, rows, total)

        block_loop(self.n, self.rows, 16, add)


def by_l_scratch(n, W, rows, width):
    return [pltpu.VMEM((n, W, rows, width), bf16), pltpu.VMEM((W - 1, n, rows, width), bf16)]


def by_w_scratch(n, W, rows, width):
    return [pltpu.VMEM((n, rows, width), bf16), pltpu.VMEM((W - 1, n, 2, rows, width), bf16)]


def norm_back(grad_normed, inputs, gain):
    inverse = lax.rsqrt(jnp.mean(inputs * inputs, -1, keepdims=True) + epsilon)
    scaled = grad_normed * gain
    inner_sum = jnp.sum(scaled * inputs, -1, keepdims=True)
    grad = inverse * scaled - inputs * (inverse**3 * inner_sum / inputs.shape[-1])
    return grad, inputs * inverse


def backward_kernel(FH, FQ, *refs):
    (normed_in, cot_in, gate_in, up_in, down_in, q_in, kv_in, o_in) = refs[:8]
    (normed_one_in, q_rot_in, k_rot_in, v_in, attended_in, tab_in) = refs[8:14]
    tok_in, bias, residual, gains = refs[14:18]
    output, grad_tokens, gate_own, up_own, grad_down, q_own, o_sum, kv_sum = refs[18:26]
    send, recv, here, gate, up, down, q_w, kv_w, o_w = refs[26:35]
    grad_row, kv_own, gain_sums = refs[35:38]
    back_bufs, out_bufs = refs[38:42], refs[42:46]
    normed, cot, grad_gate, grad_up, tab, grad_k, grad_v = refs[46:53]
    bufs = refs[53:]
    links = Links(send, recv)
    s, f = links.s, links.f
    x, core = s // 2, s % 2
    tb, q = f // FQ, f % FQ
    t = 2 * s + tb
    T, D = residual.shape
    S, F, rows_w, HC = q_w.shape
    head = grad_k.shape[1]
    row_len = grad_k.shape[0]
    heads = HC // head
    TG, W, _, _, FC = gate.shape
    two = 2 * T
    links.greet(
        [(a, 0) for a in (1, 2, 3)]
        + [(0, 1)]
        + [(0, 2 * k) for k in range(1, FH)]
        + [(a, FQ) for a in (1, 2, 3)]
    )
    back = GroupSum(links, *back_bufs, FQ)
    out = GroupSum(links, *out_bufs, FQ)
    back_parts, out_parts = back.parts, out.parts
    ffn = {}

    def feed_forward():
        order = [(1 - x, 1 - tb), (1 - x, tb), (x, 1 - tb), (x, tb)]
        pairs = [(gate_in, gate), (up_in, up), (down_in, down)]
        for place in order:
            pairs += [(normed_in.at[place], normed.at[place]), (cot_in.at[place], cot.at[place])]
        loads = Local(here, pairs)
        slot = D // 2
        tiles = [slice(n, min(n + 256, FC)) for n in range(0, FC, 256)]
        for j, (cx, ct) in enumerate(order):
            if j == 0:
                loads.wait(0, 1, 2)
            loads.wait(3 + 2 * j, 4 + 2 * j)
            n = normed[cx, ct].reshape(two, D)
            c = cot[cx, ct].reshape(two, D)
            for tile in tiles:
                gate_proj = dot(n, gate[:, :, :, :, tile].reshape(D, -1))
                up_proj = dot(n, up[:, :, :, :, tile].reshape(D, -1))
                grad_inner = contract_last(c, down[...].reshape(FC, D)[tile])
                sig = jax.nn.sigmoid(gate_proj)
                silu = gate_proj * sig
                place = pl.ds(pl.multiple_of(cx * slot + tile.start, 128), tile.stop - tile.start)
                hidden = (silu * up_proj).astype(bf16)
                o_w[pl.ds(ct * (F // 2), F // 2), :, place] = hidden.reshape(F // 2, rows_w, -1)
                grad_up[cx, ct, :, tile] = (grad_inner * silu).astype(bf16)
                slope = sig * (1.0 + gate_proj * (1.0 - sig))
                grad_gate[cx, ct, :, tile] = (grad_inner * up_proj * slope).astype(bf16)
            for i in range(0, TG, 2):
                columns = slice(i * FQ * rows_w, (i + 2) * FQ * rows_w)
                total = contract_last(grad_gate[cx, ct], gate[i : i + 2].reshape(-1, FC))
                total += contract_last(grad_up[cx, ct], up[i : i + 2].reshape(-1, FC))
                back_parts[cx, ct, :, :, columns] = total.astype(bf16).reshape(2, T, -1)
            back.send_core(j, cx, ct)
            inner_columns = pl.ds(pl.multiple_of(cx * slot, 128), FC)
            for i in range(0, D, 512):
                columns = slice(i, i + 512)
                hidden = o_w[pl.ds(ct * (F // 2), F // 2), :, inner_columns].reshape(two, FC)
                total = dot(hidden, down[:, :, :, :, columns].reshape(FC, 512))
                out_parts[cx, ct, :, :, columns] = total.astype(bf16).reshape(2, T, -1)
            out.send_core(j, cx, ct)
            if j == 1:
                back.far(0, 1 - tb)
            if j == 2:
                back.far(1, tb)
        back.to_t(2, 0)
        inner = [o_w[:, :, i * slot : i * slot + FC].reshape(2 * two, FC) for i in (0, 1)]
        for i in range(0, D, 256):
            columns = slice(i, i + 256)
            total = contract_first(inner[0], cot[0, :, :, :, columns].reshape(2 * two, 256))
            total += contract_first(inner[1], cot[1, :, :, :, columns].reshape(2 * two, 256))
            down[:, :, :, :, columns] = total.astype(bf16).reshape(1, W, 2, -1, 256)
            if 2 * (i + 256) == D:
                ffn["down_low"] = PieceByL(
                    links, down.at[:, :, :, :, pl.ds(0, D // 2)], *bufs[0:2]
                )
        ffn["down_high"] = PieceByW(links, down.at[:, :, :, :, pl.ds(D // 2, D // 2)], *bufs[2:4])
        width = FQ * rows_w
        for i in range(TG):
            turned = normed[:, :, :, :, i * width : (i + 1) * width].reshape(4 * two, width)
            for grad, target in ((grad_gate, gate), (grad_up, up)):
                total = contract_first(turned, grad[...].reshape(4 * two, FC))
                target[i] = total.astype(bf16).reshape(W, 2, rows_w, FC)
            if i + 1 == TG // 2:
                low = pl.ds(0, TG // 2)
                ffn["gate_low"] = PieceByL(links, gate.at[low], *bufs[4:6])
                ffn["up_low"] = PieceByL(links, up.at[low], *bufs[6:8])
        high = pl.ds(TG // 2, TG // 2)
        ffn["gate_high"] = PieceByW(links, gate.at[high], *bufs[8:10])
        ffn["up_high"] = PieceByW(links, up.at[high], *bufs[10:12])

    feed_forward()

    cot_own, tok = normed.at[1, 0, 0], normed.at[1, 0, 1]
    own = Local(here, [(cot_in.at[x, tb, core], cot_own), (tok_in, tok)], 26)
    back.arrive(3, 1)
    own.wait()
    gain_sums[...] = jnp.zeros_like(gain_sums)

    def second_norm(rows):
        grad_normed = back.total(rows)
        grad, unit = norm_back(grad_normed, residual[rows], gains[1:2])
        grad = grad + cot_own[rows].astype(f32)
        grad_tokens[rows] = grad
        grad_row[s, rows] = grad.astype(bf16)
        gain_sums[1:2] += jnp.sum(grad_normed * unit, 0, keepdims=True)

    row_loop(T, 16, second_norm)
    row_x = links.pass_on(grad_row.at[s], (2, 0))
    row_c = links.pass_on(grad_row.at[s], (1, 0))

    normed_one = normed.at[0]
    spots = {}
    for name, width in (("attended", HC), ("q", HC), ("k", head), ("v", head), ("grad", HC)):
        base = sum(w for _, w in spots.values())
        spots[name] = (base, width)

    def column(name, first=0, width=None):
        base, full_width = spots[name]
        return pl.ds(base + first, width or full_width)

    def block(name, r, first=0, width=None):
        return cot[0, r // 2, r % 2, :, column(name, first, width)]

    def whole(name, first=0, width=None):
        return cot[0, :, :, :, column(name, first, width)].reshape(row_len, -1)

    def attention():
        loads = Local(
            here,
            [
                (o_in, o_w),
                (attended_in, cot.at[0, :, :, :, column("attended")]),
                (k_rot_in, cot.at[0, :, :, :, column("k")]),
                (v_in, cot.at[0, :, :, :, column("v")]),
                (tab_in, tab),
                (q_in, q_w),
                (kv_in, kv_w),
                (normed_one_in, normed_one),
            ]
            + [
                (q_rot_in.at[n], cot.at[0, :, :, :, column("q", n * head, head)])
                for n in range(heads)
            ],
            12,
        )
        out.far(0, 1 - tb)
        out.far(1, tb)
        row_x.wait()
        row_cc = links.pass_on(grad_row.at[s ^ 2], (1, 0))
        ffn["down_low"].middle()
        ffn["down_high"].middle()
        row_c.wait()
        row_cc.wait()
        loads.wait()
        full = rows_of(grad_row)
        wo = rows_of(o_w)
        for n in range(0, heads, 2):
            both = contract_last(full, wo[n * head : (n + 2) * head]).astype(bf16)
            cot[0, :, :, :, column("grad", n * head, 2 * head)] = both.reshape(2, 2, T, 2 * head)
        for i in range(0, D, HC):
            columns = slice(i, i + HC)
            total = contract_first(whole("attended"), full[:, columns])
            o_w[:, :, columns] = total.astype(bf16).reshape(F, rows_w, HC)
        o_view = o_w.reshape(1, FH, 2, rows_w, D)
        o_piece = PieceByL(links, o_view, *bufs[12:14])
        grad_k[...] = jnp.zeros_like(grad_k)
        grad_v[...] = jnp.zeros_like(grad_v)
        scale = head ** (-0.5)
        factors = rotation(rows_of(tab))
        back_turn = (factors[0], -factors[1])
        for r in range(row_len // T):
            rows, seen = slice(r * T, (r + 1) * T), slice(0, (r + 1) * T)
            keys, values = whole("k")[seen], whole("v")[seen]
            for n in range(heads):
                query, grad_att = block("q", r, n * head, head), block("grad", r, n * head, head)
                scores = contract_last(query, keys) * scale + bias[rows, seen].astype(f32)
                scores = jnp.exp(scores - jnp.max(scores, -1, keepdims=True))
                probs = scores / jnp.sum(scores, -1, keepdims=True)
                grad_probs = contract_last(grad_att, values)
                delta = jnp.sum(probs * grad_probs, -1, keepdims=True)
                grad_scores = (probs * (grad_probs - delta)).astype(bf16)
                grad_q = dot(grad_scores, keys) * scale
                grad_q = turn(grad_q, (back_turn[0][rows], back_turn[1][rows])).astype(bf16)
                cot[1, r // 2, r % 2, :, n * head : (n + 1) * head] = grad_q
                grad_k[seen] += contract_first(grad_scores, query)
                grad_v[seen] += contract_first(probs.astype(bf16), grad_att)
        grad_key = turn(grad_k[...] * scale, back_turn).astype(bf16)
        cot[1, :, :, :, HC : HC + head] = grad_key.reshape(2, 2, T, head)
        cot[1, :, :, :, HC + head : HC + 2 * head] = grad_v[...].astype(bf16).reshape(2, 2, T, head)
        grad_qkv = slice(0, HC + 2 * head)
        for arrival in back.sent:
            arrival.wait_sent()
        row = RowSum(links, back_parts.at[:, 0], back.from_core.at[:, 0], back.from_x.at[0])
        for cx, go in ((1 - x, row.far), (x, row.near)):
            for i in range(S):
                total = contract_last(
                    cot[1, cx, :, :, :HC].reshape(two, HC), q_w[i].reshape(-1, HC)
                )
                total += contract_last(
                    cot[1, cx, :, :, HC : HC + 2 * head].reshape(two, 2 * head),
                    kv_w[i, :, :, : 2 * head].reshape(-1, 2 * head),
                )
                columns = slice(i * F * rows_w, (i + 1) * F * rows_w)
                back_parts[cx, 0, :, :, columns] = total.astype(bf16).reshape(2, T, -1)
            go()
        row.middle()
        pieces = []
        q_view = q_w.reshape(S, FH, 2, rows_w, HC)
        kv_view = kv_w.reshape(S, FH, 2, rows_w, kv_w.shape[3])
        for i in range(S):
            columns = slice(i * F * rows_w, (i + 1) * F * rows_w)
            turned = normed[0, :, :, :, columns].reshape(row_len, -1)
            total = contract_first(turned, cot[1, :, :, :, grad_qkv].reshape(row_len, -1))
            total = total.astype(bf16)
            q_w[i] = total[:, :HC].reshape(F, rows_w, HC)
            kv_w[i, :, :, : 2 * head] = total[:, HC:].reshape(F, rows_w, 2 * head)
            pieces.append(
                PieceByL(
                    links, q_view.at[pl.ds(i, 1)], bufs[14].at[pl.ds(i, 1)], bufs[15].at[:, pl.ds(i, 1)]
                )
            )
        ffn["gate_low"].middle()
        ffn["up_low"].middle()
        ffn["gate_high"].middle()
        ffn["up_high"].middle()
        out.to_t(2, 0)
        o_piece.middle()
        row.arrive()

        def first_norm(rows):
            grad_normed = row.total(rows)
            grad, unit = norm_back(grad_normed, tok[rows].astype(f32), gains[0:1])
            grad_tokens[rows] += grad
            gain_sums[0:1] += jnp.sum(grad_normed * unit, 0, keepdims=True)

        row_loop(T, 16, first_norm)
        place = lax.broadcasted_iota(jnp.int32, (8, head), 0)
        lane = lax.broadcasted_iota(jnp.int32, (8, head), 1)
        pick = jnp.where((place == lane) & (place < 2), 1.0, 0.0)
        columns = contract_first(gain_sums[...], pick).astype(bf16)
        kv_w[:, :, :, 2 * head :] = columns.reshape(S, F, rows_w, head)
        kv_piece = PieceByL(links, kv_view, *bufs[16:18])
        for piece in pieces:
            piece.middle()
        for name in ("gate_low", "up_low", "gate_high", "up_high"):
            ffn[name].last()
        w, l = q // 2, q % 2
        for a, b in group_masks(FQ):
            to = 2 * (s ^ a) + (tb ^ (b // FQ))
            links.start(gate.at[to, w, l], gate_own.at[t], (a, b))
            links.start(up.at[to, w, l], up_own.at[t], (a, b))
        pairs = [(gate.at[t, w, l], gate_own.at[t]), (up.at[t, w, l], up_own.at[t])]
        mine = Local(here, pairs, 24)
        kv_piece.middle()

        def store_down(base):
            def store(i, rows, total):
                grad_down[rows, base : base + D // 2] = total

            return store

        ffn["down_low"].last(store_down(0))
        ffn["down_high"].last(store_down(D // 2))

        def store_o(i, rows, total):
            o_sum[rows] = total

        o_piece.last(store_o)
        out.arrive(3, 1)

        def finish_output(rows):
            output[rows] = (residual[rows] + out.total(rows)).astype(bf16)

        row_loop(T, 16, finish_output)
        h = f // 2
        for piece in pieces:
            piece.last()
        for a in (1, 2, 3):
            links.start(q_view.at[s ^ a, h, l], q_own.at[s], (a, 0))
        q_own[s] = q_view[s, h, l]
        kv_piece.last()
        for a in (1, 2, 3):
            links.start(kv_view.at[s ^ a, h, l], kv_own.at[s], (a, 0))
        kv_own[s] = kv_view[s, h, l]
        links.finish()
        mine.wait()

        def add_kv(rows):
            total = kv_own[0, rows].astype(f32)
            for i in range(1, S):
                total += kv_own[i, rows].astype(f32)
            kv_sum[rows] = total

        row_loop(kv_sum.shape[0], 16, add_kv)

    attention()


def angle_tables(position_row, head_size):
    half_head = head_size // 2
    frequency = 10000.0 ** (-jnp.arange(half_head, dtype=f32) * 2.0 / head_size)
    phase_angle = position_row.astype(f32)[:, None] * frequency[None, :]
    return (jnp.cos(phase_angle), jnp.sin(phase_angle))


def per_device(
    S,
    F,
    tokens,
    segments,
    positions,
    gain_one,
    w_query,
    w_key,
    w_value,
    w_out,
    gain_two,
    w_gate,
    w_up,
    w_down,
    cotangent,
):
    T, D = tokens.shape[1:]
    head = w_key.shape[1]
    row_len = segments.shape[1]
    rows = w_query.shape[0]
    down_rows = w_down.shape[0]
    FF = w_gate.shape[1]
    FH, FQ = F // 2, F // 2
    W = FQ // 2
    TG = 2 * S
    HC = w_query.shape[1] // S
    heads = HC // head
    FC = FF // TG

    def column_blocks(weight, n):
        return weight.reshape(rows, n, -1).transpose(1, 0, 2)

    gains = jnp.stack([gain_one, gain_two], 1)
    kvg = jnp.concatenate([w_key, w_value, gains, jnp.zeros((rows, head - 2), bf16)], 1)
    KV = kvg.shape[1]
    table = jnp.concatenate(angle_tables(positions[0], head), 1)
    segment = segments[0]
    index = jnp.arange(row_len)
    allowed = (index[None, :] <= index[:, None]) & (segment[None, :] == segment[:, None])
    bias = jnp.where(allowed, 0.0, -1e30).astype(bf16)
    outs = [
        (True, (S, F, rows, HC), bf16),
        (True, (S, F, rows, KV), bf16),
        (True, (F, rows, D), bf16),
        (False, (TG, FQ, rows, FC), bf16),
        (False, (TG, FQ, rows, FC), bf16),
        (False, (FQ, down_rows, D), bf16),
        (False, (2, 2, 2, T, D), bf16),
        (True, (S, T, head), f32),
        (True, (row_len, D), bf16),
        (True, (heads, row_len, head), bf16),
        (True, (row_len, head), bf16),
        (True, (row_len, head), bf16),
        (True, (row_len, HC), bf16),
        (True, (T, head), bf16),
        (True, (T, head), bf16),
        (True, (T, D), f32),
        (False, (2, 2, 2, T, D), bf16),
        (True, (8, D), f32),
    ]
    (wq, kvg, wo, gate_w, up_w, down_w, cot, table, normed_one, query_rot, key_rot, value_low, attended, keys, values, residual, normed_all, gains) = communicate(
        functools.partial(forward_kernel, FH, FQ),
        (
            tokens[0],
            table,
            column_blocks(w_query, S),
            kvg,
            w_out,
            column_blocks(w_gate, TG),
            column_blocks(w_up, TG),
            w_down,
            cotangent[0],
            bias,
        ),
        [shape(dims, kind) for _, dims, kind in outs],
        120 + 18 * F,
        0,
        in_vmem=[False] * 9 + [True],
        out_vmem=[inside for inside, _, _ in outs],
        kept=10,
        scratch=[
            pltpu.VMEM((S, T, D), bf16),
            pltpu.VMEM((2, 2, T, D), bf16),
            pltpu.VMEM((2, T, D), bf16),
            pltpu.VMEM((T, D), bf16),
            pltpu.VMEM((T, D), bf16),
            pltpu.VMEM((T, D), bf16),
        ],
    )
    group = [pltpu.VMEM((2, 2, 2, T, D), bf16), pltpu.VMEM((2, 2, T, D), bf16)]
    group += [pltpu.VMEM((2, T, D), bf16), pltpu.VMEM((T, D), bf16)]
    half = (1, W, down_rows, D // 2)
    block = (TG // 2, W, rows, FC)
    outs = [
        (True, (T, D), bf16),
        (True, (T, D), f32),
        (False, (TG, rows, FC), bf16),
        (False, (TG, rows, FC), bf16),
        (True, (down_rows, D), f32),
        (True, (S, rows, HC), bf16),
        (True, (rows, D), f32),
        (True, (rows, KV), f32),
    ]
    output, grad_tokens, gate_own, up_own, grad_w_down, q_own, grad_w_out, grad_kvg = communicate(
        functools.partial(backward_kernel, FH, FQ),
        (
            normed_all,
            cot,
            gate_w.reshape(TG, W, 2, rows, FC),
            up_w.reshape(TG, W, 2, rows, FC),
            down_w.reshape(1, W, 2, down_rows, D),
            wq,
            kvg,
            wo,
            normed_one.reshape(2, 2, T, D),
            query_rot.reshape(heads, 2, 2, T, head),
            key_rot.reshape(2, 2, T, head),
            value_low.reshape(2, 2, T, head),
            attended.reshape(2, 2, T, HC),
            table,
            tokens[0],
            bias,
            residual,
            gains,
        ),
        [shape(dims, kind) for _, dims, kind in outs],
        100 + 4 * F,
        1,
        in_vmem=[False] * 15 + [True] * 3,
        out_vmem=[inside for inside, _, _ in outs],
        kept=28,
        scratch=[
            pltpu.VMEM((TG, W, 2, rows, FC), bf16),
            pltpu.VMEM((TG, W, 2, rows, FC), bf16),
            pltpu.VMEM((1, W, 2, down_rows, D), bf16),
            pltpu.VMEM((S, F, rows, HC), bf16),
            pltpu.VMEM((S, F, rows, KV), bf16),
            pltpu.VMEM((F, rows, D), bf16),
            pltpu.VMEM((S, T, D), bf16),
            pltpu.VMEM((S, rows, KV), bf16),
            pltpu.VMEM((8, D), f32),
            *group,
            *group,
            pltpu.VMEM((2, 2, 2, T, D), bf16),
            pltpu.VMEM((2, 2, 2, T, D), bf16),
            pltpu.VMEM((2, 2, 2 * T, FC), bf16),
            pltpu.VMEM((2, 2, 2 * T, FC), bf16),
            pltpu.VMEM((S, T, head), f32),
            pltpu.VMEM((row_len, head), f32),
            pltpu.VMEM((row_len, head), f32),
            *by_l_scratch(*half),
            *by_w_scratch(*half),
            *by_l_scratch(*block),
            *by_l_scratch(*block),
            *by_w_scratch(*block),
            *by_w_scratch(*block),
            *by_l_scratch(1, FH, rows, D),
            *by_l_scratch(S, FH, rows, HC),
            *by_l_scratch(S, FH, rows, KV),
        ],
    )
    grad_w_gate = gate_own.transpose(1, 0, 2).reshape(rows, FF).astype(f32)
    grad_w_up = up_own.transpose(1, 0, 2).reshape(rows, FF).astype(f32)
    grad_w_query = q_own.transpose(1, 0, 2).reshape(rows, S * HC).astype(f32)
    return (
        output[None],
        keys[None],
        values[None],
        grad_tokens[None],
        grad_kvg[:, 2 * head],
        grad_w_query,
        grad_kvg[:, :head],
        grad_kvg[:, head : 2 * head],
        grad_w_out,
        grad_kvg[:, 2 * head + 1],
        grad_w_gate,
        grad_w_up,
        grad_w_down,
    )


def solution(mesh):
    token_spec = P("fsdp", "seq", None)
    flat, matrix = P(("seq", "fsdp")), P(("seq", "fsdp"), None)
    return jax.shard_map(
        functools.partial(per_device, mesh.shape["seq"], mesh.shape["fsdp"]),
        mesh=mesh,
        in_specs=(
            token_spec,
            P("fsdp", None),
            P("fsdp", "seq"),
            flat,
            matrix,
            matrix,
            matrix,
            matrix,
            flat,
            matrix,
            matrix,
            matrix,
            token_spec,
        ),
        out_specs=(
            token_spec,
            token_spec,
            token_spec,
            token_spec,
            flat,
            matrix,
            matrix,
            matrix,
            matrix,
            flat,
            matrix,
            matrix,
            matrix,
        ),
        check_vma=False,
    )
```

time: 644 us -> 468 us (0.73)
  the two profiles are of different devices: /device:TPU:13 before, /device:TPU:0 now
where the time goes in v3:
time: 468 us; the launch traced here: 461 us
  Pallas kernels  434 us (93%)
  local copies, waits for them, and re-layouts  21.4 us (5%)
  other arithmetic  4.79 us (1%)
    pallas_call x2, Pallas kernels, communicate(): pl.pallas_call(body, out_shape=outs, in_specs=specs(in_vmem, len(args)),...  434 us

profile of v3, /device:TPU:0, one launch (start us, length us, event | category | flops | bytes accessed | tf_op | source)
XLA Modules:
  0.0 461.0 jit_solution(17161387733093602875)
XLA Ops:
  0.6 0.0 copy-start.5
  0.7 0.0 copy-start.4
  0.7 0.8 convert_bitcast_fusion.3
  1.4 0.8 copy.29
  2.2 0.8 copy.30
  3.0 1.4 concatenate.7.refs_3_
  4.4 0.3 multiply_cosine_fusion
  4.7 0.7 pad_maximum_fusion.refs_1_
  5.4 1.7 copy.41
  7.1 1.7 select_convert_fusion.refs_9_.refs_15_
  8.9 0.0 copy-done.4
  8.9 0.7 reshape.82
  9.5 0.7 reshape.83
  10.2 1.5 copy_bitcast_fusion
  11.7 198.3 %shard_map.228 = (bf16[4,8,64,512]{3,2,1,0:T(8,128)(2,1)}, bf16[4,8,64,384]{3,2,1,0:T(8,128)(2,1)}, bf16[8,64,2048]{2,1,0:T(8,128)(2,1)}, bf16[8,4,64,704]{3,2,1...) custom-call(bf16[128,2048]{1,0:T(8,128)(2,1)} %bitcast.41, ...), custom_call_target="tpu_custom_call" | custom-call | tf_op jit(solution)/shard_map/pallas_call | solution.py:142
  210.0 235.5 %shard_map.229 = (bf16[128,2048]{1,0:T(8,128)(2,1)}, f32[128,2048]{1,0:T(8,128)}, bf16[8,64,704]{2,1,0:T(8,128)(2,1)}, bf16[8,64,704]{2,1,0:T(8,128)(2,1)}, f32[...) custom-call(bf16[2,2,2,128,2048]{4,3,2,1,0:T(8,128)(2,1)} %get-tuple-element.39.refs_0_, ...), custom_call_target="tpu_custom_call" | custom-call | tf_op jit(solution)/shard_map/pallas_call | solution.py:142
  445.5 1.6 slice_reduce_fusion
  447.1 1.4 fusion.1
  448.5 1.0 convert_bitcast_fusion.2
  449.5 0.8 copy.37
  450.3 0.1 convert_bitcast_fusion.1
  450.5 0.9 copy.34
  451.4 1.7 reshape.93
  453.1 0.1 convert_bitcast_fusion
  453.2 0.9 copy.35
  454.2 1.7 reshape.94
  455.8 0.8 copy.48
  456.6 0.6 copy.49
  457.3 0.6 copy.50
  457.9 1.0 copy.51
  458.9 0.8 copy.52
  459.7 1.1 copy.53
  (19 shorter events, 0.0 us)
Async XLA Ops:
  0.6 8.9 %copy-start.5 = (bf16[64,5632]{1,0:T(8,128)(2,1)S(1)}, bf16[64,5632]{1,0:T(8,128)(2,1)}, u32[]{:S(2)}) copy-start(bf16[64,5632]{1,0:T(8,128)(2,1)} %param.23) | copy-start | bytes 2162692
  0.7 8.2 %copy-start.4 = (bf16[64,5632]{1,0:T(8,128)(2,1)S(1)}, bf16[64,5632]{1,0:T(8,128)(2,1)}, u32[]{:S(2)}) copy-start(bf16[64,5632]{1,0:T(8,128)(2,1)} %param.22) | copy-start | bytes 2162692
  445.5 4.8 %copy-start.3 = (bf16[8,64,704]{2,1,0:T(8,128)(2,1)S(1)}, bf16[8,64,704]{2,1,0:T(8,128)(2,1)}, u32[]{:S(2)}) copy-start(bf16[8,64,704]{2,1,0:T(8,128)(2,1)} %get-tuple-element.62) | copy-start | bytes 2162692
  451.4 1.7 copy-start.2
  454.1 1.7 copy-start.7
  454.1 2.5 copy-start.9
  454.1 3.1 copy-start.8
  454.2 3.7 copy-start.1
  455.8 3.0 copy-start.6
  457.9 1.8 copy-start

commit v4 on v3

v4 whole, which is shorter than its diff:
```python
import functools

import jax
import jax.numpy as jnp
from jax import lax
from jax.experimental import pallas as pl
from jax.experimental.pallas import tpu as pltpu
from jax.sharding import PartitionSpec as P

epsilon = 1e-05
MESH = pl.DeviceIdType.MESH
VMEM_LIMIT = 64 * 2**20 - 2**18
bf16 = jnp.bfloat16
f32 = jnp.float32


def dot(left, right):
    return jnp.dot(left, right, preferred_element_type=f32)


def contract_last(left, right):
    return lax.dot_general(left, right, (((1,), (1,)), ((), ())), preferred_element_type=f32)


def contract_first(left, right):
    return lax.dot_general(left, right, (((0,), (0,)), ((), ())), preferred_element_type=f32)


class Arrival:
    def __init__(self, copy):
        self.copy, self.waited, self.left = copy, False, False

    def wait(self):
        if not self.waited:
            self.waited = True
            self.copy.wait_recv()

    def wait_sent(self):
        if not self.left:
            self.left = True
            self.copy.wait_send()


class Links:
    def __init__(self, send, recv):
        self.send, self.recv, self.sent, self.count = send, recv, [], 0
        self.s, self.f = lax.axis_index("seq"), lax.axis_index("fsdp")

    def greet(self, masks):
        barrier = pltpu.get_barrier_semaphore()
        for a, b in masks:
            pl.semaphore_signal(
                barrier, inc=1, device_id=(self.s ^ a, self.f ^ b), device_id_type=MESH
            )
        pl.semaphore_wait(barrier, len(masks))

    def copy(self, source, target, device):
        self.count += 1
        return pltpu.make_async_remote_copy(
            src_ref=source,
            dst_ref=target,
            send_sem=self.send.at[self.count - 1],
            recv_sem=self.recv.at[self.count - 1],
            device_id=device,
            device_id_type=MESH,
        )

    def start(self, source, target, mask):
        copy = self.copy(source, target, (self.s ^ mask[0], self.f ^ mask[1]))
        copy.start()
        self.sent.append(Arrival(copy))
        return self.sent[-1]

    def pass_on(self, block, mask):
        return self.start(block, block, mask)

    def finish(self):
        for arrival in self.sent:
            arrival.wait()
        for arrival in self.sent:
            arrival.wait_sent()


class Group:
    def __init__(self, links, own, full, FQ):
        self.links, self.full, self.FQ, self.own = links, full, FQ, own
        self.x, self.core, self.tb = links.s // 2, links.s % 2, links.f // FQ
        place = full.at[self.x, self.tb, self.core]
        self.there = links.start(own, place, (0, FQ))
        self.across = links.start(own, place, (2, 0))
        self.beside = links.start(own, place, (1, 0))

    def pass_core(self, x, tb):
        return self.links.pass_on(self.full.at[x, tb, self.core], (1, 0))

    def near(self):
        self.beside.wait()

    def other_x(self):
        self.across.wait()
        self.beside_x = self.pass_core(1 - self.x, self.tb)

    def other_t(self):
        self.there.wait()
        self.across_t = self.links.pass_on(self.full.at[self.x, 1 - self.tb, self.core], (2, 0))
        self.beside_t = self.pass_core(self.x, 1 - self.tb)

    def far(self):
        self.across_t.wait()
        self.beside_far = self.pass_core(1 - self.x, 1 - self.tb)

    def relay(self):
        self.other_x()
        self.other_t()
        self.far()


class Local:
    def __init__(self, sems, pairs, base=0):
        self.copies = [
            pltpu.make_async_copy(a, b, sems.at[base + i]) for i, (a, b) in enumerate(pairs)
        ]
        self.open = set(range(len(pairs)))
        for copy in self.copies:
            copy.start()

    def wait(self, *which):
        for i in which or sorted(self.open):
            self.open.discard(i)
            self.copies[i].wait()


def row_loop(rows, step, body):
    block_loop(1, rows, step, lambda i, part: body(part))


def block_loop(n, rows, step, body):
    if rows % step:
        for i in range(n):
            body(i, slice(0, rows))
        return
    steps = rows // step

    @pl.loop(0, n * steps)
    def _(k):
        body(k // steps, pl.ds(pl.multiple_of(lax.rem(k, steps) * step, step), step))


def communicate(
    body, args, outs, copies, collective_id, in_vmem=False, out_vmem=False, scratch=(), kept=1
):
    def specs(inside, n):
        inside = [inside] * n if isinstance(inside, bool) else inside
        return [pl.BlockSpec(memory_space=pltpu.VMEM if i else pl.ANY) for i in inside]

    return pl.pallas_call(
        body,
        out_shape=outs,
        in_specs=specs(in_vmem, len(args)),
        out_specs=specs(out_vmem, len(outs)),
        scratch_shapes=[
            pltpu.SemaphoreType.DMA((copies,)),
            pltpu.SemaphoreType.DMA((copies,)),
            pltpu.SemaphoreType.DMA((kept,)),
            *scratch,
        ],
        compiler_params=pltpu.CompilerParams(
            collective_id=collective_id, has_side_effects=True, vmem_limit_bytes=VMEM_LIMIT
        ),
    )(*args)


def shape(dims, kind=bf16):
    return jax.ShapeDtypeStruct(dims, kind)


def group_masks(FQ):
    return [(a, b) for a in range(4) for b in (0, FQ) if (a, b) != (0, 0)]


class Line:
    def __init__(self, links, views, FH):
        self.links, self.views, self.FH = links, views, FH
        self.h, self.l = links.f // 2, links.f % 2
        self.right, self.left, self.pending = [], [], []

    def here(self, h):
        return self.views(2 * h + self.l)

    def step(self, j):
        h, FH = self.h, self.FH
        rights = [
            self.links.copy(block, block, (self.links.s, self.links.f + 2))
            for block in self.here(lax.max(h - j, 0))
        ]
        lefts = [
            self.links.copy(block, block, (self.links.s, self.links.f - 2))
            for block in self.here(lax.min(h + j, FH - 1))
        ]
        for i in range(len(rights)):

            @pl.when((h >= j) & (h < FH - 1))
            def _():
                rights[i].start()

            @pl.when((h + j < FH) & (h > 0))
            def _():
                lefts[i].start()

        self.right.append(rights)
        self.left.append(lefts)

    def arrived(self, j):
        h, FH = self.h, self.FH
        up = self.here(lax.max(h - 1 - j, 0))
        down = self.here(lax.min(h + 1 + j, FH - 1))
        for i in range(len(up)):
            for blocks, copies, there in (
                (up, self.right[j], h - 1 - j >= 0),
                (down, self.left[j], h + 1 + j < FH),
            ):
                on = self.links.copy(
                    blocks[i], blocks[i], (self.links.s, self.links.f ^ 1)
                )
                self.pending.append((on, there))

                @pl.when(there)
                def _():
                    copies[i].wait_recv()
                    on.start()

    def finish(self):
        h, FH = self.h, self.FH
        for on, there in self.pending:

            @pl.when(there)
            def _():
                on.wait_recv()
                on.wait_send()

        for j in range(FH - 1):
            for i in range(len(self.right[j])):

                @pl.when((h >= j) & (h < FH - 1))
                def _():
                    self.right[j][i].wait_send()

                @pl.when((h + j < FH) & (h > 0))
                def _():
                    self.left[j][i].wait_send()


def rows_of(ref):
    return ref[...].reshape(-1, ref.shape[-1])


def rotation(table):
    half = table.shape[-1] // 2
    swapped = pltpu.roll(table, half, 1)
    first = lax.broadcasted_iota(jnp.int32, table.shape, 1) < half
    return jnp.where(first, table, swapped), jnp.where(first, -swapped, table)


def turn(vector, factors):
    return vector * factors[0] + pltpu.roll(vector, vector.shape[-1] // 2, 1) * factors[1]


class RowSum:
    def __init__(self, links, parts, from_core, from_x):
        self.links, self.parts, self.from_core, self.from_x = links, parts, from_core, from_x
        self.x, self.core, self.sent = links.s // 2, links.s % 2, []

    def far(self):
        x, core = 1 - self.x, 1 - self.core
        self.to_far = self.links.start(self.parts.at[x, core], self.from_core.at[x], (1, 0))
        self.sent.append(self.to_far)

    def near(self):
        x, core = self.x, 1 - self.core
        self.to_near = self.links.start(self.parts.at[x, core], self.from_core.at[x], (1, 0))
        self.sent.append(self.to_near)

    def middle(self):
        self.to_far.wait()
        x, core = 1 - self.x, self.core

        def add(rows):
            total = self.parts[x, core, rows].astype(f32) + self.from_core[x, rows].astype(f32)
            self.parts[x, core, rows] = total.astype(bf16)

        row_loop(self.from_x.shape[0], 16, add)
        self.across = self.links.start(self.parts.at[x, core], self.from_x, (2, 0))
        self.sent.append(self.across)

    def arrive(self):
        self.to_near.wait()
        self.across.wait()

    def total(self, rows):
        return (
            self.parts[self.x, self.core, rows].astype(f32)
            + self.from_core[self.x, rows].astype(f32)
            + self.from_x[rows].astype(f32)
        )


class GroupSum:
    def __init__(self, links, parts, from_core, from_x, from_t, FQ):
        self.links, self.parts, self.FQ = links, parts, FQ
        self.from_core, self.from_x, self.from_t = from_core, from_x, from_t
        self.x, self.core, self.tb = links.s // 2, links.s % 2, links.f // FQ
        self.T = from_t.shape[0]
        self.by_core, self.by_x, self.sent = {}, {}, []

    def send_core(self, name, x, tb):
        arrival = self.links.start(
            self.parts.at[x, tb, 1 - self.core], self.from_core.at[x, tb], (1, 0)
        )
        self.by_core[name] = arrival
        self.sent.append(arrival)

    def far(self, name, tb):
        self.by_core[name].wait()
        x, core = 1 - self.x, self.core

        def add(rows):
            total = self.parts[x, tb, core, rows].astype(f32)
            total += self.from_core[x, tb, rows].astype(f32)
            self.parts[x, tb, core, rows] = total.astype(bf16)

        row_loop(self.T, 16, add)
        arrival = self.links.start(self.parts.at[x, tb, core], self.from_x.at[tb], (2, 0))
        self.by_x[name] = arrival
        self.sent.append(arrival)

    def partial(self, tb, rows):
        return (
            self.parts[self.x, tb, self.core, rows].astype(f32)
            + self.from_core[self.x, tb, rows].astype(f32)
            + self.from_x[tb, rows].astype(f32)
        )

    def to_t(self, core_name, x_name):
        self.by_core[core_name].wait()
        self.by_x[x_name].wait()
        tb = 1 - self.tb

        def add(rows):
            self.parts[self.x, tb, self.core, rows] = self.partial(tb, rows).astype(bf16)

        row_loop(self.T, 16, add)
        self.there = self.links.start(
            self.parts.at[self.x, tb, self.core], self.from_t, (0, self.FQ)
        )
        self.sent.append(self.there)

    def arrive(self, core_name, x_name):
        self.by_core[core_name].wait()
        self.by_x[x_name].wait()
        self.there.wait()

    def total(self, rows):
        return self.partial(self.tb, rows) + self.from_t[rows].astype(f32)


class PieceByL:
    def __init__(self, links, parts, by_l, by_w):
        self.links, self.parts, self.by_l, self.by_w = links, parts, by_l, by_w
        self.n, self.W, _, self.rows = parts.shape[:4]
        self.l = links.f % 2
        self.w = (links.f // 2) % self.W
        self.first = links.start(parts.at[:, :, 1 - self.l], by_l, (0, 1))

    def middle(self):
        self.first.wait()
        l, self.second = self.l, []
        for k in range(1, self.W):
            w = self.w ^ k

            def add(i, rows, w=w):
                total = self.parts[i, w, l, rows].astype(f32) + self.by_l[i, w, rows].astype(f32)
                self.parts[i, w, l, rows] = total.astype(bf16)

            block_loop(self.n, self.rows, 16, add)
            self.second.append(
                self.links.start(self.parts.at[:, w, l], self.by_w.at[k - 1], (0, 2 * k))
            )

    def last(self, store=None):
        for arrival in self.second:
            arrival.wait()

        def add(i, rows):
            total = self.parts[i, self.w, self.l, rows].astype(f32)
            total += self.by_l[i, self.w, rows].astype(f32)
            for k in range(1, self.W):
                total += self.by_w[k - 1, i, rows].astype(f32)
            if store is None:
                self.parts[i, self.w, self.l, rows] = total.astype(bf16)
            else:
                store(i, rows, total)

        block_loop(self.n, self.rows, 16, add)


class PieceByW:
    def __init__(self, links, parts, by_l, by_w):
        self.links, self.parts, self.by_l, self.by_w = links, parts, by_l, by_w
        self.n, self.W, _, self.rows = parts.shape[:4]
        self.l = links.f % 2
        self.w = (links.f // 2) % self.W
        self.first = [
            links.start(parts.at[:, self.w ^ k], by_w.at[k - 1], (0, 2 * k))
            for k in range(1, self.W)
        ]

    def partial(self, i, l, rows):
        total = self.parts[i, self.w, l, rows].astype(f32)
        for k in range(1, self.W):
            total += self.by_w[k - 1, i, l, rows].astype(f32)
        return total

    def middle(self):
        for arrival in self.first:
            arrival.wait()
        l = 1 - self.l

        def add(i, rows):
            self.parts[i, self.w, l, rows] = self.partial(i, l, rows).astype(bf16)

        block_loop(self.n, self.rows, 16, add)
        self.second = self.links.start(self.parts.at[:, self.w, l], self.by_l, (0, 1))

    def last(self, store=None):
        self.second.wait()

        def add(i, rows):
            total = self.partial(i, self.l, rows) + self.by_l[i, rows].astype(f32)
            if store is None:
                self.parts[i, self.w, self.l, rows] = total.astype(bf16)
            else:
                store(i, rows, total)

        block_loop(self.n, self.rows, 16, add)


def low_part(n):
    return n * 5 // 8


def by_l_scratch(n, W, rows, width):
    return [pltpu.VMEM((n, W, rows, width), bf16), pltpu.VMEM((W - 1, n, rows, width), bf16)]


def by_w_scratch(n, W, rows, width):
    return [pltpu.VMEM((n, rows, width), bf16), pltpu.VMEM((W - 1, n, 2, rows, width), bf16)]


def norm_back(grad_normed, inputs, gain):
    inverse = lax.rsqrt(jnp.mean(inputs * inputs, -1, keepdims=True) + epsilon)
    scaled = grad_normed * gain
    inner_sum = jnp.sum(scaled * inputs, -1, keepdims=True)
    grad = inverse * scaled - inputs * (inverse**3 * inner_sum / inputs.shape[-1])
    return grad, inputs * inverse


def layer_kernel(FH, FQ, *refs):
    tok, tab_in, wq_in, kvg_in, wo_in, gate_in, up_in, down_in, cot_in, bias = refs[:10]
    output, keys, values, grad_tokens, gate_own, up_own, grad_down = refs[10:17]
    q_own, o_sum, kv_sum, normed_kept, side_kept, o_kept = refs[17:23]
    send, recv, here, gate, up, down, q_w, kv_w, o_w = refs[23:32]
    residual, gains, gain_sums, grad_row = refs[32:36]
    back_bufs, out_bufs = refs[36:40], refs[40:44]
    normed, cot, grad_gate, grad_up, tab, grad_k, grad_v = refs[44:51]
    bufs = refs[51:]
    links = Links(send, recv)
    s, f = links.s, links.f
    x, core = s // 2, s % 2
    tb, q = f // FQ, f % FQ
    w, l = q // 2, q % 2
    t = 2 * s + tb
    T, D = residual.shape
    S, F, rows_w, HC = q_w.shape
    row_len, head = grad_k.shape
    heads = HC // head
    TG, W, _, _, FC = gate.shape
    two = 2 * T
    cut, lead_cut = low_part(D), low_part(TG)
    scale = head ** (-0.5)
    evens_q = [2 * k for k in range(1, W)]
    back = GroupSum(links, *back_bufs, FQ)
    out = GroupSum(links, *out_bufs, FQ)
    back_parts, out_parts = back.parts, out.parts
    tok_g = grad_row
    spots = {}
    for name, width in (("attended", HC), ("q", HC), ("k", head), ("v", head), ("grad", HC)):
        base = sum(n for _, n in spots.values())
        spots[name] = (base, width)
    side_width = spots["grad"][0]

    def column(name, first=0, width=None):
        base, full_width = spots[name]
        return pl.ds(base + first, width or full_width)

    def block(where, name, r, first=0, width=None):
        return where[r // 2, r % 2, :, column(name, first, width)]

    def whole(where, name, first=0, width=None):
        return where[:, :, :, column(name, first, width)].reshape(row_len, -1)

    links.greet(
        [(a, 0) for a in (1, 2, 3)]
        + [(0, 1)]
        + [(0, 2 * k) for k in range(1, FH)]
        + [(a, FQ) for a in (1, 2, 3)]
    )
    local = Local(
        here,
        [
            (wq_in.at[s], q_w.at[s, f]),
            (kvg_in, kv_w.at[s, f]),
            (gate_in.at[t], gate.at[t, w, l]),
            (up_in.at[t], up.at[t, w, l]),
            (wo_in, o_w.at[f]),
            (tok, tok_g.at[s]),
            (tab_in, tab.at[s]),
            (down_in, down.at[0, w, l]),
            (cot_in, cot.at[x, tb, core]),
        ],
    )
    first = [links.start(wq_in.at[s ^ a], q_w.at[s, f], (a, 0)) for a in (1, 2, 3)]
    local.wait(1, 4)
    kv_line = Line(links, lambda place: [kv_w.at[s, place]], FH)
    o_line = Line(links, lambda place: [o_w.at[place]], FH)
    q_line = Line(links, lambda place: [q_w.at[:, place]], FH)
    kv_line.step(0)
    kv_y = links.pass_on(kv_w.at[s, f], (0, 1))
    o_line.step(0)
    needed = [links.pass_on(o_w.at[f], (0, 1))]
    local.wait(0)
    for arrival in first:
        arrival.wait()
    q_line.step(0)
    needed.append(links.pass_on(q_w.at[:, f], (0, 1)))
    tok_x = links.start(tok, tok_g.at[s], (2, 0))
    needed.append(links.start(tok, tok_g.at[s], (1, 0)))
    needed += [links.start(tab_in, tab.at[s], (a, 0)) for a in (1, 2, 3)]
    ffn_in = []

    def to_group(masks):
        for a, b in masks:
            to = 2 * (s ^ a) + (tb ^ (b // FQ))
            ffn_in.append(links.start(gate_in.at[to], gate.at[t, w, l], (a, b)))
            ffn_in.append(links.start(up_in.at[to], up.at[t, w, l], (a, b)))

    to_group([(a, 0) for a in (1, 2, 3)])
    for j in range(FH - 1):
        for way in (kv_line, o_line, q_line):
            way.arrived(j)
            if j + 1 < FH - 1:
                way.step(j + 1)
        if j == 0:
            tok_x.wait()
            needed.append(links.pass_on(tok_g.at[s ^ 2], (1, 0)))
    kv_y.wait()
    kv_line.finish()
    kv_x = links.pass_on(kv_w.at[s], (2, 0))
    needed.append(links.pass_on(kv_w.at[s], (1, 0)))
    same_tb = len(ffn_in)
    to_group([(a, FQ) for a in range(4)])
    down_y = links.start(down_in, down.at[0, w, l], (0, 1))
    down_z = [links.start(down_in, down.at[0, w, l], (0, b)) for b in evens_q]

    class Spread:
        def __init__(self, view, low):
            self.view, self.low, self.high = view, pl.ds(0, low), pl.ds(low, S - low)
            self.by_y = links.pass_on(view.at[:, w, l], (0, 1))
            self.by_z = [links.pass_on(view.at[:, w, l], (0, b)) for b in evens_q]

        def second(self):
            self.by_y.wait()
            hops = [links.pass_on(self.view.at[self.high, w, 1 - l], (0, b)) for b in evens_q]
            for arrival, b in zip(self.by_z, evens_q):
                arrival.wait()
                hops.append(links.pass_on(self.view.at[self.low, w ^ (b // 2), l], (0, 1)))
            return hops

    gate_by_tb = gate.reshape(S, 2, W, 2, rows_w, FC)
    up_by_tb = up.reshape(S, 2, W, 2, rows_w, FC)
    local.wait(2, 3)
    for arrival in ffn_in[:same_tb]:
        arrival.wait()
    spreads = [Spread(r.at[:, tb], 3) for r in (gate_by_tb, up_by_tb)]
    kv_x.wait()
    needed.append(links.pass_on(kv_w.at[s ^ 2], (1, 0)))
    for arrival in needed:
        arrival.wait()
    o_line.finish()
    q_line.finish()
    local.wait(5, 6)
    kept_o = Local(here, [(o_w, o_kept)], 9)

    normed_one, side = out_parts.at[0], out_parts.at[1]
    place = lax.broadcasted_iota(jnp.int32, (8, head), 0)
    lane = lax.broadcasted_iota(jnp.int32, (8, head), 1)
    pick = (place == lane).astype(bf16)
    kv_full = rows_of(kv_w)
    gains[...] = contract_last(pick, kv_full[:, 2 * head :])

    def norm_one(i, rows):
        value = tok_g[i, rows].astype(f32)
        inverse = lax.rsqrt(jnp.mean(value * value, -1, keepdims=True) + epsilon)
        normed_one[i // 2, lax.rem(i, 2), rows] = (value * inverse * gains[0:1]).astype(bf16)

    block_loop(S, T, 16, norm_one)
    factors = rotation(rows_of(tab))

    def put(name, first, value):
        columns = column(name, first, value.shape[1])
        side[:, :, :, columns] = value.astype(bf16).reshape(2, 2, T, -1)

    kv = dot(rows_of(normed_one), kv_full[:, : 2 * head])
    put("k", 0, turn(kv[:, :head], factors))
    put("v", 0, kv[:, head:])
    for n in range(0, heads, 2):
        columns = slice(n * head, (n + 2) * head)
        both = dot(rows_of(normed_one), q_w[:, :, :, columns].reshape(D, 2 * head))
        for j in (0, 1):
            put("q", (n + j) * head, turn(both[:, j * head : (j + 1) * head], factors))
    keys[...] = side[x, core, :, column("k")]
    values[...] = side[x, core, :, column("v")]
    for r in range(S):
        rows, seen = slice(r * T, (r + 1) * T), slice(0, (r + 1) * T)
        keys_seen, values_seen = whole(side, "k")[seen], whole(side, "v")[seen]
        for n in range(heads):
            query = block(side, "q", r, n * head, head)
            scores = contract_last(query, keys_seen) * scale + bias[rows, seen].astype(f32)
            scores = jnp.exp(scores - jnp.max(scores, -1, keepdims=True))
            probs = (scores / jnp.sum(scores, -1, keepdims=True)).astype(bf16)
            side[r // 2, r % 2, :, column("attended", n * head, head)] = dot(
                probs, values_seen
            ).astype(bf16)
    low_half, high_half = pl.ds(0, cut), pl.ds(cut, D - cut)
    arriving = []
    down_y.wait()
    for b in evens_q:
        arriving.append(links.pass_on(down.at[0, w, 1 - l, :, high_half], (0, b)))
    for arrival, b in zip(down_z, evens_q):
        arrival.wait()
        arriving.append(links.pass_on(down.at[0, w ^ (b // 2), l, :, low_half], (0, 1)))

    parts = RowSum(links, back_parts.at[:, 0], back.from_core.at[:, 0], back.from_x.at[0])

    def project(x_to):
        rows = side[x_to, :, :, column("attended")].reshape(two, HC)
        for n in range(0, D, HC):
            columns = slice(n, n + HC)
            total = dot(rows, o_w[:, :, columns].reshape(HC, HC))
            parts.parts[x_to, :, :, columns] = total.astype(bf16).reshape(2, T, HC)

    project(1 - x)
    parts.far()
    project(x)
    parts.near()
    parts.middle()
    for arrival in ffn_in[same_tb:]:
        arrival.wait()
    spreads += [Spread(r.at[:, 1 - tb], 2) for r in (gate_by_tb, up_by_tb)]
    cot_group = Group(links, cot_in, cot, FQ)
    for spread in spreads[:2]:
        arriving += spread.second()
    kept = Local(
        here, [(normed_one, normed_kept), (side.at[:, :, :, pl.ds(0, side_width)], side_kept)], 10
    )
    parts.arrive()

    def norm_two(rows):
        total = tok_g[s, rows].astype(f32) + parts.total(rows)
        residual[rows] = total
        inverse = lax.rsqrt(jnp.mean(total * total, -1, keepdims=True) + epsilon)
        normed[x, tb, core, rows] = (total * inverse * gains[1:2]).astype(bf16)

    row_loop(T, 16, norm_two)
    group_start = len(links.sent)
    group = Group(links, normed.at[x, tb, core], normed, FQ)
    for spread in spreads[2:]:
        arriving += spread.second()
    cot_group.other_x()
    cot_group.other_t()
    local.wait(7, 8)
    kept_o.wait()
    kept.wait()
    for arrival in arriving:
        arrival.wait()
    weights_sent = links.sent[:group_start]
    for arrival in weights_sent:
        arrival.wait_sent()

    slot = D // 2
    tiles = [slice(n, min(n + 256, FC)) for n in range(0, FC, 256)]

    def feed_forward(name, cx, ct):
        n = normed[cx, ct].reshape(two, D)
        c = cot[cx, ct].reshape(two, D)
        for tile in tiles:
            gate_proj = dot(n, gate[:, :, :, :, tile].reshape(D, -1))
            up_proj = dot(n, up[:, :, :, :, tile].reshape(D, -1))
            grad_inner = contract_last(c, down[...].reshape(FC, D)[tile])
            sig = jax.nn.sigmoid(gate_proj)
            silu = gate_proj * sig
            spot = pl.ds(pl.multiple_of(cx * slot + tile.start, 128), tile.stop - tile.start)
            hidden = (silu * up_proj).astype(bf16)
            o_w[pl.ds(ct * (F // 2), F // 2), :, spot] = hidden.reshape(F // 2, rows_w, -1)
            grad_up[cx, ct, :, tile] = (grad_inner * silu).astype(bf16)
            slope = sig * (1.0 + gate_proj * (1.0 - sig))
            grad_gate[cx, ct, :, tile] = (grad_inner * up_proj * slope).astype(bf16)
        for i in range(0, TG, 2):
            columns = slice(i * FQ * rows_w, (i + 2) * FQ * rows_w)
            total = contract_last(grad_gate[cx, ct], gate[i : i + 2].reshape(-1, FC))
            total += contract_last(grad_up[cx, ct], up[i : i + 2].reshape(-1, FC))
            back_parts[cx, ct, :, :, columns] = total.astype(bf16).reshape(2, T, -1)
        back.send_core(name, cx, ct)
        inner_columns = pl.ds(pl.multiple_of(cx * slot, 128), FC)
        hidden = o_w[pl.ds(ct * (F // 2), F // 2), :, inner_columns].reshape(two, FC)
        for i in range(0, D, 512):
            columns = slice(i, i + 512)
            total = dot(hidden, down[:, :, :, :, columns].reshape(FC, 512))
            out_parts[cx, ct, :, :, columns] = total.astype(bf16).reshape(2, T, -1)
        out.send_core(name, cx, ct)

    group.near()
    cot_group.near()
    feed_forward("near", x, tb)
    group.other_x()
    group.beside_x.wait()
    cot_group.beside_x.wait()
    feed_forward("x", 1 - x, tb)
    group.other_t()
    back.far("x", tb)
    group.beside_t.wait()
    cot_group.beside_t.wait()
    feed_forward("t", x, 1 - tb)
    group.far()
    cot_group.far()
    group.beside_far.wait()
    cot_group.beside_far.wait()
    feed_forward("far", 1 - x, 1 - tb)
    back.far("far", 1 - tb)
    out.far("x", tb)
    for arrival in links.sent[group_start:]:
        if arrival not in back.sent and arrival not in out.sent:
            arrival.wait_sent()
    ffn = {}
    inner = [o_w[:, :, i * slot : i * slot + FC].reshape(2 * two, FC) for i in (0, 1)]
    for i in range(0, D, 256):
        columns = slice(i, i + 256)
        total = contract_first(inner[0], cot[0, :, :, :, columns].reshape(2 * two, 256))
        total += contract_first(inner[1], cot[1, :, :, :, columns].reshape(2 * two, 256))
        down[:, :, :, :, columns] = total.astype(bf16).reshape(1, W, 2, -1, 256)
        if i + 256 == cut:
            ffn["down_low"] = PieceByL(links, down.at[:, :, :, :, pl.ds(0, cut)], *bufs[0:2])
    ffn["down_high"] = PieceByW(links, down.at[:, :, :, :, pl.ds(cut, D - cut)], *bufs[2:4])
    out.far("far", 1 - tb)
    width = FQ * rows_w
    for i in range(TG):
        turned = normed[:, :, :, :, i * width : (i + 1) * width].reshape(4 * two, width)
        for grad, target in ((grad_gate, gate), (grad_up, up)):
            total = contract_first(turned, grad[...].reshape(4 * two, FC))
            target[i] = total.astype(bf16).reshape(W, 2, rows_w, FC)
        if i + 1 == lead_cut:
            low = pl.ds(0, lead_cut)
            ffn["gate_low"] = PieceByL(links, gate.at[low], *bufs[4:6])
            ffn["up_low"] = PieceByL(links, up.at[low], *bufs[6:8])
            back.to_t("t", "far")
    high = pl.ds(lead_cut, TG - lead_cut)
    ffn["gate_high"] = PieceByW(links, gate.at[high], *bufs[8:10])
    ffn["up_high"] = PieceByW(links, up.at[high], *bufs[10:12])
    ffn["down_low"].middle()
    ffn["down_high"].middle()
    out.to_t("t", "far")

    cot_own, tok_own = normed.at[1, 0, 0], normed.at[1, 0, 1]
    own = Local(here, [(cot_in, cot_own), (tok, tok_own)], 12)
    gain_sums[...] = jnp.zeros_like(gain_sums)
    own.wait()
    back.arrive("near", "x")

    def second_norm(rows):
        grad_normed = back.total(rows)
        grad, unit = norm_back(grad_normed, residual[rows], gains[1:2])
        grad = grad + cot_own[rows].astype(f32)
        grad_tokens[rows] = grad
        grad_row[s, rows] = grad.astype(bf16)
        gain_sums[1:2] += jnp.sum(grad_normed * unit, 0, keepdims=True)

    row_loop(T, 16, second_norm)
    row_x = links.pass_on(grad_row.at[s], (2, 0))
    row_c = links.pass_on(grad_row.at[s], (1, 0))

    side = cot.at[0]
    normed_one = normed.at[0]
    loads = Local(
        here,
        [
            (o_kept, o_w),
            (side_kept, cot.at[0, :, :, :, pl.ds(0, side_width)]),
            (normed_kept, normed_one),
        ],
        14,
    )
    ffn["gate_low"].middle()
    row_x.wait()
    row_cc = links.pass_on(grad_row.at[s ^ 2], (1, 0))
    ffn["gate_high"].middle()
    ffn["up_high"].middle()
    row_c.wait()
    row_cc.wait()
    loads.wait()
    full = rows_of(grad_row)
    wo = rows_of(o_w)
    for n in range(0, heads, 2):
        both = contract_last(full, wo[n * head : (n + 2) * head]).astype(bf16)
        side[:, :, :, column("grad", n * head, 2 * head)] = both.reshape(2, 2, T, 2 * head)
    for i in range(0, D, HC):
        columns = slice(i, i + HC)
        total = contract_first(whole(side, "attended"), full[:, columns])
        o_w[:, :, columns] = total.astype(bf16).reshape(F, rows_w, HC)
    o_piece = PieceByL(links, o_w.reshape(1, FH, 2, rows_w, D), *bufs[12:14])
    grad_k[...] = jnp.zeros_like(grad_k)
    grad_v[...] = jnp.zeros_like(grad_v)
    factors = rotation(rows_of(tab))
    back_turn = (factors[0], -factors[1])
    for r in range(S):
        rows, seen = slice(r * T, (r + 1) * T), slice(0, (r + 1) * T)
        keys_seen, values_seen = whole(side, "k")[seen], whole(side, "v")[seen]
        for n in range(heads):
            query = block(side, "q", r, n * head, head)
            grad_att = block(side, "grad", r, n * head, head)
            scores = contract_last(query, keys_seen) * scale + bias[rows, seen].astype(f32)
            scores = jnp.exp(scores - jnp.max(scores, -1, keepdims=True))
            probs = scores / jnp.sum(scores, -1, keepdims=True)
            grad_probs = contract_last(grad_att, values_seen)
            delta = jnp.sum(probs * grad_probs, -1, keepdims=True)
            grad_scores = (probs * (grad_probs - delta)).astype(bf16)
            grad_q = dot(grad_scores, keys_seen) * scale
            grad_q = turn(grad_q, (back_turn[0][rows], back_turn[1][rows])).astype(bf16)
            cot[1, r // 2, r % 2, :, n * head : (n + 1) * head] = grad_q
            grad_k[seen] += contract_first(grad_scores, query)
            grad_v[seen] += contract_first(probs.astype(bf16), grad_att)
    grad_key = turn(grad_k[...] * scale, back_turn).astype(bf16)
    cot[1, :, :, :, HC : HC + head] = grad_key.reshape(2, 2, T, head)
    cot[1, :, :, :, HC + head : HC + 2 * head] = grad_v[...].astype(bf16).reshape(2, 2, T, head)
    grad_qkv = slice(0, HC + 2 * head)
    for arrival in back.sent:
        arrival.wait_sent()
    row = RowSum(links, back_parts.at[:, 0], back.from_core.at[:, 0], back.from_x.at[0])
    for cx, go in ((1 - x, row.far), (x, row.near)):
        for i in range(S):
            total = contract_last(cot[1, cx, :, :, :HC].reshape(two, HC), q_w[i].reshape(-1, HC))
            total += contract_last(
                cot[1, cx, :, :, HC : HC + 2 * head].reshape(two, 2 * head),
                kv_w[i, :, :, : 2 * head].reshape(-1, 2 * head),
            )
            columns = slice(i * F * rows_w, (i + 1) * F * rows_w)
            back_parts[cx, 0, :, :, columns] = total.astype(bf16).reshape(2, T, -1)
        go()
    row.middle()
    ffn["up_low"].middle()
    pieces = []
    q_view = q_w.reshape(S, FH, 2, rows_w, HC)
    kv_view = kv_w.reshape(S, FH, 2, rows_w, kv_w.shape[3])
    for i in range(S):
        columns = slice(i * F * rows_w, (i + 1) * F * rows_w)
        turned = normed[0, :, :, :, columns].reshape(row_len, -1)
        total = contract_first(turned, cot[1, :, :, :, grad_qkv].reshape(row_len, -1))
        total = total.astype(bf16)
        q_w[i] = total[:, :HC].reshape(F, rows_w, HC)
        kv_w[i, :, :, : 2 * head] = total[:, HC:].reshape(F, rows_w, 2 * head)
        one = pl.ds(i, 1)
        pieces.append(PieceByL(links, q_view.at[one], bufs[14].at[one], bufs[15].at[:, one]))
    def to_owners(target, own):
        for a, b in group_masks(FQ):
            to = 2 * (s ^ a) + (tb ^ (b // FQ))
            links.start(target.at[to, w, l], own.at[t], (a, b))

    ffn["gate_low"].last()
    ffn["gate_high"].last()
    to_owners(gate, gate_own)
    row.arrive()

    def first_norm(rows):
        grad_normed = row.total(rows)
        grad, unit = norm_back(grad_normed, tok_own[rows].astype(f32), gains[0:1])
        grad_tokens[rows] += grad
        gain_sums[0:1] += jnp.sum(grad_normed * unit, 0, keepdims=True)

    row_loop(T, 16, first_norm)
    pick = jnp.where((place == lane) & (place < 2), 1.0, 0.0)
    columns = contract_first(gain_sums[...], pick).astype(bf16)
    kv_w[:, :, :, 2 * head :] = columns.reshape(S, F, rows_w, head)
    kv_row = RowSum(links, kv_w.reshape(2, 2, F * rows_w, kv_w.shape[3]), *bufs[16:18])
    kv_row.far()
    kv_row.near()
    kv_row.middle()
    ffn["up_low"].last()
    ffn["up_high"].last()
    to_owners(up, up_own)
    mine = Local(here, [(gate.at[t, w, l], gate_own.at[t]), (up.at[t, w, l], up_own.at[t])], 17)
    o_piece.middle()
    pieces[0].middle()
    kv_row.arrive()

    def keep_kv(rows):
        kv_row.parts[x, core, rows] = kv_row.total(rows).astype(bf16)

    row_loop(F * rows_w, 16, keep_kv)
    kv_piece = PieceByL(links, kv_view.at[pl.ds(s, 1)], *bufs[18:20])
    for piece in pieces[1:]:
        piece.middle()
    kv_piece.middle()

    def store_down(base):
        def store(i, rows, total):
            grad_down[rows, base : base + total.shape[1]] = total

        return store

    ffn["down_low"].last(store_down(0))
    ffn["down_high"].last(store_down(cut))

    def store_o(i, rows, total):
        o_sum[rows] = total

    o_piece.last(store_o)
    out.arrive("near", "x")

    def finish_output(rows):
        output[rows] = (residual[rows] + out.total(rows)).astype(bf16)

    row_loop(T, 16, finish_output)
    h = f // 2
    for piece in pieces:
        piece.last()
    for a in (1, 2, 3):
        links.start(q_view.at[s ^ a, h, l], q_own.at[s], (a, 0))
    q_own[s] = q_view[s, h, l]

    def store_kv(i, rows, total):
        kv_sum[rows] = total

    kv_piece.last(store_kv)
    links.finish()
    mine.wait()


def angle_tables(position_row, head_size):
    half_head = head_size // 2
    frequency = 10000.0 ** (-jnp.arange(half_head, dtype=f32) * 2.0 / head_size)
    phase_angle = position_row.astype(f32)[:, None] * frequency[None, :]
    return (jnp.cos(phase_angle), jnp.sin(phase_angle))


def per_device(
    S,
    F,
    tokens,
    segments,
    positions,
    gain_one,
    w_query,
    w_key,
    w_value,
    w_out,
    gain_two,
    w_gate,
    w_up,
    w_down,
    cotangent,
):
    T, D = tokens.shape[1:]
    head = w_key.shape[1]
    row_len = segments.shape[1]
    rows = w_query.shape[0]
    down_rows = w_down.shape[0]
    FF = w_gate.shape[1]
    FH, FQ = F // 2, F // 2
    W = FQ // 2
    TG = 2 * S
    HC = w_query.shape[1] // S
    heads = HC // head
    FC = FF // TG

    def column_blocks(weight, n):
        return weight.reshape(rows, n, -1).transpose(1, 0, 2)

    gains = jnp.stack([gain_one, gain_two], 1)
    kvg = jnp.concatenate([w_key, w_value, gains, jnp.zeros((rows, head - 2), bf16)], 1)
    KV = kvg.shape[1]
    table = jnp.concatenate(angle_tables(positions[0], head), 1)
    segment = segments[0]
    index = jnp.arange(row_len)
    allowed = (index[None, :] <= index[:, None]) & (segment[None, :] == segment[:, None])
    bias = jnp.where(allowed, 0.0, -1e30).astype(bf16)
    group = [pltpu.VMEM((2, 2, 2, T, D), bf16), pltpu.VMEM((2, 2, T, D), bf16)]
    group += [pltpu.VMEM((2, T, D), bf16), pltpu.VMEM((T, D), bf16)]
    low, low_columns = low_part(TG), low_part(D)
    outs = [
        (True, (T, D), bf16),
        (True, (T, head), bf16),
        (True, (T, head), bf16),
        (True, (T, D), f32),
        (False, (TG, rows, FC), bf16),
        (False, (TG, rows, FC), bf16),
        (True, (down_rows, D), f32),
        (True, (S, rows, HC), bf16),
        (True, (rows, D), f32),
        (True, (rows, KV), f32),
        (False, (2, 2, T, D), bf16),
        (False, (2, 2, T, 2 * HC + 2 * head), bf16),
        (False, (F, rows, D), bf16),
    ]
    results = communicate(
        functools.partial(layer_kernel, FH, FQ),
        (
            tokens[0],
            table,
            column_blocks(w_query, S),
            kvg,
            w_out,
            column_blocks(w_gate, TG),
            column_blocks(w_up, TG),
            w_down,
            cotangent[0],
            bias,
        ),
        [shape(dims, kind) for _, dims, kind in outs],
        220 + 20 * F,
        0,
        in_vmem=[False] * 9 + [True],
        out_vmem=[inside for inside, _, _ in outs],
        kept=24,
        scratch=[
            pltpu.VMEM((TG, W, 2, rows, FC), bf16),
            pltpu.VMEM((TG, W, 2, rows, FC), bf16),
            pltpu.VMEM((1, W, 2, down_rows, D), bf16),
            pltpu.VMEM((S, F, rows, HC), bf16),
            pltpu.VMEM((S, F, rows, KV), bf16),
            pltpu.VMEM((F, rows, D), bf16),
            pltpu.VMEM((T, D), f32),
            pltpu.VMEM((8, D), f32),
            pltpu.VMEM((8, D), f32),
            pltpu.VMEM((S, T, D), bf16),
            *group,
            *group,
            pltpu.VMEM((2, 2, 2, T, D), bf16),
            pltpu.VMEM((2, 2, 2, T, D), bf16),
            pltpu.VMEM((2, 2, 2 * T, FC), bf16),
            pltpu.VMEM((2, 2, 2 * T, FC), bf16),
            pltpu.VMEM((S, T, head), f32),
            pltpu.VMEM((row_len, head), f32),
            pltpu.VMEM((row_len, head), f32),
            *by_l_scratch(1, W, down_rows, low_columns),
            *by_w_scratch(1, W, down_rows, D - low_columns),
            *by_l_scratch(low, W, rows, FC),
            *by_l_scratch(low, W, rows, FC),
            *by_w_scratch(TG - low, W, rows, FC),
            *by_w_scratch(TG - low, W, rows, FC),
            *by_l_scratch(1, FH, rows, D),
            *by_l_scratch(S, FH, rows, HC),
            pltpu.VMEM((2, F * rows, KV), bf16),
            pltpu.VMEM((F * rows, KV), bf16),
            *by_l_scratch(1, FH, rows, KV),
        ],
    )
    output, keys, values, grad_tokens, gate_own, up_own, grad_w_down, q_own, grad_w_out, grad_kvg = results[:10]
    grad_w_gate = gate_own.transpose(1, 0, 2).reshape(rows, FF).astype(f32)
    grad_w_up = up_own.transpose(1, 0, 2).reshape(rows, FF).astype(f32)
    grad_w_query = q_own.transpose(1, 0, 2).reshape(rows, S * HC).astype(f32)
    return (
        output[None],
        keys[None],
        values[None],
        grad_tokens[None],
        grad_kvg[:, 2 * head],
        grad_w_query,
        grad_kvg[:, :head],
        grad_kvg[:, head : 2 * head],
        grad_w_out,
        grad_kvg[:, 2 * head + 1],
        grad_w_gate,
        grad_w_up,
        grad_w_down,
    )


def solution(mesh):
    token_spec = P("fsdp", "seq", None)
    flat, matrix = P(("seq", "fsdp")), P(("seq", "fsdp"), None)
    return jax.shard_map(
        functools.partial(per_device, mesh.shape["seq"], mesh.shape["fsdp"]),
        mesh=mesh,
        in_specs=(
            token_spec,
            P("fsdp", None),
            P("fsdp", "seq"),
            flat,
            matrix,
            matrix,
            matrix,
            matrix,
            flat,
            matrix,
            matrix,
            matrix,
            token_spec,
        ),
        out_specs=(
            token_spec,
            token_spec,
            token_spec,
            token_spec,
            flat,
            matrix,
            matrix,
            matrix,
            matrix,
            flat,
            matrix,
            matrix,
            matrix,
        ),
        check_vma=False,
    )
```

time: 468 us -> 408 us (0.87)
  Pallas kernels: 434 us -> 373 us
    pallas_call x2 -> x1, Pallas kernels: 434 us -> 373 us  [communicate(): pl.pallas_call(body, out_shape=outs, in_specs=specs(in_vmem, len(args)),...]
where the time goes in v4:
time: 408 us; the launch traced here: 401 us
  Pallas kernels  373 us (91%)
  local copies, waits for them, and re-layouts  22 us (5%)
  other arithmetic  4.72 us (1%)
    pallas_call x1, Pallas kernels, communicate(): pl.pallas_call(body, out_shape=outs, in_specs=specs(in_vmem, len(args)),...  373 us

profile of v4, /device:TPU:0, one launch (start us, length us, event | category | flops | bytes accessed | tf_op | source)
XLA Modules:
  0.0 400.8 jit_solution(433655500164332528)
XLA Ops:
  0.7 0.7 convert_bitcast_fusion.3
  1.4 0.8 copy.29
  2.2 0.8 copy.30
  2.9 1.4 concatenate.7.refs_3_
  4.4 0.3 multiply_cosine_fusion
  4.7 0.7 pad_maximum_fusion.refs_1_
  5.4 1.7 copy.43
  7.1 1.7 select_convert_fusion.refs_9_
  8.8 0.7 reshape.58
  9.5 1.0 copy.42
  10.5 0.7 reshape.59
  11.2 1.0 copy.41
  12.2 373.1 %shard_map.228 = (bf16[128,2048]{1,0:T(8,128)(2,1)}, bf16[128,128]{1,0:T(8,128)(2,1)}, bf16[128,128]{1,0:T(8,128)(2,1)}, f32[128,2048]{1,0:T(8,128)}, bf16[8,64,...) custom-call(bf16[128,2048]{1,0:T(8,128)(2,1)} %bitcast.36, ...), custom_call_target="tpu_custom_call" | custom-call | tf_op jit(solution)/shard_map/pallas_call | solution.py:156
  385.3 0.0 copy-start.2
  385.4 0.0 copy-start.3
  385.4 1.6 slice_reduce_fusion
  387.0 1.4 fusion.1
  388.4 1.0 convert_bitcast_fusion.2
  389.4 0.8 copy.37
  390.2 0.2 convert_bitcast_fusion
  390.4 0.9 copy.35
  391.4 1.7 reshape.62
  393.0 0.9 copy.34
  394.0 1.7 reshape.61
  395.7 0.0 copy-done.7
  395.7 0.8 copy.50
  396.5 0.0 copy-done.9
  396.5 0.6 copy.51
  397.1 0.6 copy.52
  397.7 1.0 copy.53
  398.7 0.8 copy.54
  399.5 1.1 copy.55
  (18 shorter events, 0.0 us)
Async XLA Ops:
  0.6 8.2 %copy-start.4 = (bf16[64,5632]{1,0:T(8,128)(2,1)S(1)}, bf16[64,5632]{1,0:T(8,128)(2,1)}, u32[]{:S(2)}) copy-start(bf16[64,5632]{1,0:T(8,128)(2,1)} %param.22) | copy-start | bytes 2162692
  8.8 1.7 copy-start.5
  385.3 4.9 %copy-start.2 = (bf16[8,64,704]{2,1,0:T(8,128)(2,1)S(1)}, bf16[8,64,704]{2,1,0:T(8,128)(2,1)}, u32[]{:S(2)}) copy-start(bf16[8,64,704]{2,1,0:T(8,128)(2,1)} %get-tuple-element.30) | copy-start | bytes 2162692
  385.4 4.9 %copy-start.3 = (bf16[8,64,704]{2,1,0:T(8,128)(2,1)S(1)}, bf16[8,64,704]{2,1,0:T(8,128)(2,1)}, u32[]{:S(2)}) copy-start(bf16[8,64,704]{2,1,0:T(8,128)(2,1)} %get-tuple-element.31) | copy-start | bytes 2162692
  394.0 1.7 copy-start.7
  394.0 2.5 copy-start.9
  394.0 3.1 copy-start.8
  394.0 3.7 copy-start.1
  395.7 3.0 copy-start.6
  397.7 1.8 copy-start

commit v5 on v4

v5 whole, which is shorter than its diff:
```python
import functools

import jax
import jax.numpy as jnp
from jax import lax
from jax.experimental import pallas as pl
from jax.experimental.pallas import tpu as pltpu
from jax.sharding import PartitionSpec as P

epsilon = 1e-05
MESH = pl.DeviceIdType.MESH
Z = 4
VMEM_LIMIT = 64 * 2**20 - 2**18
bf16 = jnp.bfloat16
f32 = jnp.float32


def dot(left, right):
    return jnp.dot(left, right, preferred_element_type=f32)


def contract_last(left, right):
    return lax.dot_general(left, right, (((1,), (1,)), ((), ())), preferred_element_type=f32)


def contract_first(left, right):
    return lax.dot_general(left, right, (((0,), (0,)), ((), ())), preferred_element_type=f32)


class Arrival:
    def __init__(self, copy):
        self.copy, self.waited, self.left = copy, False, False

    def wait(self):
        if not self.waited:
            self.waited = True
            self.copy.wait_recv()

    def wait_sent(self):
        if not self.left:
            self.left = True
            self.copy.wait_send()


class Links:
    def __init__(self, send, recv):
        self.send, self.recv, self.sent, self.count = send, recv, [], 0
        self.s, self.f = lax.axis_index("seq"), lax.axis_index("fsdp")

    def greet(self, masks):
        barrier = pltpu.get_barrier_semaphore()
        for a, b in masks:
            pl.semaphore_signal(
                barrier, inc=1, device_id=(self.s ^ a, self.f ^ b), device_id_type=MESH
            )
        pl.semaphore_wait(barrier, len(masks))

    def copy(self, source, target, device):
        self.count += 1
        return pltpu.make_async_remote_copy(
            src_ref=source,
            dst_ref=target,
            send_sem=self.send.at[self.count - 1],
            recv_sem=self.recv.at[self.count - 1],
            device_id=device,
            device_id_type=MESH,
        )

    def start(self, source, target, mask):
        copy = self.copy(source, target, (self.s ^ mask[0], self.f ^ mask[1]))
        copy.start()
        self.sent.append(Arrival(copy))
        return self.sent[-1]

    def pass_on(self, block, mask):
        return self.start(block, block, mask)

    def finish(self):
        for arrival in self.sent:
            arrival.wait()
        for arrival in self.sent:
            arrival.wait_sent()


class Local:
    def __init__(self, sems, pairs, base=0):
        self.copies = [
            pltpu.make_async_copy(a, b, sems.at[base + i]) for i, (a, b) in enumerate(pairs)
        ]
        self.open = set(range(len(pairs)))
        for copy in self.copies:
            copy.start()

    def wait(self, *which):
        for i in which or sorted(self.open):
            self.open.discard(i)
            self.copies[i].wait()


def row_loop(rows, step, body):
    block_loop(1, rows, step, lambda i, part: body(part))


def block_loop(n, rows, step, body):
    if rows % step:
        for i in range(n):
            body(i, slice(0, rows))
        return
    steps = rows // step

    @pl.loop(0, n * steps)
    def _(k):
        body(k // steps, pl.ds(pl.multiple_of(lax.rem(k, steps) * step, step), step))


def communicate(
    body, args, outs, copies, collective_id, in_vmem=False, out_vmem=False, scratch=(), kept=1
):
    def specs(inside, n):
        inside = [inside] * n if isinstance(inside, bool) else inside
        return [pl.BlockSpec(memory_space=pltpu.VMEM if i else pl.ANY) for i in inside]

    return pl.pallas_call(
        body,
        out_shape=outs,
        in_specs=specs(in_vmem, len(args)),
        out_specs=specs(out_vmem, len(outs)),
        scratch_shapes=[
            pltpu.SemaphoreType.DMA((copies,)),
            pltpu.SemaphoreType.DMA((copies,)),
            pltpu.SemaphoreType.DMA((kept,)),
            *scratch,
        ],
        compiler_params=pltpu.CompilerParams(
            collective_id=collective_id, has_side_effects=True, vmem_limit_bytes=VMEM_LIMIT
        ),
    )(*args)


def shape(dims, kind=bf16):
    return jax.ShapeDtypeStruct(dims, kind)


class Line:
    def __init__(self, links, here, h, FH, forward):
        self.links, self.here, self.h, self.FH, self.forward = links, here, h, FH, forward
        self.right, self.left, self.pending = [], [], []
        self.settled = set()

    def step(self, j):
        h, FH = self.h, self.FH
        rights = [
            self.links.copy(block, block, (self.links.s, self.links.f + 2))
            for block in self.here(lax.max(h - j, 0))
        ]
        lefts = [
            self.links.copy(block, block, (self.links.s, self.links.f - 2))
            for block in self.here(lax.min(h + j, FH - 1))
        ]
        for i in range(len(rights)):

            @pl.when((h >= j) & (h < FH - 1))
            def _():
                rights[i].start()

            @pl.when((h + j < FH) & (h > 0))
            def _():
                lefts[i].start()

        self.right.append(rights)
        self.left.append(lefts)

    def arrived(self, j):
        h, FH = self.h, self.FH
        up = self.here(lax.max(h - 1 - j, 0))
        down = self.here(lax.min(h + 1 + j, FH - 1))
        for i in range(len(up)):
            for blocks, copies, there in (
                (up, self.right[j], h - 1 - j >= 0),
                (down, self.left[j], h + 1 + j < FH),
            ):
                a, b = self.forward
                on = self.links.copy(blocks[i], blocks[i], (self.links.s ^ a, self.links.f ^ b))
                self.pending.append((j, on, there))

                @pl.when(there)
                def _():
                    copies[i].wait_recv()
                    on.start()

    def came(self, j):
        self.settled.add(j)
        for step, on, there in self.pending:
            if step == j:

                @pl.when(there)
                def _():
                    on.wait_recv()

    def finish(self):
        h, FH = self.h, self.FH
        for j in range(FH - 1):
            if j not in self.settled:
                self.came(j)
        for _, on, there in self.pending:

            @pl.when(there)
            def _():
                on.wait_send()

        for j in range(FH - 1):
            for i in range(len(self.right[j])):

                @pl.when((h >= j) & (h < FH - 1))
                def _():
                    self.right[j][i].wait_send()

                @pl.when((h + j < FH) & (h > 0))
                def _():
                    self.left[j][i].wait_send()


def rows_of(ref):
    return ref[...].reshape(-1, ref.shape[-1])


def rotation(table):
    half = table.shape[-1] // 2
    swapped = pltpu.roll(table, half, 1)
    first = lax.broadcasted_iota(jnp.int32, table.shape, 1) < half
    return jnp.where(first, table, swapped), jnp.where(first, -swapped, table)


def turn(vector, factors):
    return vector * factors[0] + pltpu.roll(vector, vector.shape[-1] // 2, 1) * factors[1]


class RowSum:
    def __init__(self, links, parts, from_core, from_x):
        self.links, self.parts, self.from_core, self.from_x = links, parts, from_core, from_x
        self.x, self.core, self.sent = links.s // 2, links.s % 2, []

    def far(self):
        x, core = 1 - self.x, 1 - self.core
        self.to_far = self.links.start(self.parts.at[x, core], self.from_core.at[x], (1, 0))
        self.sent.append(self.to_far)

    def near(self):
        x, core = self.x, 1 - self.core
        self.to_near = self.links.start(self.parts.at[x, core], self.from_core.at[x], (1, 0))
        self.sent.append(self.to_near)

    def middle(self):
        self.to_far.wait()
        x, core = 1 - self.x, self.core

        def add(rows):
            total = self.parts[x, core, rows].astype(f32) + self.from_core[x, rows].astype(f32)
            self.parts[x, core, rows] = total.astype(bf16)

        row_loop(self.from_x.shape[0], 16, add)
        self.across = self.links.start(self.parts.at[x, core], self.from_x, (2, 0))
        self.sent.append(self.across)

    def arrive(self):
        self.to_near.wait()
        self.across.wait()

    def total(self, rows):
        return (
            self.parts[self.x, self.core, rows].astype(f32)
            + self.from_core[self.x, rows].astype(f32)
            + self.from_x[rows].astype(f32)
        )


class LineSum:
    def __init__(self, links, h, parts, from_core, chain, extra):
        self.links, self.h, self.parts = links, h, parts
        self.from_core, self.chain, self.extra = from_core, chain, extra
        self.core, self.T = links.s % 2, extra.shape[0]
        self.by_core, self.right, self.left, self.end = {}, {}, {}, {}
        s, f = links.s, links.f
        for d in range(Z):
            block = parts.at[d, self.core]
            self.right[d] = links.copy(block, chain.at[d], (s, f + 2))
            self.left[d] = links.copy(block, chain.at[d], (s, f - 2))
            self.end[d] = links.copy(block, extra, (s, f - 2))

    def send_core(self, d):
        self.by_core[d] = self.links.start(
            self.parts.at[d, 1 - self.core], self.from_core.at[d], (1, 0)
        )

    def add(self, d, chained):
        def add(rows):
            total = self.parts[d, self.core, rows].astype(f32)
            total += self.from_core[d, rows].astype(f32)
            if chained:
                total += self.chain[d, rows].astype(f32)
            self.parts[d, self.core, rows] = total.astype(bf16)

        row_loop(self.T, 16, add)

    def stage(self, k, places):
        h = self.h
        for d in places:
            self.by_core[d].wait()
            rightward, leftward = (h < d) & (h == k), (h > d) & (h == Z - 1 - k)

            @pl.when(rightward)
            def _():
                if k:
                    self.right[d].wait_recv()
                self.add(d, k > 0)
                self.right[d].start()

            @pl.when(leftward)
            def _():
                if k:
                    self.left[d].wait_recv()
                self.add(d, k > 0)

            @pl.when(leftward & (h > d + 1))
            def _():
                self.left[d].start()

            @pl.when(leftward & (h == d + 1))
            def _():
                self.end[d].start()

    def arrive(self):
        h = self.h
        for d in range(Z):
            self.by_core[d].wait()
            if d > 0:

                @pl.when(h == d)
                def _():
                    self.right[d].wait_recv()

            else:

                @pl.when(h == 0)
                def _():
                    self.chain[0] = jnp.zeros_like(self.chain[0])

            if d < Z - 1:

                @pl.when(h == d)
                def _():
                    self.end[d].wait_recv()

            else:

                @pl.when(h == Z - 1)
                def _():
                    self.extra[...] = jnp.zeros_like(self.extra)

    def total(self, rows):
        return (
            self.parts[self.h, self.core, rows].astype(f32)
            + self.from_core[self.h, rows].astype(f32)
            + self.chain[self.h, rows].astype(f32)
            + self.extra[rows].astype(f32)
        )

    def settle(self):
        h = self.h
        for d in range(Z):
            self.by_core[d].wait_sent()

            @pl.when(h < d)
            def _():
                self.right[d].wait_send()

            @pl.when(h > d + 1)
            def _():
                self.left[d].wait_send()

            @pl.when(h == d + 1)
            def _():
                self.end[d].wait_send()


class LeadFirst:
    def __init__(self, ref):
        self.ref, self.n, self.rows = ref, ref.shape[0], ref.shape[3]

    def half(self, l):
        return self.ref.at[:, :, l]

    def both(self, w):
        return self.ref.at[:, w]

    def part(self, w, l):
        return self.ref.at[:, w, l]

    def item(self, i, w, l):
        return self.ref.at[i, w, l]

    def got(self, ref, i, w):
        return ref.at[i, w]


class Natural:
    def __init__(self, ref):
        self.ref, self.n, self.rows = ref, ref.shape[2], ref.shape[4]

    def half(self, l):
        return self.ref.at[:, :, :, l]

    def both(self, w):
        return self.ref.at[w % 2, w // 2]

    def part(self, w, l):
        return self.ref.at[w % 2, w // 2, :, l]

    def item(self, i, w, l):
        return self.ref.at[w % 2, w // 2, i, l]

    def got(self, ref, i, w):
        return ref.at[w % 2, w // 2, i]


class PieceByL:
    def __init__(self, links, view, by_l, by_w, w, masks):
        self.links, self.view, self.by_l, self.by_w = links, view, by_l, by_w
        self.w, self.masks, self.l = w, masks, links.f % 2
        self.first = links.start(view.half(1 - self.l), by_l, (0, 1))

    def partial(self, i, w, rows):
        total = self.view.item(i, w, self.l)[rows].astype(f32)
        return total + self.view.got(self.by_l, i, w)[rows].astype(f32)

    def middle(self):
        self.first.wait()
        self.second = []
        for k in range(1, len(self.masks)):
            w = self.w ^ k

            def add(i, rows, w=w):
                self.view.item(i, w, self.l)[rows] = self.partial(i, w, rows).astype(bf16)

            block_loop(self.view.n, self.view.rows, 16, add)
            self.second.append(
                self.links.start(self.view.part(w, self.l), self.by_w.at[k - 1], self.masks[k])
            )

    def last(self, store=None):
        for arrival in self.second:
            arrival.wait()

        def add(i, rows):
            total = self.partial(i, self.w, rows)
            for k in range(1, len(self.masks)):
                total += self.by_w[k - 1, i, rows].astype(f32)
            if store is None:
                self.view.item(i, self.w, self.l)[rows] = total.astype(bf16)
            else:
                store(i, rows, total)

        block_loop(self.view.n, self.view.rows, 16, add)


class PieceByW:
    def __init__(self, links, view, by_l, by_w, w, masks):
        self.links, self.view, self.by_l, self.by_w = links, view, by_l, by_w
        self.w, self.masks, self.l = w, masks, links.f % 2
        self.first = [
            links.start(view.both(w ^ k), by_w.at[k - 1], masks[k]) for k in range(1, len(masks))
        ]

    def partial(self, i, l, rows):
        total = self.view.item(i, self.w, l)[rows].astype(f32)
        for k in range(1, len(self.masks)):
            total += self.by_w[k - 1, i, l, rows].astype(f32)
        return total

    def middle(self):
        for arrival in self.first:
            arrival.wait()
        l = 1 - self.l

        def add(i, rows):
            self.view.item(i, self.w, l)[rows] = self.partial(i, l, rows).astype(bf16)

        block_loop(self.view.n, self.view.rows, 16, add)
        self.second = self.links.start(self.view.part(self.w, l), self.by_l, (0, 1))

    def last(self, store=None):
        self.second.wait()

        def add(i, rows):
            total = self.partial(i, self.l, rows) + self.by_l[i, rows].astype(f32)
            if store is None:
                self.view.item(i, self.w, self.l)[rows] = total.astype(bf16)
            else:
                store(i, rows, total)

        block_loop(self.view.n, self.view.rows, 16, add)


def by_l_scratch(n, W, rows, width):
    return [pltpu.VMEM((n, W, rows, width), bf16), pltpu.VMEM((W - 1, n, rows, width), bf16)]


def by_w_scratch(n, W, rows, width):
    return [pltpu.VMEM((n, rows, width), bf16), pltpu.VMEM((W - 1, n, 2, rows, width), bf16)]


def norm_back(grad_normed, inputs, gain):
    inverse = lax.rsqrt(jnp.mean(inputs * inputs, -1, keepdims=True) + epsilon)
    scaled = grad_normed * gain
    inner_sum = jnp.sum(scaled * inputs, -1, keepdims=True)
    grad = inverse * scaled - inputs * (inverse**3 * inner_sum / inputs.shape[-1])
    return grad, inputs * inverse


def layer_kernel(FH, *refs):
    tok, tab_in, wq_in, wk_in, wv_in, gains_in, wo_in = refs[:7]
    gate_in, up_in, down_in, cot_in, bias = refs[7:12]
    output, keys, values, grad_tokens, gate_out, up_out, down_out = refs[12:19]
    wq_out, wo_out, wk_out, wv_out, gains_out = refs[19:24]
    both_own, normed_kept, side_kept, o_kept = refs[24:28]
    send, recv, here, both, down, q_w, kv_w, o_w = refs[28:36]
    residual, grad_in, gains, gain_sums, grad_row = refs[36:41]
    grad_down, o_sum, kv_sum, q_own = refs[41:45]
    back_bufs, out_bufs = refs[45:49], refs[49:53]
    normed, cot, grad_both, tab, grad_k, grad_v = refs[53:59]
    bufs = refs[59:]
    links = Links(send, recv)
    s, f = links.s, links.f
    x, core = s // 2, s % 2
    e, h, l = f // 8, (f // 2) % Z, f % 2
    t = 2 * h + core
    T, D = residual.shape
    S, F, rows_w, HC = q_w.shape
    row_len, head = grad_k.shape
    heads = HC // head
    E, FC = both.shape[2], both.shape[6] // 2
    W, TG = 2 * E, 2 * Z
    w = 2 * e + x
    two = 2 * T
    cut = D // 4 * 3
    scale = head ** (-0.5)
    group_masks = [(a, 2 * m) for m in range(Z) for a in (0, 1)][1:]
    w_masks = [(2 * (j % 2), 8 * (j // 2)) for j in range(W)]
    back = LineSum(links, h, *back_bufs)
    out = LineSum(links, h, *out_bufs)
    back_parts, out_parts = back.parts, out.parts
    tok_g = grad_row
    spots = {}
    for name, width in (("attended", HC), ("q", HC), ("k", head), ("v", head), ("grad", HC)):
        base = sum(n for _, n in spots.values())
        spots[name] = (base, width)
    side_width = spots["grad"][0]

    def column(name, first=0, width=None):
        base, full_width = spots[name]
        return pl.ds(base + first, width or full_width)

    def block(where, name, r, first=0, width=None):
        return where[r // 2, r % 2, :, column(name, first, width)]

    def to_x(ref, j):
        return ref.at[(w ^ j) % 2, :, (w ^ j) // 2]

    def whole(where, name, first=0, width=None):
        return where[:, :, :, column(name, first, width)].reshape(row_len, -1)

    links.greet(
        [(a, 0) for a in (1, 2, 3)]
        + [(0, 1)]
        + [(0, 2 * k) for k in range(1, FH)]
        + [(1, 2 * m) for m in range(1, Z)]
        + [mask for mask in w_masks if mask[0] and mask[1]]
    )
    local = Local(
        here,
        [
            (wq_in.at[:, pl.ds(pl.multiple_of(s * HC, HC), HC)], q_w.at[s, f]),
            (wk_in, kv_w.at[s, f, :, pl.ds(0, head)]),
            (wv_in, kv_w.at[s, f, :, pl.ds(head, head)]),
            (gains_in, kv_w.at[s, f, :, pl.ds(2 * head, head)]),
            (wo_in, o_w.at[f]),
            (tok, tok_g.at[s]),
            (tab_in, tab.at[s]),
            (down_in, down.at[0, w, l]),
            (cot_in, cot.at[h, core]),
        ],
    )
    first = [
        links.start(
            wq_in.at[:, pl.ds(pl.multiple_of((s ^ a) * HC, HC), HC)], q_w.at[s, f], (a, 0)
        )
        for a in (1, 2, 3)
    ]
    quarter = FC * TG // S
    natural = Local(
        here,
        [
            (r.at[:, pl.ds(i * quarter, quarter)], back_parts.at[i, j, pl.ds(0, rows_w), pl.ds(0, quarter)])
            for j, r in enumerate((gate_in, up_in))
            for i in range(S)
        ],
        9,
    )
    local.wait(1, 2, 3, 4)
    along_z = (f // 2, FH, (0, 1))
    kv_line = Line(links, lambda place: [kv_w.at[s, 2 * place + l]], *along_z)
    o_line = Line(links, lambda place: [o_w.at[2 * place + l]], *along_z)
    q_line = Line(links, lambda place: [q_w.at[:, 2 * place + l]], *along_z)
    kv_line.step(0)
    kv_y = links.pass_on(kv_w.at[s, f], (0, 1))
    o_line.step(0)
    needed = [links.pass_on(o_w.at[f], (0, 1))]
    local.wait(0)
    for arrival in first:
        arrival.wait()
    q_line.step(0)
    needed.append(links.pass_on(q_w.at[:, f], (0, 1)))
    tok_x = links.start(tok, tok_g.at[s], (2, 0))
    needed.append(links.start(tok, tok_g.at[s], (1, 0)))
    needed += [links.start(tab_in, tab.at[s], (a, 0)) for a in (1, 2, 3)]
    ffn_in = {}
    lanes = 128
    whole_tiles = FC // lanes

    def blocks_of(ref, at_h, c):
        width = 2 * FC // W // 2
        parts = []
        for at_e in range(E):
            for at_x in (0, 1):
                base = (at_e * Z + at_h) * width
                parts.append(ref(2 * at_x + c)[:, base : base + width])
        return jnp.concatenate(parts, 1)

    def side_by_side(gate_units, up_units):
        tiles = []
        for j in range(whole_tiles):
            part = slice(j * lanes, (j + 1) * lanes)
            tiles += [gate_units[:, part], up_units[:, part]]
        rest = slice(whole_tiles * lanes, FC)
        return jnp.concatenate(tiles + [gate_units[:, rest], up_units[:, rest]], 1)

    def sent_blocks(at_h, c):
        return grad_both.at[at_h, pl.ds(pl.multiple_of(c * rows_w, rows_w), rows_w)]

    natural.wait()
    columns_of = [
        [back_parts[i, j, :rows_w, :quarter].astype(f32) for i in range(S)] for j in (0, 1)
    ]
    for at_h in range(Z):
        for c in (0, 1):
            units = [blocks_of(lambda i: columns_of[j][i], at_h, c) for j in (0, 1)]
            grad_both[at_h, c * rows_w : (c + 1) * rows_w] = side_by_side(*units).astype(bf16)
    own_block = Local(here, [(sent_blocks(h, core), both.at[x, core, e, h, l])], 17)

    def to_group(m):
        for a in (0, 1):
            if (a, m) != (0, 0):
                place = (x, core, e, h, l)
                source = sent_blocks(h ^ m, core ^ a)
                ffn_in[a, m] = links.start(source, both.at[place], (a, 2 * m))

    arriving = []

    class Spread:
        def __init__(self, near, second_w, second_y):
            self.near, self.second_w, self.second_y = near, second_w, second_y

        def by_w(self):
            self.came_w = [links.pass_on(self.near, mask) for mask in w_masks[1:]]

        def by_y(self):
            self.came_y = links.pass_on(self.near, (0, 1))

        def on_w(self):
            self.came_y.wait()
            arriving.extend(links.pass_on(self.second_w, mask) for mask in w_masks[1:])

        def on_y(self):
            for j, arrival in enumerate(self.came_w):
                arrival.wait()
                arriving.append(links.pass_on(self.second_y(j + 1), (0, 1)))

    def spread_of(m):
        def second_y(j):
            return to_x(both, j).at[0, h ^ m, l]

        here_q = to_x(both, 0)
        return Spread(here_q.at[:, h ^ m, l], here_q.at[1, h ^ m, 1 - l], second_y)

    low_half, high_half = pl.ds(0, cut), pl.ds(cut, D - cut)
    spread_down = Spread(
        down.at[0, w, l],
        down.at[0, w, 1 - l, :, high_half],
        lambda j: down.at[0, w ^ j, l, :, low_half],
    )
    to_group(0)
    local.wait(7)
    spread_down.by_w()
    for j in range(FH - 1):
        for way in (kv_line, o_line, q_line):
            way.arrived(j)
            if j + 1 < FH - 1:
                way.step(j + 1)
        if j == 0:
            tok_x.wait()
            needed.append(links.pass_on(tok_g.at[s ^ 2], (1, 0)))
            own_block.wait()
            ffn_in[1, 0].wait()
            spreads = [spread_of(m) for m in range(Z)]
            spreads[0].by_w()
    kv_y.wait()
    kv_line.finish()
    kv_x = links.pass_on(kv_w.at[s], (2, 0))
    needed.append(links.pass_on(kv_w.at[s], (1, 0)))
    for m in range(1, Z):
        to_group(m)
    spread_down.by_y()
    spreads[0].by_y()
    cot_line = Line(links, lambda place: [cot.at[place, core]], h, Z, (1, 0))
    kv_x.wait()
    needed.append(links.pass_on(kv_w.at[s ^ 2], (1, 0)))
    for arrival in needed:
        arrival.wait()
    o_line.finish()
    q_line.finish()
    local.wait(5, 6)
    kept_o = Local(here, [(o_w, o_kept)], 18)

    normed_one, side = out_parts.at[pl.ds(0, 2)], out_parts.at[pl.ds(2, 2)]
    place = lax.broadcasted_iota(jnp.int32, (8, head), 0)
    lane = lax.broadcasted_iota(jnp.int32, (8, head), 1)
    pick = (place == lane).astype(bf16)
    kv_full = rows_of(kv_w)
    gains[...] = contract_last(pick, kv_full[:, 2 * head :])

    def norm_one(i, rows):
        value = tok_g[i, rows].astype(f32)
        inverse = lax.rsqrt(jnp.mean(value * value, -1, keepdims=True) + epsilon)
        normed_one[i // 2, lax.rem(i, 2), rows] = (value * inverse * gains[0:1]).astype(bf16)

    block_loop(S, T, 16, norm_one)
    local.wait(8)
    cot_line.step(0)
    arriving.append(links.pass_on(cot.at[h, core], (1, 0)))
    factors = rotation(rows_of(tab))

    def put(name, first, value):
        columns = column(name, first, value.shape[1])
        side[:, :, :, columns] = value.astype(bf16).reshape(2, 2, T, -1)

    kv = dot(rows_of(normed_one), kv_full[:, : 2 * head])
    put("k", 0, turn(kv[:, :head], factors))
    put("v", 0, kv[:, head:])
    for n in range(0, heads, 2):
        columns = slice(n * head, (n + 2) * head)
        pair = dot(rows_of(normed_one), q_w[:, :, :, columns].reshape(D, 2 * head))
        for j in (0, 1):
            put("q", (n + j) * head, turn(pair[:, j * head : (j + 1) * head], factors))
    results = [
        Local(
            here,
            [
                (side.at[x, core, :, column("k")], keys),
                (side.at[x, core, :, column("v")], values),
            ],
            21,
        )
    ]
    for r in range(S):
        rows, seen = slice(r * T, (r + 1) * T), slice(0, (r + 1) * T)
        keys_seen, values_seen = whole(side, "k")[seen], whole(side, "v")[seen]
        for n in range(heads):
            query = block(side, "q", r, n * head, head)
            scores = contract_last(query, keys_seen) * scale + bias[rows, seen].astype(f32)
            scores = jnp.exp(scores - jnp.max(scores, -1, keepdims=True))
            probs = (scores / jnp.sum(scores, -1, keepdims=True)).astype(bf16)
            side[r // 2, r % 2, :, column("attended", n * head, head)] = dot(
                probs, values_seen
            ).astype(bf16)
    spread_down.on_y()
    spread_down.on_w()

    first_two = pl.ds(0, 2)
    row_bufs = (back_parts.at[first_two], back.from_core.at[first_two], back.chain.at[0])
    parts = RowSum(links, *row_bufs)

    def project(x_to):
        rows = side[x_to, :, :, column("attended")].reshape(two, HC)
        for n in range(0, D, HC):
            columns = slice(n, n + HC)
            total = dot(rows, o_w[:, :, columns].reshape(HC, HC))
            parts.parts[x_to, :, :, columns] = total.astype(bf16).reshape(2, T, HC)

    project(1 - x)
    parts.far()
    project(x)
    parts.near()
    parts.middle()
    spreads[0].on_y()
    spreads[0].on_w()
    for m in range(1, Z):
        for a in (0, 1):
            ffn_in[a, m].wait()
        spreads[m].by_y()
        spreads[m].by_w()
    cot_line.arrived(0)
    cot_line.step(1)
    kept = Local(
        here, [(normed_one, normed_kept), (side.at[:, :, :, pl.ds(0, side_width)], side_kept)], 19
    )
    parts.arrive()

    def norm_two(rows):
        total = tok_g[s, rows].astype(f32) + parts.total(rows)
        residual[rows] = total
        inverse = lax.rsqrt(jnp.mean(total * total, -1, keepdims=True) + epsilon)
        normed[h, core, rows] = (total * inverse * gains[1:2]).astype(bf16)

    row_loop(T, 16, norm_two)
    normed_line = Line(links, lambda place: [normed.at[place, core]], h, Z, (1, 0))
    normed_line.step(0)
    beside = [links.pass_on(normed.at[h, core], (1, 0))]
    cot_line.arrived(1)
    cot_line.step(2)
    for m in range(1, Z):
        spreads[m].on_y()
        spreads[m].on_w()
        if m < Z - 1:
            normed_line.arrived(m - 1)
            normed_line.step(m)
    results[0].wait()
    kept_o.wait()
    kept.wait()
    for arrival in arriving:
        arrival.wait()
    for arrival in links.sent:
        arrival.wait_sent()

    slot = D // 2
    lane_is_low = lax.broadcasted_iota(jnp.int32, (two, lanes), 1) < lanes // 2

    def hidden_of(d):
        n = normed[d].reshape(two, D)
        c = cot[d].reshape(two, D)
        weights = down[...].reshape(FC, D)

        def units(first, width, gate_proj, up_proj, grad_inner):
            sig = jax.nn.sigmoid(gate_proj)
            silu = gate_proj * sig
            spot = pl.ds(pl.multiple_of(d // 2 * slot + first, lanes), width)
            hidden = (silu * up_proj).astype(bf16)[:, :width]
            o_w[pl.ds(d % 2 * (F // 2), F // 2), :, spot] = hidden.reshape(F // 2, rows_w, width)
            slope = sig * (1.0 + gate_proj * (1.0 - sig))
            return (grad_inner * up_proj * slope).astype(bf16), (grad_inner * silu).astype(bf16)

        for first in range(0, FC, 2 * lanes):
            width = min(2 * lanes, FC - first)
            rows = weights[first : first + width]
            if width % lanes:
                rows = jnp.concatenate([rows, rows[width - lanes // 2 :]], 0)
            grad_inner = contract_last(c, rows)
            for i in range(0, width, lanes):
                base = 2 * (first + i)
                columns = (slice(None),) * 6 + (slice(base, min(base + 2 * lanes, 2 * FC)),)
                proj = dot(n, both[columns].reshape(D, -1))
                part = slice(i, i + lanes)
                if i + lanes <= width:
                    grad_gate, grad_up = units(
                        first + i,
                        lanes,
                        proj[:, :lanes],
                        proj[:, lanes:],
                        grad_inner[:, part],
                    )
                    grad_both[d, :, base : base + lanes] = grad_gate
                    grad_both[d, :, base + lanes : base + 2 * lanes] = grad_up
                else:
                    mixed = proj
                    turned = pltpu.roll(mixed, lanes // 2, 1)
                    grad_gate, grad_up = units(
                        first + i,
                        lanes // 2,
                        jnp.where(lane_is_low, mixed, turned),
                        jnp.where(lane_is_low, turned, mixed),
                        grad_inner[:, part],
                    )
                    grad_both[d, :, base : base + lanes] = jnp.where(
                        lane_is_low, grad_gate, grad_up
                    )

    def back_of(d):
        for i in range(S):
            columns = slice(i * F * rows_w, (i + 1) * F * rows_w)
            total = contract_last(grad_both[d], both[i // 2, i % 2].reshape(-1, 2 * FC))
            back_parts[d, :, :, columns] = total.astype(bf16).reshape(2, T, -1)
        back.send_core(d)

    def out_of(d):
        spot = slice(d // 2 * slot, d // 2 * slot + FC)
        hidden = o_w[pl.ds(d % 2 * (F // 2), F // 2), :, spot].reshape(two, FC)
        for i in range(0, D, 512):
            columns = slice(i, i + 512)
            total = dot(hidden, down[:, :, :, :, columns].reshape(FC, 512))
            out_parts[d, :, :, columns] = total.astype(bf16).reshape(2, T, -1)
        out.send_core(d)

    for arrival in beside:
        arrival.wait()
    hidden_of(h)
    for line in (cot_line, normed_line):
        line.came(0)
    hidden_of(h ^ 1)
    for line in (cot_line, normed_line):
        line.came(1)
    hidden_of(h ^ 2)
    for line in (cot_line, normed_line):
        line.arrived(2)
    for line in (cot_line, normed_line):
        line.came(2)
    hidden_of(h ^ 3)
    back_of(3)
    back_of(0)
    back.stage(0, (3, 0))
    back_of(2)
    back_of(1)
    back.stage(0, (2, 1))
    for line in (cot_line, normed_line):
        line.finish()
    for d in (3, 0, 2, 1):
        out_of(d)
    ffn = {}
    inner = [o_w[:, :, i * slot : i * slot + FC].reshape(2 * two, FC) for i in (0, 1)]
    for i in range(0, D, 256):
        columns = slice(i, i + 256)
        total = contract_first(inner[0], cot[0:2, :, :, columns].reshape(2 * two, 256))
        total += contract_first(inner[1], cot[2:4, :, :, columns].reshape(2 * two, 256))
        down[:, :, :, :, columns] = total.astype(bf16).reshape(1, W, 2, -1, 256)
        if i + 256 == cut:
            ffn["down_low"] = PieceByL(
                links, LeadFirst(down.at[:, :, :, :, low_half]), *bufs[0:2], w, w_masks
            )
    ffn["down_high"] = PieceByW(
        links, LeadFirst(down.at[:, :, :, :, high_half]), *bufs[2:4], w, w_masks
    )
    back.stage(1, (3, 0))
    width = F * rows_w
    for c in (0, 1):
        for i in (0, 1):
            base = (2 * i + c) * width
            turned = normed[:, :, :, base : base + width].reshape(4 * two, width)
            for columns in [slice(n, min(n + 3 * lanes, 2 * FC)) for n in range(0, 2 * FC, 3 * lanes)]:
                total = contract_first(turned, grad_both[:, :, columns].reshape(4 * two, -1))
                both[i, c, :, :, :, :, columns] = total.astype(bf16).reshape(E, Z, 2, rows_w, -1)
        if c == 0:
            ffn["both", 0] = PieceByL(links, Natural(both.at[:, 0]), *bufs[4:6], w, w_masks)
            back.stage(1, (2, 1))
            back.stage(2, (3, 0))
    ffn["both", 1] = PieceByL(
        links, Natural(both.at[:, 1, :, first_two]), *bufs[6:8], w, w_masks
    )
    ffn["both", 2] = PieceByW(
        links, Natural(both.at[:, 1, :, pl.ds(2, 2)]), *bufs[8:10], w, w_masks
    )
    out.stage(0, (3, 0, 2, 1))
    ffn["down_low"].middle()
    ffn["down_high"].middle()

    cot_own, tok_own = normed.at[2, 0], normed.at[2, 1]
    own = Local(here, [(cot_in, cot_own), (tok, tok_own)], 23)
    gain_sums[...] = jnp.zeros_like(gain_sums)
    own.wait()
    back.arrive()

    def second_norm(rows):
        grad_normed = back.total(rows)
        grad, unit = norm_back(grad_normed, residual[rows], gains[1:2])
        grad = grad + cot_own[rows].astype(f32)
        grad_in[rows] = grad
        grad_row[s, rows] = grad.astype(bf16)
        gain_sums[1:2] += jnp.sum(grad_normed * unit, 0, keepdims=True)

    row_loop(T, 16, second_norm)
    row_x = links.pass_on(grad_row.at[s], (2, 0))
    row_c = links.pass_on(grad_row.at[s], (1, 0))

    last_two = pl.ds(2, 2)
    side = cot.at[first_two]
    normed_one = normed.at[first_two]
    grad_side = cot.at[last_two]
    loads = Local(
        here,
        [
            (o_kept, o_w),
            (side_kept, cot.at[first_two, :, :, pl.ds(0, side_width)]),
            (normed_kept, normed_one),
        ],
        25,
    )
    ffn["both", 2].middle()
    row_x.wait()
    row_cc = links.pass_on(grad_row.at[s ^ 2], (1, 0))
    out.stage(1, (3, 0, 2, 1))
    row_c.wait()
    row_cc.wait()
    loads.wait()
    per = 2 * head // rows_w
    for n in range(0, heads, 2):
        wo = o_w[n // 2 * per : (n // 2 + 1) * per].reshape(2 * head, D)
        pair = contract_last(rows_of(grad_row), wo).astype(bf16)
        side[:, :, :, column("grad", n * head, 2 * head)] = pair.reshape(2, 2, T, 2 * head)
    for i in range(0, D, HC):
        columns = slice(i, i + HC)
        grad_columns = grad_row[:, :, columns].reshape(row_len, HC)
        total = contract_first(whole(side, "attended"), grad_columns)
        o_w[:, :, columns] = total.astype(bf16).reshape(F, rows_w, HC)
    place_z, z_masks = f // 2, [(0, 2 * j) for j in range(FH)]
    o_view = LeadFirst(o_w.reshape(1, FH, 2, rows_w, D))
    o_piece = PieceByL(links, o_view, *bufs[10:12], place_z, z_masks)
    ffn["both", 0].middle()
    grad_k[...] = jnp.zeros_like(grad_k)
    grad_v[...] = jnp.zeros_like(grad_v)
    factors = rotation(rows_of(tab))
    back_turn = (factors[0], -factors[1])
    for r in range(S):
        rows, seen = slice(r * T, (r + 1) * T), slice(0, (r + 1) * T)
        keys_seen, values_seen = whole(side, "k")[seen], whole(side, "v")[seen]
        for n in range(heads):
            query = block(side, "q", r, n * head, head)
            grad_att = block(side, "grad", r, n * head, head)
            scores = contract_last(query, keys_seen) * scale + bias[rows, seen].astype(f32)
            scores = jnp.exp(scores - jnp.max(scores, -1, keepdims=True))
            probs = scores / jnp.sum(scores, -1, keepdims=True)
            grad_probs = contract_last(grad_att, values_seen)
            delta = jnp.sum(probs * grad_probs, -1, keepdims=True)
            grad_scores = (probs * (grad_probs - delta)).astype(bf16)
            grad_q = dot(grad_scores, keys_seen) * scale
            grad_q = turn(grad_q, (back_turn[0][rows], back_turn[1][rows])).astype(bf16)
            grad_side[r // 2, r % 2, :, n * head : (n + 1) * head] = grad_q
            grad_k[seen] += contract_first(grad_scores, query)
            grad_v[seen] += contract_first(probs.astype(bf16), grad_att)
    grad_key = turn(grad_k[...] * scale, back_turn).astype(bf16)
    grad_side[:, :, :, HC : HC + head] = grad_key.reshape(2, 2, T, head)
    grad_side[:, :, :, HC + head : HC + 2 * head] = grad_v[...].astype(bf16).reshape(2, 2, T, head)
    grad_qkv = slice(0, HC + 2 * head)
    back.settle()
    row = RowSum(links, *row_bufs)
    for cx, go in ((1 - x, row.far), (x, row.near)):
        for i in range(S):
            total = contract_last(grad_side[cx, :, :, :HC].reshape(two, HC), q_w[i].reshape(-1, HC))
            total += contract_last(
                grad_side[cx, :, :, HC : HC + 2 * head].reshape(two, 2 * head),
                kv_w[i, :, :, : 2 * head].reshape(-1, 2 * head),
            )
            columns = slice(i * F * rows_w, (i + 1) * F * rows_w)
            row.parts[cx, :, :, columns] = total.astype(bf16).reshape(2, T, -1)
        go()
    row.middle()
    ffn["both", 1].middle()
    out.stage(2, (3, 0))
    pieces = []
    q_view = q_w.reshape(S, FH, 2, rows_w, HC)
    kv_view = kv_w.reshape(S, FH, 2, rows_w, kv_w.shape[3])
    for i in range(S):
        columns = slice(i * F * rows_w, (i + 1) * F * rows_w)
        turned = normed_one[:, :, :, columns].reshape(row_len, -1)
        total = contract_first(turned, grad_side[:, :, :, grad_qkv].reshape(row_len, -1))
        total = total.astype(bf16)
        q_w[i] = total[:, :HC].reshape(F, rows_w, HC)
        kv_w[i, :, :, : 2 * head] = total[:, HC:].reshape(F, rows_w, 2 * head)
        one = pl.ds(i, 1)
        spare = (bufs[12].at[one], bufs[13].at[:, one])
        pieces.append(PieceByL(links, LeadFirst(q_view.at[one]), *spare, place_z, z_masks))
    for i in range(3):
        ffn["both", i].last()
    owners = [
        links.start(both.at[x, core ^ a, e, h ^ (b // 2), l], both_own.at[t], (a, b))
        for a, b in group_masks
    ]
    mine = Local(here, [(both.at[x, core, e, h, l], both_own.at[t])], 28)
    row.arrive()

    def first_norm(rows):
        grad_normed = row.total(rows)
        grad, unit = norm_back(grad_normed, tok_own[rows].astype(f32), gains[0:1])
        grad_in[rows] += grad
        gain_sums[0:1] += jnp.sum(grad_normed * unit, 0, keepdims=True)

    row_loop(T, 16, first_norm)
    results = [Local(here, [(grad_in, grad_tokens)], 29)]
    pick = jnp.where((place == lane) & (place < 2), 1.0, 0.0)
    columns = contract_first(gain_sums[...], pick).astype(bf16)
    kv_w[:, :, :, 2 * head :] = columns.reshape(S, F, rows_w, head)
    kv_row = RowSum(links, kv_w.reshape(2, 2, F * rows_w, kv_w.shape[3]), *bufs[14:16])
    kv_row.far()
    kv_row.near()
    kv_row.middle()
    o_piece.middle()
    pieces[0].middle()
    kv_row.arrive()

    def keep_kv(rows):
        kv_row.parts[x, core, rows] = kv_row.total(rows).astype(bf16)

    row_loop(F * rows_w, 16, keep_kv)
    kv_mine = LeadFirst(kv_view.at[pl.ds(s, 1)])
    kv_piece = PieceByL(links, kv_mine, *bufs[16:18], place_z, z_masks)
    for piece in pieces[1:]:
        piece.middle()
    kv_piece.middle()

    def store_down(base):
        def store(i, rows, total):
            grad_down[rows, base : base + total.shape[1]] = total

        return store

    ffn["down_low"].last(store_down(0))
    ffn["down_high"].last(store_down(cut))
    results.append(Local(here, [(grad_down, down_out)], 30))

    def store_o(i, rows, total):
        o_sum[rows] = total

    o_piece.last(store_o)
    results.append(Local(here, [(o_sum, wo_out)], 31))
    out.arrive()

    out_rows = back_parts.at[3, 0]

    def finish_output(rows):
        out_rows[rows] = (residual[rows] + out.total(rows)).astype(bf16)

    row_loop(T, 16, finish_output)
    results.append(Local(here, [(out_rows, output)], 32))
    grad_own = grad_both.reshape(Z, two // rows_w, rows_w, 2 * FC)
    for arrival in owners:
        arrival.wait()
    mine.wait()
    came = Local(
        here, [(both_own.at[pl.ds(2 * i, 2)], grad_own.at[i, pl.ds(0, 2)]) for i in range(Z)], 33
    )
    came.wait()
    results[0].wait()
    stores = [
        r.at[pl.ds(j * rows_w, rows_w), pl.ds(0, quarter)]
        for r in (residual, grad_in)
        for j in (0, 1)
    ]
    leaving = [None] * len(stores)
    count = 0
    for i, target in enumerate((gate_out, up_out)):
        units = []
        for at_h in range(Z):
            for c in (0, 1):
                block = grad_own[at_h, c].astype(f32)
                tiles = [
                    block[:, (2 * j + i) * lanes : (2 * j + i + 1) * lanes]
                    for j in range(whole_tiles)
                ]
                base = 2 * whole_tiles * lanes + i * (FC - whole_tiles * lanes)
                tiles.append(block[:, base : base + FC - whole_tiles * lanes])
                units.append(jnp.concatenate(tiles, 1))
        width = FC // W
        for at_x in (0, 1):
            for c in (0, 1):
                parts = [
                    units[2 * at_h + c][:, (2 * at_e + at_x) * width : (2 * at_e + at_x + 1) * width]
                    for at_e in range(E)
                    for at_h in range(Z)
                ]
                slot_now = count % len(stores)
                if leaving[slot_now] is not None:
                    leaving[slot_now].wait()
                stores[slot_now][...] = jnp.concatenate(parts, 1)
                columns = pl.ds((2 * at_x + c) * quarter, quarter)
                leaving[slot_now] = Local(
                    here, [(stores[slot_now], target.at[:, columns])], 37 + slot_now
                )
                count += 1
    for piece in pieces:
        piece.last()
    for a in (1, 2, 3):
        links.start(q_view.at[s ^ a, place_z, l], q_own.at[s], (a, 0))
    q_own[s] = q_view[s, place_z, l]
    q_came = links.sent[-3:]

    def store_kv(i, rows, total):
        kv_sum[rows] = total

    kv_piece.last(store_kv)
    names = (wk_out, wv_out, gains_out)
    results.append(
        Local(here, [(kv_sum.at[:, pl.ds(i * head, head)], r) for i, r in enumerate(names)], 41)
    )
    for arrival in q_came:
        arrival.wait()
    for i in leaving:
        i.wait()
    q_rows = residual.at[pl.ds(0, rows_w)]
    for i in range(S):
        q_rows[:, i * HC : (i + 1) * HC] = q_own[i].astype(f32)
    results.append(Local(here, [(q_rows, wq_out)], 44))
    out.settle()
    links.finish()
    for result in results[1:]:
        result.wait()


def angle_tables(position_row, head_size):
    half_head = head_size // 2
    frequency = 10000.0 ** (-jnp.arange(half_head, dtype=f32) * 2.0 / head_size)
    phase_angle = position_row.astype(f32)[:, None] * frequency[None, :]
    return (jnp.cos(phase_angle), jnp.sin(phase_angle))


def per_device(
    S,
    F,
    tokens,
    segments,
    positions,
    gain_one,
    w_query,
    w_key,
    w_value,
    w_out,
    gain_two,
    w_gate,
    w_up,
    w_down,
    cotangent,
):
    T, D = tokens.shape[1:]
    head = w_key.shape[1]
    row_len = segments.shape[1]
    rows = w_query.shape[0]
    down_rows = w_down.shape[0]
    FF = w_gate.shape[1]
    FH, E = F // 2, F // 8
    W, TG = 2 * E, 2 * Z
    HC = w_query.shape[1] // S
    heads = HC // head
    FC = FF // TG

    gains = jnp.stack([gain_one, gain_two], 1)
    gains = jnp.concatenate([gains, jnp.zeros((rows, head - 2), bf16)], 1)
    KV = 3 * head
    table = jnp.concatenate(angle_tables(positions[0], head), 1)
    segment = segments[0]
    index = jnp.arange(row_len)
    allowed = (index[None, :] <= index[:, None]) & (segment[None, :] == segment[:, None])
    bias = jnp.where(allowed, 0.0, -1e30).astype(bf16)
    group = [pltpu.VMEM((Z, 2, T, D), bf16), pltpu.VMEM((Z, T, D), bf16)]
    group += [pltpu.VMEM((Z, T, D), bf16), pltpu.VMEM((T, D), bf16)]
    weight = pltpu.VMEM((2, 2, E, Z, 2, rows, 2 * FC), bf16)

    def natural_by_l(n):
        block = (n, rows, 2 * FC)
        return [pltpu.VMEM((2, E, *block), bf16), pltpu.VMEM((W - 1, *block), bf16)]

    outs = [
        ((T, D), bf16),
        ((T, head), bf16),
        ((T, head), bf16),
        ((T, D), f32),
        ((rows, FF), f32),
        ((rows, FF), f32),
        ((down_rows, D), f32),
        ((rows, D), f32),
        ((rows, D), f32),
        ((rows, head), f32),
        ((rows, head), f32),
        ((rows, head), f32),
        ((TG, rows, 2 * FC), bf16),
        ((2, 2, T, D), bf16),
        ((2, 2, T, 2 * HC + 2 * head), bf16),
        ((F, rows, D), bf16),
    ]
    results = communicate(
        functools.partial(layer_kernel, FH),
        (
            tokens[0],
            table,
            w_query,
            w_key,
            w_value,
            gains,
            w_out,
            w_gate,
            w_up,
            w_down,
            cotangent[0],
            bias,
        ),
        [shape(dims, kind) for dims, kind in outs],
        300 + 40 * F,
        0,
        in_vmem=[False] * 11 + [True],
        kept=48,
        scratch=[
            weight,
            pltpu.VMEM((1, W, 2, down_rows, D), bf16),
            pltpu.VMEM((S, F, rows, HC), bf16),
            pltpu.VMEM((S, F, rows, KV), bf16),
            pltpu.VMEM((F, rows, D), bf16),
            pltpu.VMEM((T, D), f32),
            pltpu.VMEM((T, D), f32),
            pltpu.VMEM((8, D), f32),
            pltpu.VMEM((8, D), f32),
            pltpu.VMEM((S, T, D), bf16),
            pltpu.VMEM((down_rows, D), f32),
            pltpu.VMEM((rows, D), f32),
            pltpu.VMEM((rows, KV), f32),
            pltpu.VMEM((S, rows, HC), bf16),
            *group,
            *group,
            pltpu.VMEM((Z, 2, T, D), bf16),
            pltpu.VMEM((Z, 2, T, D), bf16),
            pltpu.VMEM((Z, 2 * T, 2 * FC), bf16),
            pltpu.VMEM((S, T, head), f32),
            pltpu.VMEM((row_len, head), f32),
            pltpu.VMEM((row_len, head), f32),
            *by_l_scratch(1, W, down_rows, D // 4 * 3),
            *by_w_scratch(1, W, down_rows, D // 4),
            *natural_by_l(Z),
            *natural_by_l(2),
            *by_w_scratch(2, W, rows, 2 * FC),
            *by_l_scratch(1, FH, rows, D),
            *by_l_scratch(S, FH, rows, HC),
            pltpu.VMEM((2, F * rows, KV), bf16),
            pltpu.VMEM((F * rows, KV), bf16),
            *by_l_scratch(1, FH, rows, KV),
        ],
    )
    output, keys, values, grad_tokens, gate, up, down, query, out, key, value, gains = results[:12]
    return (
        output[None],
        keys[None],
        values[None],
        grad_tokens[None],
        gains[:, 0],
        query,
        key,
        value,
        out,
        gains[:, 1],
        gate,
        up,
        down,
    )


def solution(mesh):
    token_spec = P("fsdp", "seq", None)
    flat, matrix = P(("seq", "fsdp")), P(("seq", "fsdp"), None)
    return jax.shard_map(
        functools.partial(per_device, mesh.shape["seq"], mesh.shape["fsdp"]),
        mesh=mesh,
        in_specs=(
            token_spec,
            P("fsdp", None),
            P("fsdp", "seq"),
            flat,
            matrix,
            matrix,
            matrix,
            matrix,
            flat,
            matrix,
            matrix,
            matrix,
            token_spec,
        ),
        out_specs=(
            token_spec,
            token_spec,
            token_spec,
            token_spec,
            flat,
            matrix,
            matrix,
            matrix,
            matrix,
            flat,
            matrix,
            matrix,
            matrix,
        ),
        check_vma=False,
    )
```

time: 408 us -> 397 us (0.973)
  local copies, waits for them, and re-layouts: 22 us -> 16.5 us
    unnamed x26 -> x27, local copies, waits for them, and re-layouts: 4.93 us -> 13.4 us
    convert_element_type x5 -> x0, local copies, waits for them, and re-layouts: 6.03 us -> none  [the longest x2 2.59 us: per_device(): grad_w_up = up_own.transpose(1, 0, 2).reshape(rows, FF).astype(f32)]
    reshape x5 -> x0, local copies, waits for them, and re-layouts: 5.03 us -> none  [column_blocks(): return weight.reshape(rows, n, -1).transpose(1, 0, 2)]
where the time goes in v5:
time: 397 us; the launch traced here: 391 us
  Pallas kernels  369 us (93%)
  local copies, waits for them, and re-layouts  16.5 us (4%)
  other arithmetic  4.12 us (1%)
    pallas_call x1, Pallas kernels, communicate(): pl.pallas_call(body, out_shape=outs, in_specs=specs(in_vmem, len(args)),...  369 us
    unnamed x27, local copies, waits for them, and re-layouts  13.4 us

profile of v5, /device:TPU:0, one launch (start us, length us, event | category | flops | bytes accessed | tf_op | source)
XLA Modules:
  0.0 390.9 jit_solution(9237521532576673840)
XLA Ops:
  0.6 0.7 convert_bitcast_fusion
  1.3 0.1 pad.2.clone
  1.4 0.8 copy.28
  2.2 0.8 copy.29
  2.9 0.7 maximum_maximum_fusion.refs_5_
  3.6 0.3 multiply_cosine_fusion
  3.9 0.7 pad_maximum_fusion.refs_1_
  4.6 1.7 select_convert_fusion.refs_11_
  6.4 369.1 %shard_map.228 = (bf16[128,2048]{1,0:T(8,128)(2,1)}, bf16[128,128]{1,0:T(8,128)(2,1)}, bf16[128,128]{1,0:T(8,128)(2,1)}, f32[128,2048]{1,0:T(8,128)}, f32[64,563...) custom-call(bf16[128,2048]{1,0:T(8,128)(2,1)} %bitcast.12, ...), custom_call_target="tpu_custom_call" | custom-call | tf_op jit(solution)/shard_map/pallas_call | solution.py:123
  375.5 0.0 copy-start.3
  375.5 1.6 slice_reduce_fusion
  377.1 0.0 copy-start.5
  377.1 1.9 copy.41
  379.0 1.4 copy.42
  380.4 1.4 copy.43
  381.7 0.0 copy-done.3
  381.7 0.0 copy-start.7
  381.8 1.0 copy.44
  382.7 0.0 copy-done.5
  382.7 0.8 copy.45
  383.5 0.0 copy-done.7
  383.5 0.6 copy.46
  384.1 0.0 copy-done.6
  384.2 0.6 copy.47
  384.8 0.0 copy-done.4
  384.8 0.8 copy.48
  385.6 0.0 copy-done.2
  385.6 1.1 copy.49
  386.7 0.8 copy-done.1
  387.5 1.1 copy.50
  388.6 0.8 copy-done
  389.3 1.1 copy.51
  (7 shorter events, 0.0 us)
Async XLA Ops:
  375.5 6.3 %copy-start.3 = (f32[128,2048]{1,0:T(8,128)S(1)}, f32[128,2048]{1,0:T(8,128)}, u32[]{:S(2)}) copy-start(f32[128,2048]{1,0:T(8,128)} %get-tuple-element.28) | copy-start | bytes 3145732
  377.1 5.7 %copy-start.5 = (f32[64,2048]{1,0:T(8,128)S(1)}, f32[64,2048]{1,0:T(8,128)}, u32[]{:S(2)}) copy-start(f32[64,2048]{1,0:T(8,128)} %get-tuple-element.59) | copy-start | bytes 1572868
  381.7 1.8 copy-start.7
  381.8 2.4 copy-start.6
  381.8 3.0 copy-start.4
  382.7 2.8 copy-start.2
  385.6 1.9 copy-start.1
  387.4 1.9 copy-start

commit v6 on v5

--- a/solution.py
+++ b/solution.py
@@ -433,34 +433,117 @@
         total = self.view.item(i, w, self.l)[rows].astype(f32)
         return total + self.view.got(self.by_l, i, w)[rows].astype(f32)
 
+    def place(self, k, slot=None):
+        w = self.w ^ k
+
+        def add(i, rows):
+            total = self.partial(i, w, rows)
+            if slot is not None:
+                total += self.by_w[slot, i, rows].astype(f32)
+            self.view.item(i, w, self.l)[rows] = total.astype(bf16)
+
+        block_loop(self.view.n, self.view.rows, 16, add)
+
     def middle(self):
         self.first.wait()
         self.second = []
         for k in range(1, len(self.masks)):
-            w = self.w ^ k
-
-            def add(i, rows, w=w):
-                self.view.item(i, w, self.l)[rows] = self.partial(i, w, rows).astype(bf16)
-
-            block_loop(self.view.n, self.view.rows, 16, add)
-            self.second.append(
-                self.links.start(self.view.part(w, self.l), self.by_w.at[k - 1], self.masks[k])
-            )
-
-    def last(self, store=None):
+            self.place(k)
+            block = self.view.part(self.w ^ k, self.l)
+            self.second.append(self.links.start(block, self.by_w.at[k - 1], self.masks[k]))
+
+    def arrive(self):
         for arrival in self.second:
             arrival.wait()
 
+    def last(self, store=None):
+        self.arrive()
+
         def add(i, rows):
             total = self.partial(i, self.w, rows)
-            for k in range(1, len(self.masks)):
-                total += self.by_w[k - 1, i, rows].astype(f32)
+            for k in self.slots():
+                total += self.by_w[k, i, rows].astype(f32)
             if store is None:
                 self.view.item(i, self.w, self.l)[rows] = total.astype(bf16)
             else:
                 store(i, rows, total)
 
         block_loop(self.view.n, self.view.rows, 16, add)
+
+    def slots(self):
+        return range(len(self.masks) - 1)
+
+    def inner(self):
+        pass
+
+    def settle(self):
+        pass
+
+
+class PieceAlongZ(PieceByL):
+    def __init__(self, links, view, by_l, by_w, w, masks):
+        super().__init__(links, view, by_l, by_w, w, masks)
+        self.is_inner = (w == 1) | (w == 2)
+        device = [(links.s ^ a, links.f ^ b) for a, b in masks]
+
+        def copy(k, slot, to):
+            return links.copy(view.part(w ^ k, self.l), by_w.at[slot], device[to])
+
+        self.out = [copy(k, k - 1, 1) for k in (1, 2, 3)]
+        self.over = [copy(3, 3, 3), copy(2, 3, 2)]
+        self.beside = copy(1, 0, 1)
+
+    def middle(self):
+        self.first.wait()
+
+        @pl.when(self.is_inner)
+        def _():
+            self.place(1)
+            self.beside.start()
+
+        @pl.when(jnp.logical_not(self.is_inner))
+        def _():
+            for k in (2, 3, 1):
+                self.place(k)
+                self.out[k - 1].start()
+
+    def inner(self):
+        @pl.when(self.is_inner)
+        def _():
+            for k, over in zip((3, 2), self.over):
+                self.out[4 - k].wait_recv()
+                self.place(k, 4 - k)
+                over.start()
+
+    def arrive(self):
+        @pl.when(self.is_inner)
+        def _():
+            self.out[0].wait_recv()
+            self.over[0].wait_recv()
+
+        @pl.when(jnp.logical_not(self.is_inner))
+        def _():
+            self.beside.wait_recv()
+            self.over[1].wait_recv()
+
+    def slots(self):
+        return (0, 3)
+
+    def settle(self):
+        @pl.when(self.is_inner)
+        def _():
+            for copy in [self.beside] + self.over:
+                copy.wait_send()
+
+        @pl.when(jnp.logical_not(self.is_inner))
+        def _():
+            for copy in self.out:
+                copy.wait_send()
+
+
+def z_piece(links, view, by_l, by_w, w, masks):
+    kind = PieceAlongZ if len(masks) == 4 else PieceByL
+    return kind(links, view, by_l, by_w, w, masks)
 
 
 class PieceByW:
@@ -505,6 +588,11 @@
     return [pltpu.VMEM((n, W, rows, width), bf16), pltpu.VMEM((W - 1, n, rows, width), bf16)]
 
 
+def z_scratch(n, W, rows, width):
+    slots = 4 if W == 4 else W - 1
+    return [pltpu.VMEM((n, W, rows, width), bf16), pltpu.VMEM((slots, n, rows, width), bf16)]
+
+
 def by_w_scratch(n, W, rows, width):
     return [pltpu.VMEM((n, rows, width), bf16), pltpu.VMEM((W - 1, n, 2, rows, width), bf16)]
 
@@ -517,7 +605,7 @@
     return grad, inputs * inverse
 
 
-def layer_kernel(FH, *refs):
+def layer_kernel(FH, copies, *refs):
     tok, tab_in, wq_in, wk_in, wv_in, gains_in, wo_in = refs[:7]
     gate_in, up_in, down_in, cot_in, bias = refs[7:12]
     output, keys, values, grad_tokens, gate_out, up_out, down_out = refs[12:19]
@@ -827,12 +915,13 @@
     beside = [links.pass_on(normed.at[h, core], (1, 0))]
     cot_line.arrived(1)
     cot_line.step(2)
-    for m in range(1, Z):
+    spreads[1].on_y()
+    spreads[1].on_w()
+    normed_line.arrived(0)
+    normed_line.step(1)
+    for m in range(2, Z):
         spreads[m].on_y()
         spreads[m].on_w()
-        if m < Z - 1:
-            normed_line.arrived(m - 1)
-            normed_line.step(m)
     results[0].wait()
     kept_o.wait()
     kept.wait()
@@ -915,6 +1004,8 @@
     for line in (cot_line, normed_line):
         line.came(0)
     hidden_of(h ^ 1)
+    normed_line.arrived(1)
+    normed_line.step(2)
     for line in (cot_line, normed_line):
         line.came(1)
     hidden_of(h ^ 2)
@@ -934,6 +1025,23 @@
     for d in (3, 0, 2, 1):
         out_of(d)
     ffn = {}
+    width = F * rows_w
+    for c in (0, 1):
+        for i in (0, 1):
+            base = (2 * i + c) * width
+            turned = normed[:, :, :, base : base + width].reshape(4 * two, width)
+            for columns in [slice(n, min(n + 3 * lanes, 2 * FC)) for n in range(0, 2 * FC, 3 * lanes)]:
+                total = contract_first(turned, grad_both[:, :, columns].reshape(4 * two, -1))
+                both[i, c, :, :, :, :, columns] = total.astype(bf16).reshape(E, Z, 2, rows_w, -1)
+        if c == 0:
+            ffn["both", 0] = PieceByL(links, Natural(both.at[:, 0]), *bufs[4:6], w, w_masks)
+            back.stage(1, (3, 0))
+    ffn["both", 1] = PieceByL(
+        links, Natural(both.at[:, 1, :, first_two]), *bufs[6:8], w, w_masks
+    )
+    ffn["both", 2] = PieceByW(
+        links, Natural(both.at[:, 1, :, pl.ds(2, 2)]), *bufs[8:10], w, w_masks
+    )
     inner = [o_w[:, :, i * slot : i * slot + FC].reshape(2 * two, FC) for i in (0, 1)]
     for i in range(0, D, 256):
         columns = slice(i, i + 256)
@@ -947,28 +1055,9 @@
     ffn["down_high"] = PieceByW(
         links, LeadFirst(down.at[:, :, :, :, high_half]), *bufs[2:4], w, w_masks
     )
-    back.stage(1, (3, 0))
-    width = F * rows_w
-    for c in (0, 1):
-        for i in (0, 1):
-            base = (2 * i + c) * width
-            turned = normed[:, :, :, base : base + width].reshape(4 * two, width)
-            for columns in [slice(n, min(n + 3 * lanes, 2 * FC)) for n in range(0, 2 * FC, 3 * lanes)]:
-                total = contract_first(turned, grad_both[:, :, columns].reshape(4 * two, -1))
-                both[i, c, :, :, :, :, columns] = total.astype(bf16).reshape(E, Z, 2, rows_w, -1)
-        if c == 0:
-            ffn["both", 0] = PieceByL(links, Natural(both.at[:, 0]), *bufs[4:6], w, w_masks)
-            back.stage(1, (2, 1))
-            back.stage(2, (3, 0))
-    ffn["both", 1] = PieceByL(
-        links, Natural(both.at[:, 1, :, first_two]), *bufs[6:8], w, w_masks
-    )
-    ffn["both", 2] = PieceByW(
-        links, Natural(both.at[:, 1, :, pl.ds(2, 2)]), *bufs[8:10], w, w_masks
-    )
+    back.stage(1, (2, 1))
+    back.stage(2, (3, 0))
     out.stage(0, (3, 0, 2, 1))
-    ffn["down_low"].middle()
-    ffn["down_high"].middle()
 
     cot_own, tok_own = normed.at[2, 0], normed.at[2, 1]
     own = Local(here, [(cot_in, cot_own), (tok, tok_own)], 23)
@@ -985,7 +1074,7 @@
         gain_sums[1:2] += jnp.sum(grad_normed * unit, 0, keepdims=True)
 
     row_loop(T, 16, second_norm)
-    row_x = links.pass_on(grad_row.at[s], (2, 0))
+    row_x = links.pass_on(grad_row.at[s], (3, 0))
     row_c = links.pass_on(grad_row.at[s], (1, 0))
 
     last_two = pl.ds(2, 2)
@@ -1002,8 +1091,10 @@
         25,
     )
     ffn["both", 2].middle()
+    ffn["both", 0].middle()
+    ffn["down_high"].middle()
     row_x.wait()
-    row_cc = links.pass_on(grad_row.at[s ^ 2], (1, 0))
+    row_cc = links.pass_on(grad_row.at[s ^ 3], (1, 0))
     out.stage(1, (3, 0, 2, 1))
     row_c.wait()
     row_cc.wait()
@@ -1020,8 +1111,8 @@
         o_w[:, :, columns] = total.astype(bf16).reshape(F, rows_w, HC)
     place_z, z_masks = f // 2, [(0, 2 * j) for j in range(FH)]
     o_view = LeadFirst(o_w.reshape(1, FH, 2, rows_w, D))
-    o_piece = PieceByL(links, o_view, *bufs[10:12], place_z, z_masks)
-    ffn["both", 0].middle()
+    o_piece = z_piece(links, o_view, *bufs[10:12], place_z, z_masks)
+    ffn["both", 1].middle()
     grad_k[...] = jnp.zeros_like(grad_k)
     grad_v[...] = jnp.zeros_like(grad_v)
     factors = rotation(rows_of(tab))
@@ -1060,7 +1151,13 @@
             row.parts[cx, :, :, columns] = total.astype(bf16).reshape(2, T, -1)
         go()
     row.middle()
-    ffn["both", 1].middle()
+    for i in range(3):
+        ffn["both", i].last()
+    owners = [
+        links.start(both.at[x, core ^ a, e, h ^ (b // 2), l], both_own.at[t], (a, b))
+        for a, b in group_masks
+    ]
+    mine = Local(here, [(both.at[x, core, e, h, l], both_own.at[t])], 28)
     out.stage(2, (3, 0))
     pieces = []
     q_view = q_w.reshape(S, FH, 2, rows_w, HC)
@@ -1074,14 +1171,8 @@
         kv_w[i, :, :, : 2 * head] = total[:, HC:].reshape(F, rows_w, 2 * head)
         one = pl.ds(i, 1)
         spare = (bufs[12].at[one], bufs[13].at[:, one])
-        pieces.append(PieceByL(links, LeadFirst(q_view.at[one]), *spare, place_z, z_masks))
-    for i in range(3):
-        ffn["both", i].last()
-    owners = [
-        links.start(both.at[x, core ^ a, e, h ^ (b // 2), l], both_own.at[t], (a, b))
-        for a, b in group_masks
-    ]
-    mine = Local(here, [(both.at[x, core, e, h, l], both_own.at[t])], 28)
+        pieces.append(z_piece(links, LeadFirst(q_view.at[one]), *spare, place_z, z_masks))
+    ffn["down_low"].middle()
     row.arrive()
 
     def first_norm(rows):
@@ -1101,6 +1192,7 @@
     kv_row.middle()
     o_piece.middle()
     pieces[0].middle()
+    o_piece.inner()
     kv_row.arrive()
 
     def keep_kv(rows):
@@ -1108,10 +1200,12 @@
 
     row_loop(F * rows_w, 16, keep_kv)
     kv_mine = LeadFirst(kv_view.at[pl.ds(s, 1)])
-    kv_piece = PieceByL(links, kv_mine, *bufs[16:18], place_z, z_masks)
-    for piece in pieces[1:]:
-        piece.middle()
+    kv_piece = z_piece(links, kv_mine, *bufs[16:18], place_z, z_masks)
+    for i in range(1, S):
+        pieces[i].middle()
+        pieces[i - 1].inner()
     kv_piece.middle()
+    pieces[S - 1].inner()
 
     def store_down(base):
         def store(i, rows, total):
@@ -1119,6 +1213,7 @@
 
         return store
 
+    kv_piece.inner()
     ffn["down_low"].last(store_down(0))
     ffn["down_high"].last(store_down(cut))
     results.append(Local(here, [(grad_down, down_out)], 30))
@@ -1206,9 +1301,39 @@
         q_rows[:, i * HC : (i + 1) * HC] = q_own[i].astype(f32)
     results.append(Local(here, [(q_rows, wq_out)], 44))
     out.settle()
+    for piece in [o_piece, kv_piece] + pieces:
+        piece.settle()
     links.finish()
+    assert links.count == copies, links.count
     for result in results[1:]:
         result.wait()
+
+
+def hand_over_kernel(n, *refs):
+    inputs, outputs, rooms, sems = refs[:n], refs[n : 2 * n], refs[2 * n : 3 * n], refs[3 * n]
+    loads = [pltpu.make_async_copy(inputs[i], rooms[i], sems.at[i]) for i in range(n)]
+    stores = [pltpu.make_async_copy(rooms[i], outputs[i], sems.at[n + i]) for i in range(n)]
+    for load in loads:
+        load.start()
+    for load, store in zip(loads, stores):
+        load.wait()
+        store.start()
+    for store in stores:
+        store.wait()
+
+
+def hand_over(arrays):
+    n = len(arrays)
+    anywhere = [pl.BlockSpec(memory_space=pl.ANY)] * n
+    return pl.pallas_call(
+        functools.partial(hand_over_kernel, n),
+        out_shape=[shape(a.shape, a.dtype) for a in arrays],
+        in_specs=anywhere,
+        out_specs=anywhere,
+        scratch_shapes=[pltpu.VMEM(a.shape, a.dtype) for a in arrays]
+        + [pltpu.SemaphoreType.DMA((2 * n,))],
+        compiler_params=pltpu.CompilerParams(vmem_limit_bytes=VMEM_LIMIT),
+    )(*arrays)
 
 
 def angle_tables(position_row, head_size):
@@ -1281,8 +1406,9 @@
         ((2, 2, T, 2 * HC + 2 * head), bf16),
         ((F, rows, D), bf16),
     ]
+    copies = 112 + 12 * (FH - 1) + 20 * (W - 1) + 6 * (1 + (6 if FH == 4 else FH - 1))
     results = communicate(
-        functools.partial(layer_kernel, FH),
+        functools.partial(layer_kernel, FH, copies),
         (
             tokens[0],
             table,
@@ -1298,10 +1424,10 @@
             bias,
         ),
         [shape(dims, kind) for dims, kind in outs],
-        300 + 40 * F,
+        copies,
         0,
         in_vmem=[False] * 11 + [True],
-        kept=48,
+        kept=45,
         scratch=[
             weight,
             pltpu.VMEM((1, W, 2, down_rows, D), bf16),
@@ -1330,14 +1456,16 @@
             *natural_by_l(Z),
             *natural_by_l(2),
             *by_w_scratch(2, W, rows, 2 * FC),
-            *by_l_scratch(1, FH, rows, D),
-            *by_l_scratch(S, FH, rows, HC),
+            *z_scratch(1, FH, rows, D),
+            *z_scratch(S, FH, rows, HC),
             pltpu.VMEM((2, F * rows, KV), bf16),
             pltpu.VMEM((F * rows, KV), bf16),
-            *by_l_scratch(1, FH, rows, KV),
+            *z_scratch(1, FH, rows, KV),
         ],
     )
-    output, keys, values, grad_tokens, gate, up, down, query, out, key, value, gains = results[:12]
+    output, keys, values, grad_tokens, gate, up, down, query, out, key, value, gains = hand_over(
+        results[:12]
+    )
     return (
         output[None],
         keys[None],

time: 397 us -> 349 us (0.88)
  the two profiles are of different devices: /device:TPU:0 before, /device:TPU:12 now
where the time goes in v6:
time: 349 us; the launch traced here: 343 us
  Pallas kernels  334 us (96%)
  other arithmetic  4.12 us (1%)
    pallas_call x1, Pallas kernels, communicate(): pl.pallas_call(body, out_shape=outs, in_specs=specs(in_vmem, len(args)),...  329 us

profile of v6, /device:TPU:12, one launch (start us, length us, event | category | flops | bytes accessed | tf_op | source)
XLA Modules:
  0.0 342.6 jit_solution(15274979419387319860)
XLA Ops:
  0.6 0.7 convert_bitcast_fusion
  1.3 0.1 pad.2.clone
  1.4 0.8 copy.28
  2.2 0.8 copy.29
  2.9 0.7 maximum_maximum_fusion.refs_5_
  3.6 0.3 multiply_cosine_fusion
  3.9 0.7 pad_maximum_fusion.refs_1_
  4.6 1.7 select_convert_fusion.refs_11_
  6.4 328.8 %shard_map.228 = (bf16[128,2048]{1,0:T(8,128)(2,1)}, bf16[128,128]{1,0:T(8,128)(2,1)}, bf16[128,128]{1,0:T(8,128)(2,1)}, f32[128,2048]{1,0:T(8,128)}, f32[64,563...) custom-call(bf16[128,2048]{1,0:T(8,128)(2,1)} %bitcast.11, ...), custom_call_target="tpu_custom_call" | custom-call | tf_op jit(solution)/shard_map/pallas_call | solution.py:123
  335.2 5.6 %shard_map.229 = (bf16[128,2048]{1,0:T(8,128)(2,1)}, bf16[128,128]{1,0:T(8,128)(2,1)}, bf16[128,128]{1,0:T(8,128)(2,1)}, f32[128,2048]{1,0:T(8,128)}, f32[64,563...) custom-call(bf16[128,2048]{1,0:T(8,128)(2,1)} %get-tuple-element.37., ...), custom_call_target="tpu_custom_call" | custom-call | tf_op jit(solution)/shard_map/pallas_call | solution.py:1328
  340.9 1.5 slice_reduce_fusion
  (2 shorter events, 0.0 us)

commit v7 on v6

--- a/solution.py
+++ b/solution.py
@@ -607,7 +607,7 @@
 
 def layer_kernel(FH, copies, *refs):
     tok, tab_in, wq_in, wk_in, wv_in, gains_in, wo_in = refs[:7]
-    gate_in, up_in, down_in, cot_in, bias = refs[7:12]
+    gate_in, up_in, down_in, cot_in, segments = refs[7:12]
     output, keys, values, grad_tokens, gate_out, up_out, down_out = refs[12:19]
     wq_out, wo_out, wk_out, wv_out, gains_out = refs[19:24]
     both_own, normed_kept, side_kept, o_kept = refs[24:28]
@@ -615,8 +615,8 @@
     residual, grad_in, gains, gain_sums, grad_row = refs[36:41]
     grad_down, o_sum, kv_sum, q_own = refs[41:45]
     back_bufs, out_bufs = refs[45:49], refs[49:53]
-    normed, cot, grad_both, tab, grad_k, grad_v = refs[53:59]
-    bufs = refs[59:]
+    normed, cot, grad_both, tab, grad_k, grad_v, bias = refs[53:60]
+    bufs = refs[60:]
     links = Links(send, recv)
     s, f = links.s, links.f
     x, core = s // 2, s % 2
@@ -630,7 +630,7 @@
     W, TG = 2 * E, 2 * Z
     w = 2 * e + x
     two = 2 * T
-    cut = D // 4 * 3
+    cut = D // 2
     scale = head ** (-0.5)
     group_masks = [(a, 2 * m) for m in range(Z) for a in (0, 1)][1:]
     w_masks = [(2 * (j % 2), 8 * (j // 2)) for j in range(W)]
@@ -735,6 +735,14 @@
     def sent_blocks(at_h, c):
         return grad_both.at[at_h, pl.ds(pl.multiple_of(c * rows_w, rows_w), rows_w)]
 
+    ids = jnp.broadcast_to(segments[...].astype(f32), (lanes, row_len))
+    own_ids = jnp.transpose(ids)[:, :1]
+    for r in range(S):
+        rows = slice(r * T, (r + 1) * T)
+        mine_at = lax.broadcasted_iota(jnp.int32, (T, row_len), 0) + r * T
+        seen_at = lax.broadcasted_iota(jnp.int32, (T, row_len), 1)
+        allowed = (seen_at <= mine_at) & (ids[:1] == own_ids[rows])
+        bias[rows] = jnp.where(allowed, 0.0, -1e30).astype(bf16)
     natural.wait()
     columns_of = [
         [back_parts[i, j, :rows_w, :quarter].astype(f32) for i in range(S)] for j in (0, 1)
@@ -871,7 +879,6 @@
                 probs, values_seen
             ).astype(bf16)
     spread_down.on_y()
-    spread_down.on_w()
 
     first_two = pl.ds(0, 2)
     row_bufs = (back_parts.at[first_two], back.from_core.at[first_two], back.chain.at[0])
@@ -889,6 +896,7 @@
     project(x)
     parts.near()
     parts.middle()
+    spread_down.on_w()
     spreads[0].on_y()
     spreads[0].on_w()
     for m in range(1, Z):
@@ -922,6 +930,8 @@
     for m in range(2, Z):
         spreads[m].on_y()
         spreads[m].on_w()
+    normed_line.arrived(1)
+    normed_line.step(2)
     results[0].wait()
     kept_o.wait()
     kept.wait()
@@ -1004,8 +1014,6 @@
     for line in (cot_line, normed_line):
         line.came(0)
     hidden_of(h ^ 1)
-    normed_line.arrived(1)
-    normed_line.step(2)
     for line in (cot_line, normed_line):
         line.came(1)
     hidden_of(h ^ 2)
@@ -1022,8 +1030,6 @@
     back.stage(0, (2, 1))
     for line in (cot_line, normed_line):
         line.finish()
-    for d in (3, 0, 2, 1):
-        out_of(d)
     ffn = {}
     width = F * rows_w
     for c in (0, 1):
@@ -1036,12 +1042,9 @@
         if c == 0:
             ffn["both", 0] = PieceByL(links, Natural(both.at[:, 0]), *bufs[4:6], w, w_masks)
             back.stage(1, (3, 0))
-    ffn["both", 1] = PieceByL(
-        links, Natural(both.at[:, 1, :, first_two]), *bufs[6:8], w, w_masks
-    )
-    ffn["both", 2] = PieceByW(
-        links, Natural(both.at[:, 1, :, pl.ds(2, 2)]), *bufs[8:10], w, w_masks
-    )
+    ffn["both", 1] = PieceByW(links, Natural(both.at[:, 1]), *bufs[6:8], w, w_masks)
+    for d in (3, 0, 2, 1):
+        out_of(d)
     inner = [o_w[:, :, i * slot : i * slot + FC].reshape(2 * two, FC) for i in (0, 1)]
     for i in range(0, D, 256):
         columns = slice(i, i + 256)
@@ -1052,9 +1055,6 @@
             ffn["down_low"] = PieceByL(
                 links, LeadFirst(down.at[:, :, :, :, low_half]), *bufs[0:2], w, w_masks
             )
-    ffn["down_high"] = PieceByW(
-        links, LeadFirst(down.at[:, :, :, :, high_half]), *bufs[2:4], w, w_masks
-    )
     back.stage(1, (2, 1))
     back.stage(2, (3, 0))
     out.stage(0, (3, 0, 2, 1))
@@ -1090,9 +1090,8 @@
         ],
         25,
     )
-    ffn["both", 2].middle()
+    ffn["both", 1].middle()
     ffn["both", 0].middle()
-    ffn["down_high"].middle()
     row_x.wait()
     row_cc = links.pass_on(grad_row.at[s ^ 3], (1, 0))
     out.stage(1, (3, 0, 2, 1))
@@ -1111,8 +1110,8 @@
         o_w[:, :, columns] = total.astype(bf16).reshape(F, rows_w, HC)
     place_z, z_masks = f // 2, [(0, 2 * j) for j in range(FH)]
     o_view = LeadFirst(o_w.reshape(1, FH, 2, rows_w, D))
-    o_piece = z_piece(links, o_view, *bufs[10:12], place_z, z_masks)
-    ffn["both", 1].middle()
+    o_piece = z_piece(links, o_view, *bufs[8:10], place_z, z_masks)
+    ffn["down_low"].middle()
     grad_k[...] = jnp.zeros_like(grad_k)
     grad_v[...] = jnp.zeros_like(grad_v)
     factors = rotation(rows_of(tab))
@@ -1151,7 +1150,10 @@
             row.parts[cx, :, :, columns] = total.astype(bf16).reshape(2, T, -1)
         go()
     row.middle()
-    for i in range(3):
+    ffn["down_high"] = PieceByW(
+        links, LeadFirst(down.at[:, :, :, :, high_half]), *bufs[2:4], w, w_masks
+    )
+    for i in (0, 1):
         ffn["both", i].last()
     owners = [
         links.start(both.at[x, core ^ a, e, h ^ (b // 2), l], both_own.at[t], (a, b))
@@ -1162,6 +1164,12 @@
     pieces = []
     q_view = q_w.reshape(S, FH, 2, rows_w, HC)
     kv_view = kv_w.reshape(S, FH, 2, rows_w, kv_w.shape[3])
+
+    def q_piece(i):
+        one = pl.ds(i, 1)
+        spare = (bufs[10].at[one], bufs[11].at[:, one])
+        return z_piece(links, LeadFirst(q_view.at[one]), *spare, place_z, z_masks)
+
     for i in range(S):
         columns = slice(i * F * rows_w, (i + 1) * F * rows_w)
         turned = normed_one[:, :, :, columns].reshape(row_len, -1)
@@ -1169,10 +1177,7 @@
         total = total.astype(bf16)
         q_w[i] = total[:, :HC].reshape(F, rows_w, HC)
         kv_w[i, :, :, : 2 * head] = total[:, HC:].reshape(F, rows_w, 2 * head)
-        one = pl.ds(i, 1)
-        spare = (bufs[12].at[one], bufs[13].at[:, one])
-        pieces.append(z_piece(links, LeadFirst(q_view.at[one]), *spare, place_z, z_masks))
-    ffn["down_low"].middle()
+        pieces.append(q_piece(i))
     row.arrive()
 
     def first_norm(rows):
@@ -1186,13 +1191,18 @@
     pick = jnp.where((place == lane) & (place < 2), 1.0, 0.0)
     columns = contract_first(gain_sums[...], pick).astype(bf16)
     kv_w[:, :, :, 2 * head :] = columns.reshape(S, F, rows_w, head)
-    kv_row = RowSum(links, kv_w.reshape(2, 2, F * rows_w, kv_w.shape[3]), *bufs[14:16])
+    kv_row = RowSum(links, kv_w.reshape(2, 2, F * rows_w, kv_w.shape[3]), *bufs[12:14])
     kv_row.far()
     kv_row.near()
     kv_row.middle()
     o_piece.middle()
     pieces[0].middle()
+    pieces[1].middle()
+    ffn["down_high"].middle()
     o_piece.inner()
+    pieces[2].middle()
+    pieces[0].inner()
+    pieces[3].middle()
     kv_row.arrive()
 
     def keep_kv(rows):
@@ -1200,38 +1210,13 @@
 
     row_loop(F * rows_w, 16, keep_kv)
     kv_mine = LeadFirst(kv_view.at[pl.ds(s, 1)])
-    kv_piece = z_piece(links, kv_mine, *bufs[16:18], place_z, z_masks)
-    for i in range(1, S):
-        pieces[i].middle()
-        pieces[i - 1].inner()
+    kv_piece = z_piece(links, kv_mine, *bufs[14:16], place_z, z_masks)
+    pieces[1].inner()
+    pieces[2].inner()
+    pieces[3].inner()
     kv_piece.middle()
-    pieces[S - 1].inner()
-
-    def store_down(base):
-        def store(i, rows, total):
-            grad_down[rows, base : base + total.shape[1]] = total
-
-        return store
-
     kv_piece.inner()
-    ffn["down_low"].last(store_down(0))
-    ffn["down_high"].last(store_down(cut))
-    results.append(Local(here, [(grad_down, down_out)], 30))
-
-    def store_o(i, rows, total):
-        o_sum[rows] = total
-
-    o_piece.last(store_o)
-    results.append(Local(here, [(o_sum, wo_out)], 31))
-    out.arrive()
-
-    out_rows = back_parts.at[3, 0]
-
-    def finish_output(rows):
-        out_rows[rows] = (residual[rows] + out.total(rows)).astype(bf16)
-
-    row_loop(T, 16, finish_output)
-    results.append(Local(here, [(out_rows, output)], 32))
+
     grad_own = grad_both.reshape(Z, two // rows_w, rows_w, 2 * FC)
     for arrival in owners:
         arrival.wait()
@@ -1239,6 +1224,46 @@
     came = Local(
         here, [(both_own.at[pl.ds(2 * i, 2)], grad_own.at[i, pl.ds(0, 2)]) for i in range(Z)], 33
     )
+    for piece in pieces:
+        piece.last()
+    for a in (1, 2, 3):
+        links.start(q_view.at[s ^ a, place_z, l], q_own.at[s], (a, 0))
+    q_own[s] = q_view[s, place_z, l]
+    q_came = links.sent[-3:]
+
+    def store_kv(i, rows, total):
+        kv_sum[rows] = total
+
+    kv_piece.last(store_kv)
+    names = (wk_out, wv_out, gains_out)
+    results.append(
+        Local(here, [(kv_sum.at[:, pl.ds(i * head, head)], r) for i, r in enumerate(names)], 41)
+    )
+
+    def store_down(base):
+        def store(i, rows, total):
+            grad_down[rows, base : base + total.shape[1]] = total
+
+        return store
+
+    ffn["down_low"].last(store_down(0))
+    ffn["down_high"].last(store_down(cut))
+    results.append(Local(here, [(grad_down, down_out)], 30))
+
+    def store_o(i, rows, total):
+        o_sum[rows] = total
+
+    o_piece.last(store_o)
+    results.append(Local(here, [(o_sum, wo_out)], 31))
+    out.arrive()
+
+    out_rows = back_parts.at[3, 0]
+
+    def finish_output(rows):
+        out_rows[rows] = (residual[rows] + out.total(rows)).astype(bf16)
+
+    row_loop(T, 16, finish_output)
+    results.append(Local(here, [(out_rows, output)], 32))
     came.wait()
     results[0].wait()
     stores = [
@@ -1277,21 +1302,6 @@
                     here, [(stores[slot_now], target.at[:, columns])], 37 + slot_now
                 )
                 count += 1
-    for piece in pieces:
-        piece.last()
-    for a in (1, 2, 3):
-        links.start(q_view.at[s ^ a, place_z, l], q_own.at[s], (a, 0))
-    q_own[s] = q_view[s, place_z, l]
-    q_came = links.sent[-3:]
-
-    def store_kv(i, rows, total):
-        kv_sum[rows] = total
-
-    kv_piece.last(store_kv)
-    names = (wk_out, wv_out, gains_out)
-    results.append(
-        Local(here, [(kv_sum.at[:, pl.ds(i * head, head)], r) for i, r in enumerate(names)], 41)
-    )
     for arrival in q_came:
         arrival.wait()
     for i in leaving:
@@ -1376,10 +1386,6 @@
     gains = jnp.concatenate([gains, jnp.zeros((rows, head - 2), bf16)], 1)
     KV = 3 * head
     table = jnp.concatenate(angle_tables(positions[0], head), 1)
-    segment = segments[0]
-    index = jnp.arange(row_len)
-    allowed = (index[None, :] <= index[:, None]) & (segment[None, :] == segment[:, None])
-    bias = jnp.where(allowed, 0.0, -1e30).astype(bf16)
     group = [pltpu.VMEM((Z, 2, T, D), bf16), pltpu.VMEM((Z, T, D), bf16)]
     group += [pltpu.VMEM((Z, T, D), bf16), pltpu.VMEM((T, D), bf16)]
     weight = pltpu.VMEM((2, 2, E, Z, 2, rows, 2 * FC), bf16)
@@ -1406,7 +1412,7 @@
         ((2, 2, T, 2 * HC + 2 * head), bf16),
         ((F, rows, D), bf16),
     ]
-    copies = 112 + 12 * (FH - 1) + 20 * (W - 1) + 6 * (1 + (6 if FH == 4 else FH - 1))
+    copies = 111 + 12 * (FH - 1) + 19 * (W - 1) + 6 * (1 + (6 if FH == 4 else FH - 1))
     results = communicate(
         functools.partial(layer_kernel, FH, copies),
         (
@@ -1421,7 +1427,7 @@
             w_up,
             w_down,
             cotangent[0],
-            bias,
+            segments,
         ),
         [shape(dims, kind) for dims, kind in outs],
         copies,
@@ -1451,11 +1457,11 @@
             pltpu.VMEM((S, T, head), f32),
             pltpu.VMEM((row_len, head), f32),
             pltpu.VMEM((row_len, head), f32),
-            *by_l_scratch(1, W, down_rows, D // 4 * 3),
-            *by_w_scratch(1, W, down_rows, D // 4),
+            pltpu.VMEM((row_len, row_len), bf16),
+            *by_l_scratch(1, W, down_rows, D // 2),
+            *by_w_scratch(1, W, down_rows, D // 2),
             *natural_by_l(Z),
-            *natural_by_l(2),
-            *by_w_scratch(2, W, rows, 2 * FC),
+            *by_w_scratch(Z, W, rows, 2 * FC),
             *z_scratch(1, FH, rows, D),
             *z_scratch(S, FH, rows, HC),
             pltpu.VMEM((2, F * rows, KV), bf16),

time: 349 us -> 327 us (0.937)
  the two profiles are of different devices: /device:TPU:12 before, /device:TPU:0 now
where the time goes in v7:
time: 327 us; the launch traced here: 321 us
  Pallas kernels  314 us (96%)
    pallas_call x1, Pallas kernels, communicate(): pl.pallas_call(body, out_shape=outs, in_specs=specs(in_vmem, len(args)),...  309 us

profile of v7, /device:TPU:0, one launch (start us, length us, event | category | flops | bytes accessed | tf_op | source)
XLA Modules:
  0.0 320.9 jit_solution(4742672164688376660)
XLA Ops:
  0.6 0.7 convert_bitcast_fusion
  1.3 0.1 pad.2.clone
  1.4 0.8 copy.28
  2.2 0.8 copy.29
  2.9 0.7 maximum_maximum_fusion.refs_5_
  3.6 0.3 multiply_cosine_fusion
  3.9 0.7 pad_maximum_fusion.refs_1_
  4.6 308.8 %shard_map.228 = (bf16[128,2048]{1,0:T(8,128)(2,1)}, bf16[128,128]{1,0:T(8,128)(2,1)}, bf16[128,128]{1,0:T(8,128)(2,1)}, f32[128,2048]{1,0:T(8,128)}, f32[64,563...) custom-call(bf16[128,2048]{1,0:T(8,128)(2,1)} %bitcast.10, ...), custom_call_target="tpu_custom_call" | custom-call | tf_op jit(solution)/shard_map/pallas_call | solution.py:123
  313.5 5.6 %shard_map.229 = (bf16[128,2048]{1,0:T(8,128)(2,1)}, bf16[128,128]{1,0:T(8,128)(2,1)}, bf16[128,128]{1,0:T(8,128)(2,1)}, f32[128,2048]{1,0:T(8,128)}, f32[64,563...) custom-call(bf16[128,2048]{1,0:T(8,128)(2,1)} %get-tuple-element.37., ...), custom_call_target="tpu_custom_call" | custom-call | tf_op jit(solution)/shard_map/pallas_call | solution.py:1338
  319.1 1.5 slice_reduce_fusion
  (2 shorter events, 0.0 us)

commit v8 on v7

--- a/solution.py
+++ b/solution.py
@@ -1,4 +1,5 @@
 import functools
+import math
 
 import jax
 import jax.numpy as jnp
@@ -606,8 +607,8 @@
 
 
 def layer_kernel(FH, copies, *refs):
-    tok, tab_in, wq_in, wk_in, wv_in, gains_in, wo_in = refs[:7]
-    gate_in, up_in, down_in, cot_in, segments = refs[7:12]
+    tok, wq_in, wk_in, wv_in, wo_in, gate_in, up_in, down_in, cot_in = refs[:9]
+    segments, positions, gains_in = refs[9:12]
     output, keys, values, grad_tokens, gate_out, up_out, down_out = refs[12:19]
     wq_out, wo_out, wk_out, wv_out, gains_out = refs[19:24]
     both_own, normed_kept, side_kept, o_kept = refs[24:28]
@@ -615,8 +616,8 @@
     residual, grad_in, gains, gain_sums, grad_row = refs[36:41]
     grad_down, o_sum, kv_sum, q_own = refs[41:45]
     back_bufs, out_bufs = refs[45:49], refs[49:53]
-    normed, cot, grad_both, tab, grad_k, grad_v, bias = refs[53:60]
-    bufs = refs[60:]
+    normed, cot, grad_both, tab, grad_k, grad_v, bias, gain_block = refs[53:61]
+    bufs = refs[61:]
     links = Links(send, recv)
     s, f = links.s, links.f
     x, core = s // 2, s % 2
@@ -664,16 +665,22 @@
         + [(1, 2 * m) for m in range(1, Z)]
         + [mask for mask in w_masks if mask[0] and mask[1]]
     )
+    place = lax.broadcasted_iota(jnp.int32, (8, head), 0)
+    lane = lax.broadcasted_iota(jnp.int32, (8, head), 1)
+    pick = jnp.where((place == lane) & (place < 2), 1.0, 0.0)
+    row_at = lax.broadcasted_iota(jnp.int32, (8, rows_w), 0)
+    both_gains = [jnp.broadcast_to(gains_in[i : i + 1].astype(f32), (8, rows_w)) for i in (0, 1)]
+    gain_rows = jnp.where(row_at == 0, both_gains[0], jnp.where(row_at == 1, both_gains[1], 0.0))
+    gain_block[...] = contract_first(gain_rows, pick).astype(bf16)
     local = Local(
         here,
         [
             (wq_in.at[:, pl.ds(pl.multiple_of(s * HC, HC), HC)], q_w.at[s, f]),
             (wk_in, kv_w.at[s, f, :, pl.ds(0, head)]),
             (wv_in, kv_w.at[s, f, :, pl.ds(head, head)]),
-            (gains_in, kv_w.at[s, f, :, pl.ds(2 * head, head)]),
+            (gain_block, kv_w.at[s, f, :, pl.ds(2 * head, head)]),
             (wo_in, o_w.at[f]),
             (tok, tok_g.at[s]),
-            (tab_in, tab.at[s]),
             (down_in, down.at[0, w, l]),
             (cot_in, cot.at[h, core]),
         ],
@@ -708,9 +715,15 @@
         arrival.wait()
     q_line.step(0)
     needed.append(links.pass_on(q_w.at[:, f], (0, 1)))
+    at = jnp.broadcast_to(positions[...].astype(f32), (T, T))
+    frequency = lax.broadcasted_iota(jnp.int32, (1, head), 1)
+    frequency = lax.rem(frequency, head // 2).astype(f32) * (-2.0 / head * math.log(10000.0))
+    angle = jnp.transpose(at)[:, :1] * jnp.exp(frequency)
+    first_half = lax.broadcasted_iota(jnp.int32, (T, head), 1) < head // 2
+    tab[s] = jnp.where(first_half, jnp.cos(angle), jnp.sin(angle))
     tok_x = links.start(tok, tok_g.at[s], (2, 0))
     needed.append(links.start(tok, tok_g.at[s], (1, 0)))
-    needed += [links.start(tab_in, tab.at[s], (a, 0)) for a in (1, 2, 3)]
+    needed += [links.pass_on(tab.at[s], (a, 0)) for a in (1, 2, 3)]
     ffn_in = {}
     lanes = 128
     whole_tiles = FC // lanes
@@ -795,7 +808,7 @@
         lambda j: down.at[0, w ^ j, l, :, low_half],
     )
     to_group(0)
-    local.wait(7)
+    local.wait(6)
     spread_down.by_w()
     for j in range(FH - 1):
         for way in (kv_line, o_line, q_line):
@@ -824,15 +837,12 @@
         arrival.wait()
     o_line.finish()
     q_line.finish()
-    local.wait(5, 6)
+    local.wait(5)
     kept_o = Local(here, [(o_w, o_kept)], 18)
 
     normed_one, side = out_parts.at[pl.ds(0, 2)], out_parts.at[pl.ds(2, 2)]
-    place = lax.broadcasted_iota(jnp.int32, (8, head), 0)
-    lane = lax.broadcasted_iota(jnp.int32, (8, head), 1)
-    pick = (place == lane).astype(bf16)
     kv_full = rows_of(kv_w)
-    gains[...] = contract_last(pick, kv_full[:, 2 * head :])
+    gains[...] = contract_last(pick.astype(bf16), kv_full[:, 2 * head :])
 
     def norm_one(i, rows):
         value = tok_g[i, rows].astype(f32)
@@ -840,7 +850,7 @@
         normed_one[i // 2, lax.rem(i, 2), rows] = (value * inverse * gains[0:1]).astype(bf16)
 
     block_loop(S, T, 16, norm_one)
-    local.wait(8)
+    local.wait(7)
     cot_line.step(0)
     arriving.append(links.pass_on(cot.at[h, core], (1, 0)))
     factors = rotation(rows_of(tab))
@@ -1045,16 +1055,20 @@
     ffn["both", 1] = PieceByW(links, Natural(both.at[:, 1]), *bufs[6:8], w, w_masks)
     for d in (3, 0, 2, 1):
         out_of(d)
+    quarters = [pl.ds(i * (cut // 2), cut // 2) for i in (0, 1)]
     inner = [o_w[:, :, i * slot : i * slot + FC].reshape(2 * two, FC) for i in (0, 1)]
     for i in range(0, D, 256):
         columns = slice(i, i + 256)
         total = contract_first(inner[0], cot[0:2, :, :, columns].reshape(2 * two, 256))
         total += contract_first(inner[1], cot[2:4, :, :, columns].reshape(2 * two, 256))
         down[:, :, :, :, columns] = total.astype(bf16).reshape(1, W, 2, -1, 256)
-        if i + 256 == cut:
-            ffn["down_low"] = PieceByL(
-                links, LeadFirst(down.at[:, :, :, :, low_half]), *bufs[0:2], w, w_masks
-            )
+    def down_low(i):
+        view = LeadFirst(down.at[:, :, :, :, quarters[i]])
+        ffn["down_low", i] = PieceByL(
+            links, view, bufs[0].at[:, :, :, quarters[i]], bufs[1].at[:, :, :, quarters[i]], w, w_masks
+        )
+
+    down_low(0)
     back.stage(1, (2, 1))
     back.stage(2, (3, 0))
     out.stage(0, (3, 0, 2, 1))
@@ -1092,9 +1106,10 @@
     )
     ffn["both", 1].middle()
     ffn["both", 0].middle()
+    down_low(1)
     row_x.wait()
     row_cc = links.pass_on(grad_row.at[s ^ 3], (1, 0))
-    out.stage(1, (3, 0, 2, 1))
+    out.stage(1, (3, 0))
     row_c.wait()
     row_cc.wait()
     loads.wait()
@@ -1111,7 +1126,24 @@
     place_z, z_masks = f // 2, [(0, 2 * j) for j in range(FH)]
     o_view = LeadFirst(o_w.reshape(1, FH, 2, rows_w, D))
     o_piece = z_piece(links, o_view, *bufs[8:10], place_z, z_masks)
-    ffn["down_low"].middle()
+
+    owned = []
+
+    def give(c):
+        ffn["both", c].last()
+        for source in (0, 1):
+            for m in range(Z):
+                if (source, m) != (c, 0):
+                    copy = links.copy(
+                        both.at[x, c, e, h ^ m, l], both_own.at[2 * h + source], (2 * x + c, f ^ (2 * m))
+                    )
+                    owned.append((c, source, copy))
+
+                    @pl.when(core == source)
+                    def _():
+                        copy.start()
+
+    give(1)
     grad_k[...] = jnp.zeros_like(grad_k)
     grad_v[...] = jnp.zeros_like(grad_v)
     factors = rotation(rows_of(tab))
@@ -1150,16 +1182,9 @@
             row.parts[cx, :, :, columns] = total.astype(bf16).reshape(2, T, -1)
         go()
     row.middle()
-    ffn["down_high"] = PieceByW(
-        links, LeadFirst(down.at[:, :, :, :, high_half]), *bufs[2:4], w, w_masks
-    )
-    for i in (0, 1):
-        ffn["both", i].last()
-    owners = [
-        links.start(both.at[x, core ^ a, e, h ^ (b // 2), l], both_own.at[t], (a, b))
-        for a, b in group_masks
-    ]
+    give(0)
     mine = Local(here, [(both.at[x, core, e, h, l], both_own.at[t])], 28)
+    out.stage(1, (2, 1))
     out.stage(2, (3, 0))
     pieces = []
     q_view = q_w.reshape(S, FH, 2, rows_w, HC)
@@ -1188,17 +1213,20 @@
 
     row_loop(T, 16, first_norm)
     results = [Local(here, [(grad_in, grad_tokens)], 29)]
-    pick = jnp.where((place == lane) & (place < 2), 1.0, 0.0)
     columns = contract_first(gain_sums[...], pick).astype(bf16)
     kv_w[:, :, :, 2 * head :] = columns.reshape(S, F, rows_w, head)
     kv_row = RowSum(links, kv_w.reshape(2, 2, F * rows_w, kv_w.shape[3]), *bufs[12:14])
     kv_row.far()
     kv_row.near()
     kv_row.middle()
+    ffn["down_high"] = PieceByW(
+        links, LeadFirst(down.at[:, :, :, :, high_half]), *bufs[2:4], w, w_masks
+    )
+    for i in (0, 1):
+        ffn["down_low", i].middle()
     o_piece.middle()
     pieces[0].middle()
     pieces[1].middle()
-    ffn["down_high"].middle()
     o_piece.inner()
     pieces[2].middle()
     pieces[0].inner()
@@ -1215,46 +1243,35 @@
     pieces[2].inner()
     pieces[3].inner()
     kv_piece.middle()
+    ffn["down_high"].middle()
     kv_piece.inner()
 
     grad_own = grad_both.reshape(Z, two // rows_w, rows_w, 2 * FC)
-    for arrival in owners:
-        arrival.wait()
+    for c, source, copy in owned:
+
+        @pl.when(core == c)
+        def _():
+            copy.wait_recv()
+
+        @pl.when(core == source)
+        def _():
+            copy.wait_send()
+
     mine.wait()
     came = Local(
         here, [(both_own.at[pl.ds(2 * i, 2)], grad_own.at[i, pl.ds(0, 2)]) for i in range(Z)], 33
     )
-    for piece in pieces:
-        piece.last()
-    for a in (1, 2, 3):
-        links.start(q_view.at[s ^ a, place_z, l], q_own.at[s], (a, 0))
-    q_own[s] = q_view[s, place_z, l]
-    q_came = links.sent[-3:]
-
-    def store_kv(i, rows, total):
-        kv_sum[rows] = total
-
-    kv_piece.last(store_kv)
-    names = (wk_out, wv_out, gains_out)
-    results.append(
-        Local(here, [(kv_sum.at[:, pl.ds(i * head, head)], r) for i, r in enumerate(names)], 41)
-    )
-
     def store_down(base):
         def store(i, rows, total):
             grad_down[rows, base : base + total.shape[1]] = total
 
         return store
 
-    ffn["down_low"].last(store_down(0))
+    for i in (0, 1):
+        ffn["down_low", i].last(store_down(i * (cut // 2)))
     ffn["down_high"].last(store_down(cut))
     results.append(Local(here, [(grad_down, down_out)], 30))
 
-    def store_o(i, rows, total):
-        o_sum[rows] = total
-
-    o_piece.last(store_o)
-    results.append(Local(here, [(o_sum, wo_out)], 31))
     out.arrive()
 
     out_rows = back_parts.at[3, 0]
@@ -1302,6 +1319,27 @@
                     here, [(stores[slot_now], target.at[:, columns])], 37 + slot_now
                 )
                 count += 1
+    def store_o(i, rows, total):
+        o_sum[rows] = total
+
+    o_piece.last(store_o)
+    results.append(Local(here, [(o_sum, wo_out)], 31))
+    for piece in pieces:
+        piece.last()
+    for a in (1, 2, 3):
+        links.start(q_view.at[s ^ a, place_z, l], q_own.at[s], (a, 0))
+    q_own[s] = q_view[s, place_z, l]
+    q_came = links.sent[-3:]
+
+    def store_kv(i, rows, total):
+        kv_sum[rows] = total
+
+    kv_piece.last(store_kv)
+    names = (wk_out, wv_out, gains_out)
+    results.append(
+        Local(here, [(kv_sum.at[:, pl.ds(i * head, head)], r) for i, r in enumerate(names)], 41)
+    )
+
     for arrival in q_came:
         arrival.wait()
     for i in leaving:
@@ -1344,13 +1382,6 @@
         + [pltpu.SemaphoreType.DMA((2 * n,))],
         compiler_params=pltpu.CompilerParams(vmem_limit_bytes=VMEM_LIMIT),
     )(*arrays)
-
-
-def angle_tables(position_row, head_size):
-    half_head = head_size // 2
-    frequency = 10000.0 ** (-jnp.arange(half_head, dtype=f32) * 2.0 / head_size)
-    phase_angle = position_row.astype(f32)[:, None] * frequency[None, :]
-    return (jnp.cos(phase_angle), jnp.sin(phase_angle))
 
 
 def per_device(
@@ -1382,10 +1413,8 @@
     heads = HC // head
     FC = FF // TG
 
-    gains = jnp.stack([gain_one, gain_two], 1)
-    gains = jnp.concatenate([gains, jnp.zeros((rows, head - 2), bf16)], 1)
+    gains = jnp.stack([gain_one, gain_two])
     KV = 3 * head
-    table = jnp.concatenate(angle_tables(positions[0], head), 1)
     group = [pltpu.VMEM((Z, 2, T, D), bf16), pltpu.VMEM((Z, T, D), bf16)]
     group += [pltpu.VMEM((Z, T, D), bf16), pltpu.VMEM((T, D), bf16)]
     weight = pltpu.VMEM((2, 2, E, Z, 2, rows, 2 * FC), bf16)
@@ -1412,27 +1441,27 @@
         ((2, 2, T, 2 * HC + 2 * head), bf16),
         ((F, rows, D), bf16),
     ]
-    copies = 111 + 12 * (FH - 1) + 19 * (W - 1) + 6 * (1 + (6 if FH == 4 else FH - 1))
+    copies = 119 + 12 * (FH - 1) + 20 * (W - 1) + 6 * (1 + (6 if FH == 4 else FH - 1))
     results = communicate(
         functools.partial(layer_kernel, FH, copies),
         (
             tokens[0],
-            table,
             w_query,
             w_key,
             w_value,
-            gains,
             w_out,
             w_gate,
             w_up,
             w_down,
             cotangent[0],
             segments,
+            positions,
+            gains,
         ),
         [shape(dims, kind) for dims, kind in outs],
         copies,
         0,
-        in_vmem=[False] * 11 + [True],
+        in_vmem=[False] * 9 + [True] * 3,
         kept=45,
         scratch=[
             weight,
@@ -1458,6 +1487,7 @@
             pltpu.VMEM((row_len, head), f32),
             pltpu.VMEM((row_len, head), f32),
             pltpu.VMEM((row_len, row_len), bf16),
+            pltpu.VMEM((rows, head), bf16),
             *by_l_scratch(1, W, down_rows, D // 2),
             *by_w_scratch(1, W, down_rows, D // 2),
             *natural_by_l(Z),

time: 327 us -> 320 us (0.979)
  the two profiles are of different devices: /device:TPU:0 before, /device:TPU:17 now
where the time goes in v8:
time: 320 us; the launch traced here: 314 us
  Pallas kernels  311 us (97%)
    pallas_call x1, Pallas kernels, communicate(): pl.pallas_call(body, out_shape=outs, in_specs=specs(in_vmem, len(args)),...  305 us

profile of v8, /device:TPU:17, one launch (start us, length us, event | category | flops | bytes accessed | tf_op | source)
XLA Modules:
  0.0 314.3 jit_solution(14531475254985584757)
XLA Ops:
  0.6 1.2 pad_maximum_fusion.refs_11_
  1.8 305.1 %shard_map.228 = (bf16[128,2048]{1,0:T(8,128)(2,1)}, bf16[128,128]{1,0:T(8,128)(2,1)}, bf16[128,128]{1,0:T(8,128)(2,1)}, f32[128,2048]{1,0:T(8,128)}, f32[64,563...) custom-call(bf16[128,2048]{1,0:T(8,128)(2,1)} %bitcast.8, ...), custom_call_target="tpu_custom_call" | custom-call | tf_op jit(solution)/shard_map/pallas_call | solution.py:124
  306.9 5.6 %shard_map.229 = (bf16[128,2048]{1,0:T(8,128)(2,1)}, bf16[128,128]{1,0:T(8,128)(2,1)}, bf16[128,128]{1,0:T(8,128)(2,1)}, f32[128,2048]{1,0:T(8,128)}, f32[64,563...) custom-call(bf16[128,2048]{1,0:T(8,128)(2,1)} %get-tuple-element.37., ...), custom_call_target="tpu_custom_call" | custom-call | tf_op jit(solution)/shard_map/pallas_call | solution.py:1376
  312.6 1.5 slice_reduce_fusion

commit v9 on v8

--- a/solution.py
+++ b/solution.py
@@ -1106,7 +1106,6 @@
     )
     ffn["both", 1].middle()
     ffn["both", 0].middle()
-    down_low(1)
     row_x.wait()
     row_cc = links.pass_on(grad_row.at[s ^ 3], (1, 0))
     out.stage(1, (3, 0))
@@ -1118,14 +1117,18 @@
         wo = o_w[n // 2 * per : (n // 2 + 1) * per].reshape(2 * head, D)
         pair = contract_last(rows_of(grad_row), wo).astype(bf16)
         side[:, :, :, column("grad", n * head, 2 * head)] = pair.reshape(2, 2, T, 2 * head)
+    place_z, z_masks = f // 2, [(0, 2 * j) for j in range(FH)]
+    o_whole, o_pieces = o_w.reshape(1, FH, 2, rows_w, D), []
     for i in range(0, D, HC):
         columns = slice(i, i + HC)
         grad_columns = grad_row[:, :, columns].reshape(row_len, HC)
         total = contract_first(whole(side, "attended"), grad_columns)
         o_w[:, :, columns] = total.astype(bf16).reshape(F, rows_w, HC)
-    place_z, z_masks = f // 2, [(0, 2 * j) for j in range(FH)]
-    o_view = LeadFirst(o_w.reshape(1, FH, 2, rows_w, D))
-    o_piece = z_piece(links, o_view, *bufs[8:10], place_z, z_masks)
+        if (i + HC) % (D // 2) == 0:
+            half = pl.ds(i + HC - D // 2, D // 2)
+            view = LeadFirst(o_whole.at[:, :, :, :, half])
+            spare = [r.at[:, :, :, half] for r in bufs[8:10]]
+            o_pieces.append(z_piece(links, view, *spare, place_z, z_masks))
 
     owned = []
 
@@ -1203,6 +1206,8 @@
         q_w[i] = total[:, :HC].reshape(F, rows_w, HC)
         kv_w[i, :, :, : 2 * head] = total[:, HC:].reshape(F, rows_w, 2 * head)
         pieces.append(q_piece(i))
+    down_low(1)
+    o_pieces[0].middle()
     row.arrive()
 
     def first_norm(rows):
@@ -1222,12 +1227,12 @@
     ffn["down_high"] = PieceByW(
         links, LeadFirst(down.at[:, :, :, :, high_half]), *bufs[2:4], w, w_masks
     )
-    for i in (0, 1):
-        ffn["down_low", i].middle()
-    o_piece.middle()
+    ffn["down_low", 0].middle()
+    o_pieces[1].middle()
     pieces[0].middle()
     pieces[1].middle()
-    o_piece.inner()
+    o_pieces[0].inner()
+    o_pieces[1].inner()
     pieces[2].middle()
     pieces[0].inner()
     pieces[3].middle()
@@ -1245,6 +1250,7 @@
     kv_piece.middle()
     ffn["down_high"].middle()
     kv_piece.inner()
+    ffn["down_low", 1].middle()
 
     grad_own = grad_both.reshape(Z, two // rows_w, rows_w, 2 * FC)
     for c, source, copy in owned:
@@ -1319,10 +1325,14 @@
                     here, [(stores[slot_now], target.at[:, columns])], 37 + slot_now
                 )
                 count += 1
-    def store_o(i, rows, total):
-        o_sum[rows] = total
-
-    o_piece.last(store_o)
+    def store_o(base):
+        def store(i, rows, total):
+            o_sum[rows, base : base + D // 2] = total
+
+        return store
+
+    for i in (0, 1):
+        o_pieces[i].last(store_o(i * D // 2))
     results.append(Local(here, [(o_sum, wo_out)], 31))
     for piece in pieces:
         piece.last()
@@ -1349,7 +1359,7 @@
         q_rows[:, i * HC : (i + 1) * HC] = q_own[i].astype(f32)
     results.append(Local(here, [(q_rows, wq_out)], 44))
     out.settle()
-    for piece in [o_piece, kv_piece] + pieces:
+    for piece in [*o_pieces, kv_piece, *pieces]:
         piece.settle()
     links.finish()
     assert links.count == copies, links.count
@@ -1441,7 +1451,7 @@
         ((2, 2, T, 2 * HC + 2 * head), bf16),
         ((F, rows, D), bf16),
     ]
-    copies = 119 + 12 * (FH - 1) + 20 * (W - 1) + 6 * (1 + (6 if FH == 4 else FH - 1))
+    copies = 119 + 12 * (FH - 1) + 20 * (W - 1) + 7 * (1 + (6 if FH == 4 else FH - 1))
     results = communicate(
         functools.partial(layer_kernel, FH, copies),
         (

time: 320 us -> 319 us (level)
  the two profiles are of different devices: /device:TPU:17 before, /device:TPU:0 now
where the time goes in v9:
time: 319 us; the launch traced here: 313 us
  Pallas kernels  309 us (97%)
    pallas_call x1, Pallas kernels, communicate(): pl.pallas_call(body, out_shape=outs, in_specs=specs(in_vmem, len(args)),...  304 us

profile of v9, /device:TPU:0, one launch (start us, length us, event | category | flops | bytes accessed | tf_op | source)
XLA Modules:
  0.0 312.9 jit_solution(17108155122729905908)
XLA Ops:
  0.6 1.2 pad_maximum_fusion.refs_11_
  1.8 303.7 %shard_map.228 = (bf16[128,2048]{1,0:T(8,128)(2,1)}, bf16[128,128]{1,0:T(8,128)(2,1)}, bf16[128,128]{1,0:T(8,128)(2,1)}, f32[128,2048]{1,0:T(8,128)}, f32[64,563...) custom-call(bf16[128,2048]{1,0:T(8,128)(2,1)} %bitcast.8, ...), custom_call_target="tpu_custom_call" | custom-call | tf_op jit(solution)/shard_map/pallas_call | solution.py:124
  305.5 5.6 %shard_map.229 = (bf16[128,2048]{1,0:T(8,128)(2,1)}, bf16[128,128]{1,0:T(8,128)(2,1)}, bf16[128,128]{1,0:T(8,128)(2,1)}, f32[128,2048]{1,0:T(8,128)}, f32[64,563...) custom-call(bf16[128,2048]{1,0:T(8,128)(2,1)} %get-tuple-element.37., ...), custom_call_target="tpu_custom_call" | custom-call | tf_op jit(solution)/shard_map/pallas_call | solution.py:1386
  311.2 1.5 slice_reduce_fusion
